TPU v7x, 32 devices: a whole 2x2x4 slice. The times are simulated.
32 devices in a mesh: groups: 2 (over y), dp: 4 (over x, core), tensor: 4 (over z).
Axes of the slice: x: 2, y: 2, z: 4, core: 2. Of those that a mesh axis runs over, the one named last changes fastest.
Arguments:
- tokens: bfloat16 [6144, 8192], P(('groups', 'dp'), 'tensor'), parts along dimension 0, may hold values from -6 to 6
- query_base_weight: bfloat16 [8192, 8192], P(None, 'tensor'), may hold values from -0.0625 to 0.0625
- stored_shrink_factors: bfloat16 [1024, 16, 8192], P('dp', None, 'tensor'), may hold values from -0.0625 to 0.0625
- stored_expand_factors: bfloat16 [1024, 16, 8192], P('dp', None, 'tensor'), may hold values from -1.5 to 1.5
- segment_adapter: int32 [8, 64], P('groups'), parts along dimension 0, may hold values from 0 to 1023, as said below
- segment_length: int32 [8, 64], P(('groups', 'dp')), parts along dimension 0, may hold values from 1 to 48, 768 in all within a row
- adapter_storage_slot: int32 [2048], P('groups'), parts along dimension 0, may hold values from 0 to 1023, as said below
Outputs:
- queries: bfloat16 [6144, 8192], P(('groups', 'dp'), 'tensor'), parts along dimension 0
There are 2 independent parts, one for each index of `groups`. A program takes and returns all parts, laid end to end along the dimension named above; an argument that names none is the same for every part. Nothing has to cross between parts.
Inputs may be any that keep to these rules, and one draw needn't show every extreme that they name: `segment_adapter`: each dp group's 64 segments name distinct adapters; in every group exactly 32 of them have one home dp group, and no home holds more than 32 of one group's adapters. `adapter_storage_slot`: A permutation of the slots. `segment_length`: each row sums to 768.
All inputs are finite; a program needn't handle non-finite values.
Results may differ from a plain program's by a relative error of at most 0.004.
Values may be sent and summed in bfloat16 or wider, within the bound.
No kernel may reach another device: no remote copies, remote signals or barrier semaphores. Data moves between devices by JAX's collectives and lax.ppermute only.
A program may use at most 320 MiB of HBM per device.

v0:
```python
import jax
import jax.numpy as jnp
from jax import lax
from jax.sharding import PartitionSpec as P


def body(
    tokens,
    query_base_weight,
    stored_shrink_factors,
    stored_expand_factors,
    segment_adapter,
    segment_length,
    adapter_storage_slot,
):
    groups = lax.axis_size("dp")
    me = lax.axis_index("dp")
    stored_factors = stored_shrink_factors.shape[0]
    used = segment_adapter.shape[1]
    rows = tokens.shape[0]
    group_rank = stored_shrink_factors.shape[1]
    expand_width = stored_expand_factors.shape[2]
    count_all = adapter_storage_slot.shape[0]
    base = jnp.dot(
        lax.all_gather(tokens, "tensor", axis=1, tiled=True),
        query_base_weight,
        preferred_element_type=jnp.float32,
    )
    flat_ids = segment_adapter.reshape(-1)
    match = flat_ids[:, None] == jnp.arange(count_all, dtype=jnp.int32)[None, :]
    seg_slot = jnp.sum(jnp.where(match, adapter_storage_slot[None, :], 0), axis=1).reshape(
        groups, used
    )
    seg_home = seg_slot // stored_factors
    seg_local = seg_slot % stored_factors
    owned_by_group = seg_home == me
    my_home = lax.dynamic_index_in_dim(seg_home, me, 0, keepdims=False)
    lookup_index = jnp.where(owned_by_group, seg_local, 0)
    outgoing_shrink = jnp.where(
        owned_by_group[:, :, None, None],
        stored_shrink_factors[lookup_index],
        jnp.zeros((), jnp.bfloat16),
    )
    outgoing_expand = jnp.where(
        owned_by_group[:, :, None, None],
        stored_expand_factors[lookup_index],
        jnp.zeros((), jnp.bfloat16),
    )
    recv_a, recv_b = (
        lax.all_to_all(outgoing_shrink, "dp", split_axis=0, concat_axis=0, tiled=True),
        lax.all_to_all(outgoing_expand, "dp", split_axis=0, concat_axis=0, tiled=True),
    )
    pick = jnp.arange(groups, dtype=jnp.int32)[:, None] == my_home[None, :]
    fac_a = jnp.sum(jnp.where(pick[:, :, None, None], recv_a, jnp.zeros((), jnp.bfloat16)), axis=0)
    fac_b = jnp.sum(jnp.where(pick[:, :, None, None], recv_b, jnp.zeros((), jnp.bfloat16)), axis=0)
    ends = jnp.cumsum(segment_length[0])
    seg_of = jnp.sum(
        jnp.where(ends[None, :] <= jnp.arange(rows, dtype=jnp.int32)[:, None], 1, 0), axis=1
    )
    member = seg_of[:, None] == jnp.arange(used, dtype=jnp.int32)[None, :]
    shrink_all = jnp.einsum("rd,skd->rsk", tokens, fac_a, preferred_element_type=jnp.float32)
    partial_value = jnp.sum(jnp.where(member[:, :, None], shrink_all, 0.0), axis=1)
    shrink = lax.psum(partial_value, "tensor")
    shrink_low = shrink.astype(jnp.bfloat16)
    spread = jnp.where(member[:, :, None], shrink_low[:, None, :], jnp.zeros((), jnp.bfloat16))
    spread = spread.reshape(rows, used * group_rank)
    expand = jnp.dot(
        spread, fac_b.reshape(used * group_rank, expand_width), preferred_element_type=jnp.float32
    )
    return (base + expand).astype(jnp.bfloat16)


def solution(mesh):
    in_specs = (
        P(("groups", "dp"), "tensor"),
        P(None, "tensor"),
        P("dp", None, "tensor"),
        P("dp", None, "tensor"),
        P("groups", None),
        P(("groups", "dp"), None),
        P("groups"),
    )
    out_specs = P(("groups", "dp"), "tensor")
    return jax.shard_map(body, mesh=mesh, in_specs=in_specs, out_specs=out_specs, check_vma=False)
```

profile of v0, /device:TPU:0, one launch (start us, length us, event | category | flops | bytes accessed | tf_op | source)
XLA Modules:
  0.0 546.4 jit_solution(14996064826203427636)
XLA Ops:
  6.5 0.8 eq.78
  7.3 1.0 select_reduce_fusion.2
  8.3 0.1 reshape.217
  8.3 0.1 reshape.216
  8.4 0.1 reshape.220
  8.5 15.0 %gather_fusion = bf16[256,16,2048]{2,1,0:T(8,128)(2,1)} fusion(bf16[256,16,2048]{2,1,0:T(8,128)(2,1)} %param.9, s32[1024]{0:T(1024)S(1)} %pad_clamp_fusion), kind=kCustom, calls=%fused_computation | custom fusion | bytes 33555456 | tf_op jit(solution)/shard_map/gather | solution.py:41
  23.6 14.9 %gather_fusion.1 = bf16[256,16,2048]{2,1,0:T(8,128)(2,1)} fusion(bf16[256,16,2048]{2,1,0:T(8,128)(2,1)} %param.10, s32[1024]{0:T(1024)S(1)} %pad_clamp_fusion), kind=kCustom, calls=%fused_computation.1 | custom fusion | bytes 33555456 | tf_op jit(solution)/shard_map/gather | solution.py:46
  38.5 22.7 %broadcast_select_fusion = (bf16[4,64,16,2048]{3,2,1,0:T(8,128)(2,1)}, bf16[4,64,16,2048]{3,2,1,0:T(8,128)(2,1)}) fusion(bf16[4,64,16,2048]{3,2,1,0:T(8,128)(2,1)} %bitcast.23, pred[4,64]{1,0:T(4,128)(4,1)S(1)} %get-tuple-element.7, bf16[4,64,16,2048]{3,2,1,0:T(8,128)(2,1)} %bitcast.22), kind=kLoop, calls=%fused_computation.4 | loop fusion | flops 16777216 | bytes 67109120 | tf_op jit(solution)/shard_map/jit(_where)/select_n | solution.py:44
  61.2 7.0 %all-to-all-start = ((bf16[4,64,16,2048]{3,2,1,0:T(8,128)(2,1)}), bf16[4,64,16,2048]{3,2,1,0:T(8,128)(2,1)}, u32[]{:S(2)}, u32[]{:S(2)}) async-start(bf16[4,64,16,2048]{3,2,1,0:T(8,128)(2,1)} %get-tuple-element.10), calls=%async_computation | async-start | bytes 33554432 | tf_op jit(solution)/shard_map/all_to_all | solution.py:50
  68.2 0.0 all-gather.2.cloned.1.call-start
  68.2 0.7 all-gather.2.cloned.1.call-update
  68.9 183.0 %all-to-all-done = bf16[4,64,16,2048]{3,2,1,0:T(8,128)(2,1)} async-done(((bf16[4,64,16,2048]{3,2,1,0:T(8,128)(2,1)}), bf16[4,64,16,2048]{3,2,1,0:T(8,128)(2,1)}, u32[]{:S(2)}, u32[]{:S(2)}) %all-to-all-start) | async-done | bytes 16777248 | tf_op jit(solution)/shard_map/all_to_all | solution.py:50
  251.9 0.0 copy-start.1
  251.9 7.4 %all-to-all-start.1 = ((bf16[4,64,16,2048]{3,2,1,0:T(8,128)(2,1)}), bf16[4,64,16,2048]{3,2,1,0:T(8,128)(2,1)}, u32[]{:S(2)}, u32[]{:S(2)}) async-start(bf16[4,64,16,2048]{3,2,1,0:T(8,128)(2,1)} %get-tuple-element.9), calls=%async_computation.1 | async-start | bytes 33554432 | tf_op jit(solution)/shard_map/all_to_all | solution.py:51
  259.3 0.0 copy-done.1
  259.3 0.1 copy.15
  259.4 0.1 reduce-window.8
  259.5 0.1 reduce.2
  259.6 0.1 select_reduce_fusion.3
  259.8 0.0 copy-start
  259.8 182.4 %all-to-all-done.1 = bf16[4,64,16,2048]{3,2,1,0:T(8,128)(2,1)} async-done(((bf16[4,64,16,2048]{3,2,1,0:T(8,128)(2,1)}), bf16[4,64,16,2048]{3,2,1,0:T(8,128)(2,1)}, u32[]{:S(2)}, u32[]{:S(2)}) %all-to-all-start.1) | async-done | bytes 16777248 | tf_op jit(solution)/shard_map/all_to_all | solution.py:51
  442.2 19.2 %select_reduce_fusion.1 = (bf16[64,16,2048]{2,1,0:T(8,128)(2,1)S(1)}, bf16[64,16,2048]{2,1,0:T(8,128)(2,1)}) fusion(bf16[4,64,16,2048]{3,2,1,0:T(8,128)(2,1)} %all-to-all-done, pred[4,64]{1,0:T(4,128)(4,1)S(1)} %iota_compare_fusion.3, bf16[4,64,16,2048]{3,2,1,0:T(8,128)(2,1)} %all-to-all-done.1), kind=kLoop, calls=%fused_computation.3 | loop fusion | flops 29360128 | bytes 41943296 | tf_op jit(solution)/shard_map/reduce_sum | solution.py:54
  461.4 0.0 copy-done
  461.4 8.0 %fusion.5 = f32[768,16]{0,1:T(8,128)S(1)} fusion(pred[768,64]{0,1:T(8,128)(4,1)S(1)} %iota_compare_fusion.1, bf16[768,2048]{1,0:T(8,128)(2,1)S(1)} %copy-done, bf16[64,16,2048]{2,1,0:T(8,128)(2,1)S(1)} %get-tuple-element.5), kind=kOutput, calls=%fused_computation.13 | convolution fusion | flops 3222786048 | bytes 7438336 | tf_op jit(solution)/shard_map/rd,skd->rsk/dot_general | solution.py:61
  469.4 20.6 %psum.7 = bf16[768,16]{0,1:T(8,128)(2,1)S(1)} all-reduce(f32[768,16]{0,1:T(8,128)S(1)} %fusion.5), channel_id=1, replica_groups=mesh['groups'=2,'dp'=4,'tensor'=4] {'tensor'}, use_global_device_ids=true, to_apply=%region_5.6 | all-reduce | flops 12288 | bytes 73728 | tf_op jit(solution)/shard_map/psum | solution.py:63
  490.0 14.6 %fusion.1 = f32[768,2048,1]{1,0,2:T(8,128)} fusion(bf16[64,16,2048]{2,1,0:T(8,128)(2,1)} %get-tuple-element.6, pred[768,64]{0,1:T(8,128)(4,1)S(1)} %iota_compare_fusion.1, bf16[768,16]{0,1:T(8,128)(2,1)S(1)} %psum.7), kind=kOutput, calls=%fused_computation.8 | convolution fusion | flops 3222011904 | bytes 10559488 | tf_op jit(solution)/shard_map/dot_general | solution.py:67
  504.6 0.0 all-gather.2.cloned.1.call-done
  504.6 34.9 %fusion = bf16[768,2048]{1,0:T(8,128)(2,1)} fusion(f32[768,2048,1]{1,0,2:T(8,128)} %fusion.1, bf16[768,8192]{1,0:T(8,128)(2,1)} %all-gather.2.cloned.1.call-done, bf16[8192,2048]{1,0:T(8,128)(2,1)} %param.8), kind=kOutput, calls=%fused_computation.7 | convolution fusion | flops 25772949504 | bytes 55574528 | tf_op jit(solution)/shard_map/dot_general | solution.py:24
  (6 shorter events, 0.1 us)
Async XLA Ops:
  61.2 190.7 %all-to-all-start = ((bf16[4,64,16,2048]{3,2,1,0:T(8,128)(2,1)}), bf16[4,64,16,2048]{3,2,1,0:T(8,128)(2,1)}, u32[]{:S(2)}, u32[]{:S(2)}) async-start(bf16[4,64,16,2048]{3,2,1,0:T(8,128)(2,1)} %get-tuple-element.10), calls=%async_computation | async-start | bytes 33554432 | tf_op jit(solution)/shard_map/all_to_all | solution.py:50
  68.2 436.4 %all-gather.2.cloned.1.call-start = ((), (), s32[]{:S(2)}) async-start(), calls=%async_computation.2 | async-start | bytes 15728640 | tf_op jit(solution)/shard_map/all_gather | solution.py:25
  251.9 7.4 %copy-start.1 = (s32[1,64]{1,0:T(1,128)S(1)}, s32[1,64]{1,0:T(1,128)}, u32[]{:S(2)}) copy-start(s32[1,64]{1,0:T(1,128)} %param.12) | copy-start | bytes 772
  251.9 190.3 %all-to-all-start.1 = ((bf16[4,64,16,2048]{3,2,1,0:T(8,128)(2,1)}), bf16[4,64,16,2048]{3,2,1,0:T(8,128)(2,1)}, u32[]{:S(2)}, u32[]{:S(2)}) async-start(bf16[4,64,16,2048]{3,2,1,0:T(8,128)(2,1)} %get-tuple-element.9), calls=%async_computation.1 | async-start | bytes 33554432 | tf_op jit(solution)/shard_map/all_to_all | solution.py:51
  259.8 201.6 %copy-start = (bf16[768,2048]{1,0:T(8,128)(2,1)S(1)}, bf16[768,2048]{1,0:T(8,128)(2,1)}, u32[]{:S(2)}) copy-start(bf16[768,2048]{1,0:T(8,128)(2,1)} %param.7) | copy-start | bytes 9437188
Sparse Core Ops, SparseCore 0:
  70.6 221.6 all-gather.1
where the time goes:
time: 547 us; the launch traced here: 546 us
  waiting for transfers between devices  366 us (67%)
  matrix products  57.6 us (11%)
  other arithmetic  43.2 us (8%)
  local copies, waits for them, and re-layouts  31.1 us (6%)
  blocking collectives  20.6 us (4%)
  starting transfers between devices  14.4 us (3%)
  between operations  13.5 us (2%)
    all_to_all x1, waiting for transfers between devices, body(): lax.all_to_all(outgoing_shrink, 'dp', split_axis=0, concat_axis=0, tiled=...  183 us
    all_to_all x1, waiting for transfers between devices, body(): lax.all_to_all(outgoing_expand, 'dp', split_axis=0, concat_axis=0, tiled=...  182 us
    dot_general x1, matrix products, body(): jnp.dot(lax.all_gather(tokens, 'tensor', axis=1, tiled=True), query_base_...  34.9 us
    select_n x1, other arithmetic, body(): jnp.where(owned_by_group[:, :, None, None], stored_expand_factors[lookup_...  22.7 us
    psum x1, blocking collectives, body(): shrink = lax.psum(partial_value, 'tensor')  20.6 us
    reduce_sum x1, other arithmetic, body(): jnp.sum(jnp.where(pick[:, :, None, None], recv_a, jnp.zeros((), jnp.bfloa...  19.2 us
    gather x1, local copies, waits for them, and re-layouts, body(): stored_shrink_factors[lookup_index]  15 us
    gather x1, local copies, waits for them, and re-layouts, body(): stored_expand_factors[lookup_index]  14.9 us
  transfers between devices with their start and end apart: 3, of which 2 were waited for; matrix products, arithmetic and copies ran while one was open for 8% of the time, Pallas kernels for 0%

commit v1 on v0

v1 whole, which is shorter than its diff:
```python
import functools

import jax
import jax.numpy as jnp
from jax import lax
from jax.experimental import pallas as pl
from jax.experimental.pallas import tpu as pltpu
from jax.sharding import PartitionSpec as P

F32 = jnp.float32
BF16 = jnp.bfloat16
ROOM = 48 * 1024 * 1024
TILE = 512


class Order:
    def __init__(self, first):
        self.last = first

    def call(self, kernel, at, args, specs, waits=(), **rest):
        after = [] if rest.get("input_output_aliases") else [self.last]
        after += waits

        def body(at_ref, *refs):
            kernel(at_ref, *refs[: len(args)], *refs[len(args) + len(after) :])

        outs = pl.pallas_call(
            body,
            grid_spec=pltpu.PrefetchScalarGridSpec(
                num_scalar_prefetch=1,
                in_specs=list(specs) + [pl.BlockSpec(memory_space=pl.ANY)] * len(after),
                **rest.pop("grid_spec"),
            ),
            compiler_params=pltpu.CompilerParams(vmem_limit_bytes=ROOM),
            cost_estimate=pl.CostEstimate(flops=1, bytes_accessed=1, transcendentals=0),
            **rest,
        )(at, *args, *after)
        self.last = outs[0] if isinstance(outs, (list, tuple)) else outs
        return outs


    def hold(self, x):
        self.last = pl.pallas_call(
            lambda *_: None,
            out_shape=jax.ShapeDtypeStruct(x.shape, x.dtype),
            in_specs=[pl.BlockSpec(memory_space=pl.ANY)] * 2,
            out_specs=pl.BlockSpec(memory_space=pl.ANY),
            input_output_aliases={0: 0},
            cost_estimate=pl.CostEstimate(flops=1, bytes_accessed=1, transcendentals=0),
        )(x, self.last)
        return self.last


def fetch_kernel(lists_ref, *refs, stores, plan):
    outs, (held, in_sem, out_sem) = refs[stores:-3], refs[-3:]
    count = held.shape[1]
    steps = [(o, at, s, n) for o, pairs in enumerate(plan) for at, (s, n) in enumerate(pairs)]
    for i, (_, _, s, n) in enumerate(steps):
        @pl.loop(0, count)
        def _(j, i=i, s=s, n=n):
            pltpu.make_async_copy(
                refs[s].at[lists_ref[n, j]], held.at[i, j], in_sem.at[i]
            ).start()
    copies = []
    for i, (o, at, _, _) in enumerate(steps):
        pltpu.make_async_copy(held.at[i], held.at[i], in_sem.at[i]).wait()
        copies.append(
            pltpu.make_async_copy(
                held.at[i], outs[o].at[pl.ds(at * count, count)], out_sem.at[i]
            )
        )
        copies[-1].start()
    for copy in copies:
        copy.wait()


def fetch(order, lists, stores, plan):
    count = lists.shape[1]
    shape = stores[0].shape[1:]
    total = sum(map(len, plan))
    outs = order.call(
        functools.partial(fetch_kernel, stores=len(stores), plan=plan),
        lists,
        stores,
        [pl.BlockSpec(memory_space=pl.ANY)] * len(stores),
        out_shape=[jax.ShapeDtypeStruct((len(p) * count,) + shape, BF16) for p in plan],
        grid_spec=dict(
            grid=(1,),
            out_specs=[pl.BlockSpec(memory_space=pl.ANY)] * len(plan),
            scratch_shapes=[
                pltpu.VMEM((total, count) + shape, BF16),
                pltpu.SemaphoreType.DMA((total,)),
                pltpu.SemaphoreType.DMA((total,)),
            ],
        ),
    )
    return [o.reshape(o.shape[0] * shape[0], shape[1]) for o in outs]


def sum_kernel(at_ref, *refs, plan, has_total, has_out, rounded):
    refs = list(refs)
    factors = [([refs.pop(0) for _ in range(n)], refs.pop(0)) for n in plan]
    total = refs.pop(0) if has_total else None
    if has_out:
        refs.pop(0)
    out = refs.pop(0)
    value = total[...] if has_total else None
    for xs, w in factors:
        if len(xs) == 2:
            both = refs.pop(0)

            @pl.when(pl.program_id(0) == 0)
            def _(xs=xs, both=both):
                both[...] = xs[0][...] + xs[1][...]

            x = both
        else:
            x = xs[0]
        product = jnp.dot(x[...], w[...], preferred_element_type=F32)
        value = product if value is None else value + product
    out[...] = value.astype(BF16) if rounded else value


def add_products(order, terms, total=None, take=0, piece=(0, 1), out=None, rounded=False):
    rows = terms[0][0][0].shape[0]
    width = terms[0][1].shape[1]
    tile = min(TILE, width)
    at = jnp.stack([jnp.asarray(t[2], jnp.int32) for t in terms])
    here = piece[0]
    specs, args, scratch = [], [], []
    for n, (xs, w, _) in enumerate(terms):
        depth = xs[0].shape[1]
        for x in xs:
            specs.append(pl.BlockSpec((rows, depth), lambda j, at: (0, 0)))
            args.append(x)
        specs.append(pl.BlockSpec((depth, tile), lambda j, at, n=n: (at[n], j)))
        args.append(w)
        if len(xs) == 2:
            scratch.append(pltpu.VMEM((rows, depth), BF16))
    if total is not None:
        specs.append(pl.BlockSpec((rows, tile), lambda j, at: (take, j)))
        args.append(total)
    aliases = {}
    if out is not None:
        aliases = {len(args) + 1: 0}
        specs.append(pl.BlockSpec(memory_space=pl.ANY))
        args.append(out)
    dtype = BF16 if rounded else F32
    return order.call(
        functools.partial(
            sum_kernel,
            plan=[len(t[0]) for t in terms],
            has_total=total is not None,
            has_out=out is not None,
            rounded=rounded,
        ),
        at,
        args,
        specs,
        out_shape=jax.ShapeDtypeStruct((rows * piece[1], width), dtype),
        grid_spec=dict(
            grid=(width // tile,),
            out_specs=pl.BlockSpec((rows, tile), lambda j, at: (here, j)),
            scratch_shapes=scratch,
        ),
        input_output_aliases=aliases,
    )


def shrink_kernel(at_ref, code_ref, x_ref, *refs, most, rank):
    blocks, out = refs[:-1], refs[-1]
    value = 0.0
    width = most * rank
    place = lax.broadcasted_iota(jnp.int32, (width, 1), 0) // rank
    fold = lax.broadcasted_iota(jnp.int32, (rank, width), 1) % rank == lax.broadcasted_iota(
        jnp.int32, (rank, width), 0
    )
    for n, block in enumerate(blocks):
        product = lax.dot_general(
            block[...], x_ref[...], (((1,), (1,)), ((), ())), preferred_element_type=F32
        )
        value = value + jnp.where(at_ref[n] * most + place == code_ref[...], product, 0.0)
    out[...] = jnp.dot(
        fold.astype(F32), value, precision=lax.Precision.HIGHEST, preferred_element_type=F32
    )


def shrink_parts(order, tokens, blocks, at, code, most, rank, waits=()):
    rows, depth = tokens.shape
    width = most * rank
    full = lambda *_: (0, 0)
    return order.call(
        functools.partial(shrink_kernel, most=most, rank=rank),
        jnp.stack(at),
        [code[None, :], tokens, *blocks],
        [pl.BlockSpec((1, rows), full), pl.BlockSpec((rows, depth), full)]
        + [pl.BlockSpec((width, depth), full)] * len(blocks),
        waits=list(waits),
        out_shape=jax.ShapeDtypeStruct((rank, rows), F32),
        grid_spec=dict(grid=(1,), out_specs=pl.BlockSpec((rank, rows), full)),
    )


def body(
    tokens,
    query_base_weight,
    stored_shrink_factors,
    stored_expand_factors,
    segment_adapter,
    segment_length,
    adapter_storage_slot,
):
    groups = lax.axis_size("dp")
    lanes = lax.axis_size("tensor")
    me = lax.axis_index("dp")
    stored, rank, depth = stored_shrink_factors.shape
    used = segment_adapter.shape[1]
    most = used // 2
    rows = tokens.shape[0]
    count_all = adapter_storage_slot.shape[0]

    flat_ids = segment_adapter.reshape(-1)
    match = flat_ids[:, None] == jnp.arange(count_all, dtype=jnp.int32)[None, :]
    slot = jnp.sum(jnp.where(match, adapter_storage_slot[None, :], 0), axis=1)
    slot = slot.reshape(groups, used)
    home, local = slot // stored, slot % stored

    earlier = jnp.arange(used)[None, :] < jnp.arange(used)[:, None]
    same = home[:, :, None] == home[:, None, :]
    place = jnp.sum(jnp.where(same & earlier[None], 1, 0), axis=2)

    mine = (home == me)[:, :, None] & (place[:, :, None] == jnp.arange(most)[None, None, :])
    lists = jnp.sum(jnp.where(mine, local[:, :, None], 0), axis=1)
    to = me ^ jnp.arange(groups, dtype=jnp.int32)
    lists = jnp.sum(jnp.where((to[:, None] == jnp.arange(groups)[None])[:, :, None], lists[None], 0), axis=1)

    def send(block, k):
        return lax.ppermute(block, "dp", [(i, i ^ k) for i in range(groups)])

    here = (jnp.arange(groups) == me)[:, None]
    code_of = jnp.sum(jnp.where(here, home * most + place, 0), axis=0)
    ends = jnp.cumsum(segment_length[0])
    row_ids = jnp.arange(rows, dtype=jnp.int32)
    starts = ends - segment_length[0]
    member = (starts[None, :] <= row_ids[:, None]) & (row_ids[:, None] < ends[None, :])
    code = jnp.sum(jnp.where(member, code_of[None, :], 0), axis=1)

    half = groups // 2
    order = Order(code)
    stores = [stored_shrink_factors, stored_expand_factors]
    pairs = [(k, k + 1) for k in range(half, groups, 2)]
    far_a = fetch(order, lists, stores, [[(0, k), (0, l)] for k, l in pairs])
    far_a = [send(x, k) for x, (k, _) in zip(far_a, pairs)]
    rest = fetch(
        order,
        lists,
        stores,
        [[(s, k)] for s in range(2) for k in range(half)] + [[(1, k)] for k in range(half, groups)],
    )
    near_a, near_b, far_b = rest[:half], rest[half : 2 * half], rest[2 * half :]
    near_a = near_a[:1] + [send(x, k) for k, x in enumerate(near_a[1:], 1)]
    near_b = near_b[:1] + [send(x, k) for k, x in enumerate(near_b[1:], 1)]

    weight = query_base_weight
    line = lax.axis_index("tensor")

    def shrink_of(blocks, ks):
        return shrink_parts(order, tokens, blocks, [me ^ k for k in ks], code, most, rank)

    part = shrink_of(near_a, range(half))
    near_b = near_b[:1] + [order.hold(x) for x in near_b[1:]]
    if lanes == 4:
        swap = [(0, 1), (1, 0), (2, 3), (3, 2)]
        middle = [(1, 2), (2, 1)]
        outward = [(1, 0), (2, 3)]
        near = order.hold(lax.ppermute(tokens, "tensor", swap))
        cross = order.hold(lax.ppermute(tokens, "tensor", middle))
        far = lax.ppermute(near, "tensor", middle)
        out_near = lax.ppermute(cross, "tensor", outward)
        own = add_products(order, [([tokens], weight, line), ([near], weight, line ^ 1)])

    deep = most * rank
    far_a = [order.hold(x) for x in far_a]
    handed = [
        [send(x[deep + i * deep // 2 : deep + (i + 1) * deep // 2], 1) for i in range(2)]
        for x in far_a
    ]
    part = part + shrink_of(far_a, [k for k, _ in pairs])
    part = part + shrink_of([jnp.concatenate(h) for h in handed], [l for _, l in pairs])
    far_b = [far_b[i] if i % 2 else order.hold(far_b[i]) for i in range(half)]
    far_b = [send(x, k) for k, x in enumerate(far_b, half)]
    if lanes == 4:
        pieces = 2
        step = rows // pieces

        def onward(i):
            return lax.ppermute(far[i * step : (i + 1) * step], "tensor", outward)

        shrink = part + lax.ppermute(part, "tensor", [(i, i ^ 1) for i in range(4)])
        out_near = order.hold(out_near)
        shrink = order.hold(shrink)
        shrink = shrink + lax.ppermute(shrink, "tensor", [(i, i ^ 2) for i in range(4)])
        far = order.hold(far)
        out_far = [onward(i) for i in range(pieces)]
        own = add_products(order, [([far, out_near], weight, line ^ 2)], own)
    else:
        shrink = lax.psum(part, "tensor")
    low = shrink.astype(BF16)
    column = jnp.arange(most * rank, dtype=jnp.int32)
    fold = (column[None, :] % rank == jnp.arange(rank)[:, None]).astype(BF16)
    spread = lax.dot_general(
        low, fold, (((0,), (0,)), ((), ())), preferred_element_type=F32
    ).astype(BF16)

    def chosen(k):
        mine = ((me ^ k) * most + column // rank)[None, :] == code[:, None]
        return jnp.where(mine, spread, jnp.zeros((), BF16))

    near_terms = [([chosen(k)], near_b[k], 0) for k in range(half)]
    far_terms = [([chosen(k)], x, 0) for k, x in enumerate(far_b, half)]

    if lanes != 4:
        whole = lax.all_gather(tokens, "tensor", axis=1, tiled=True)
        base = jnp.dot(whole, weight, preferred_element_type=F32)
        for (x,), w, i in near_terms + far_terms:
            base = base + jnp.dot(x, w[i * deep : (i + 1) * deep], preferred_element_type=F32)
        return base.astype(BF16)

    total = add_products(order, near_terms, own)

    def last_slice(i):
        return [([cross[i * step : (i + 1) * step], out_far[i]], weight, line ^ 3)]

    first = add_products(order, last_slice(0), total, 0)

    def far_part(i):
        return [([x[i * step : (i + 1) * step] for x in xs], w, n) for xs, w, n in far_terms]

    out = add_products(order, far_part(0), first, 0, (0, pieces), None, True)
    second = add_products(order, far_part(1), total, 1)
    return add_products(order, last_slice(1), second, 0, (1, pieces), out, True)


def solution(mesh):
    in_specs = (
        P(("groups", "dp"), "tensor"),
        P(None, "tensor"),
        P("dp", None, "tensor"),
        P("dp", None, "tensor"),
        P("groups", None),
        P(("groups", "dp"), None),
        P("groups"),
    )
    out_specs = P(("groups", "dp"), "tensor")
    return jax.shard_map(body, mesh=mesh, in_specs=in_specs, out_specs=out_specs, check_vma=False)
```

time: 547 us -> 245 us (0.45)
  waiting for transfers between devices: 366 us -> 91.4 us
  Pallas kernels: 0 us -> 103 us
  matrix products: 57.6 us -> 0.72 us
  other arithmetic: 43.2 us -> 5.1 us
  blocking collectives: 20.6 us -> 0 us
  local copies, waits for them, and re-layouts: 31.1 us -> 15.6 us
  starting transfers between devices: 14.4 us -> 27.8 us
  between operations: 13.5 us -> 0.23 us
    all_to_all x2 -> x0, waiting for transfers between devices: 365 us -> none  [the longest x1 183 us: body(): lax.all_to_all(outgoing_shrink, 'dp', split_axis=0, concat_axis=0, tiled=...]
    pallas_call x0 -> x20, Pallas kernels: none -> 103 us  [the longest x12 103 us: call(): pl.pallas_call(body, grid_spec=pltpu.PrefetchScalarGridSpec(num_scalar_pr...]
    ppermute x0 -> x15, waiting for transfers between devices: none -> 91.4 us  [the longest x1 38.1 us: body(): near = order.hold(lax.ppermute(tokens, 'tensor', swap))]
    dot_general x3 -> x1, matrix products: 57.6 us -> 0.72 us  [body(): lax.dot_general(low, fold, (((0,), (0,)), ((), ())), preferred_element_ty...]
    gather x2 -> x0, local copies, waits for them, and re-layouts: 30 us -> none  [the longest x1 15 us: body(): stored_shrink_factors[lookup_index]]
    ppermute x0 -> x15, starting transfers between devices: none -> 27.8 us  [the longest x1 7.8 us: body(): shrink = part + lax.ppermute(part, 'tensor', [(i, i ^ 1) for i in range(4)])]
    select_n x2, other arithmetic: 22.7 us -> 0.01 us  [the longest x1 0.01 us: body(): home, local = (slot // stored, slot % stored)]
    psum x1 -> x0, blocking collectives: 20.6 us -> none  [body(): shrink = lax.psum(partial_value, 'tensor')]
  transfers between devices with their start and end apart: 3 -> 15, of which waited for: 2 -> 5; matrix products, arithmetic and copies ran while one was open for 8% -> 5% of each run, Pallas kernels for 0% -> 37%
where the time goes in v1:
time: 245 us; the launch traced here: 244 us
  Pallas kernels  103 us (42%)
  waiting for transfers between devices  91.4 us (37%)
  starting transfers between devices  27.8 us (11%)
  local copies, waits for them, and re-layouts  15.6 us (6%)
  other arithmetic  5.1 us (2%)
    pallas_call x12, Pallas kernels, call(): pl.pallas_call(body, grid_spec=pltpu.PrefetchScalarGridSpec(num_scalar_pr...  103 us
    ppermute x1, waiting for transfers between devices, body(): near = order.hold(lax.ppermute(tokens, 'tensor', swap))  38.1 us
    ppermute x1, waiting for transfers between devices, body(): shrink = part + lax.ppermute(part, 'tensor', [(i, i ^ 1) for i in range(4)])  31.8 us
    ppermute x2, waiting for transfers between devices, onward(): return lax.ppermute(far[i * step:(i + 1) * step], 'tensor', outward)  17.6 us
    ppermute x1, starting transfers between devices, body(): shrink = part + lax.ppermute(part, 'tensor', [(i, i ^ 1) for i in range(4)])  7.8 us
    ppermute x7, starting transfers between devices, send(): return lax.ppermute(block, 'dp', [(i, i ^ k) for i in range(groups)])  5.37 us
  transfers between devices with their start and end apart: 15, of which 5 were waited for; matrix products, arithmetic and copies ran while one was open for 5% of the time, Pallas kernels for 37%

profile of v1, /device:TPU:0, one launch (start us, length us, event | category | flops | bytes accessed | tf_op | source)
XLA Modules:
  0.0 244.2 jit_solution(4031122327752246229)
XLA Ops:
  0.0 0.8 eq.142
  0.8 1.0 select_reduce_fusion
  1.7 0.1 reshape.205
  1.9 0.7 copy.19
  2.6 0.1 reduce-window.4
  2.7 0.1 reduce
  2.8 0.7 fusion.15
  3.5 0.1 iota_compare_fusion.7
  3.6 0.2 select_reduce_fusion.2
  3.8 0.1 select_reduce_fusion.5
  3.9 0.1 select_reduce_fusion.1.refs_2_
  4.0 0.1 select_reduce_fusion.3
  4.2 0.1 select_reduce_fusion.4.at_ref
  4.3 0.0 copy-start
  4.3 5.3 %shard_map.73.refs_2_ = bf16[64,16,2048]{2,1,0:T(8,128)(2,1)} custom-call(s32[4,32]{1,0:T(4,128)S(1)} %select_reduce_fusion.4.at_ref, bf16[256,16,2048]{2,1,0:T(8,128)(2,1)} %refs_0_.4, bf16[256,16,2048]{2,1,0:T(8,128)(2,1)} %refs_1_.7, s32[768]{0:T(1024)S(1)} %select_reduce_fusion.1.refs_2_), custom_call_target="tpu_custom_call" | custom-call | flops 1 | bytes 1 | tf_op jit(solution)/shard_map/pallas_call | solution.py:27
  9.6 3.7 %collective-permute-start.5 = (bf16[1024,2048]{1,0:T(8,128)(2,1)}, bf16[1024,2048]{1,0:T(8,128)(2,1)}, u32[]{:S(2)}, u32[]{:S(2)}) collective-permute-start(bf16[1024,2048]{1,0:T(8,128)(2,1)} %bitcast.9), channel_id=1, source_target_pairs={{0,8},{4,12},{8,0},{12,4},{1,9},{5,13},{9,1},{13,5},{2,10},{6,14},... | collective-permute-start | bytes 12582920 | tf_op jit(solution)/shard_map/ppermute | solution.py:238
  13.2 1.6 collective-permute-start.1
  14.8 2.3 collective-permute-start
  17.1 13.0 %shard_map.74 = (bf16[32,16,2048]{2,1,0:T(8,128)(2,1)S(1)}, bf16[32,16,2048]{2,1,0:T(8,128)(2,1)}, bf16[32,16,2048]{2,1,0:T(8,128)(2,1)}, bf16[32,16,2048]{2,1,0...) custom-call(s32[4,32]{1,0:T(4,128)S(1)} %select_reduce_fusion.4.at_ref, ...), custom_call_target="tpu_custom_call" | custom-call | flops 1 | bytes 1 | tf_op jit(solution)/shard_map/pallas_call | solution.py:27
  30.2 1.3 copy-done.2
  31.5 0.0 collective-permute-start.3
  31.5 0.5 collective-permute-start.2
  32.0 0.1 pad_add_fusion.at_ref
  32.1 3.9 %collective-permute-done.3.refs_3_ = bf16[512,2048]{1,0:T(8,128)(2,1)} collective-permute-done((bf16[512,2048]{1,0:T(8,128)(2,1)}, bf16[512,2048]{1,0:T(8,128)(2,1)}, u32[]{:S(2)}, u32[]{:S(2)}) %collective-permute-start.3) | collective-permute-done | bytes 2097184 | tf_op jit(solution)/shard_map/ppermute | solution.py:238
  36.0 1.6 copy-done.3
  37.6 7.2 %shard_map.75.__1_ = f32[16,768]{1,0:T(8,128)S(1)} custom-call(s32[2]{0:T(128)S(1)} %pad_add_fusion.at_ref, s32[1,768]{1,0:T(1,128)S(1)} %broadcast_in_dim.129.refs_0_, bf16[768,2048]{1,0:T(8,128)(2,1)} %refs_1_.11, bf16[512,2048]{1,0:T(8,128)(2,1)S(1)} %bitcast.22, bf16[512,2048]{1,0:T(8,128)(2,1)} %collective-permute-done.3.refs_3_, ...), custom_call_target="tpu_custom_call" | custom-call | flops 1 | bytes 1 | tf_op jit(solution)/shard_map/pallas_call | solution.py:27
  44.8 0.6 copy-done.5
  45.4 0.0 collective-permute-done.2.__0_
  45.4 38.1 %collective-permute-done.1.__0_ = bf16[768,2048]{1,0:T(8,128)(2,1)} collective-permute-done((bf16[768,2048]{1,0:T(8,128)(2,1)S(1)}, bf16[768,2048]{1,0:T(8,128)(2,1)}, u32[]{:S(2)}, u32[]{:S(2)}) %collective-permute-start.1) | collective-permute-done | bytes 3145760 | tf_op jit(solution)/shard_map/ppermute | solution.py:276
  83.5 0.0 collective-permute-done.__0_
  83.6 1.6 collective-permute-start.9
  85.1 2.3 collective-permute-start.4
  87.4 0.1 pad_add_fusion.1.at_ref
  87.5 18.7 %shard_map.79.__1_.refs_3_ = f32[768,2048]{1,0:T(8,128)} custom-call(s32[2]{0:T(128)S(1)} %pad_add_fusion.1.at_ref, bf16[768,2048]{1,0:T(8,128)(2,1)S(1)} %copy-done.1, bf16[8192,2048]{1,0:T(8,128)(2,1)} %refs_2_.5, bf16[768,2048]{1,0:T(8,128)(2,1)} %shard_map.77.__1_.refs_2_, bf16[8192,2048]{1,0:T(8,128)(2,1)} %refs_2_.5, bf16[768,2048]{1,0:T(8,128)(2,1)} %shard_map.78.refs_4_), custom_call_target="tpu_custom_call" | custom-call | flops 1 | bytes 1 | tf_op jit(solution)/shard_map/pallas_call | solution.py:27
  106.2 0.0 collective-permute-done.5.__0_
  106.2 3.1 %fusion.16 = (bf16[256,2048]{1,0:T(8,128)(2,1)}, bf16[256,2048]{1,0:T(8,128)(2,1)}) fusion(bf16[1024,2048]{1,0:T(8,128)(2,1)} %shard_map.80.refs_2_.refs_3_), kind=kLoop, calls=%fused_computation.54 | loop fusion | bytes 4194304 | tf_op jit(solution)/shard_map/slice | solution.py:285
  109.3 0.0 collective-permute-start.6
  109.3 0.5 collective-permute-start.7
  109.8 0.0 collective-permute-start.13
  109.8 4.5 %shard_map.81.refs_3_ = f32[16,768]{1,0:T(8,128)S(1)} custom-call(s32[1]{0:T(128)} %bitcast.8.at_ref, s32[1,768]{1,0:T(1,128)S(1)} %broadcast_in_dim.129.refs_0_, bf16[768,2048]{1,0:T(8,128)(2,1)S(1)} %copy-done.1, bf16[1024,2048]{1,0:T(8,128)(2,1)} %shard_map.80.refs_2_.refs_3_, bf16[1024,2048]{1,0:T(8,128)(2,1)} %shard_map.80.refs_2_.refs_3_), custom_call_target="tpu_custom_call" | custom-call | flops 1 | bytes 1 | tf_op jit(solution)/shard_map/pallas_call | solution.py:27
  114.3 0.0 collective-permute-done.6
  114.3 0.0 collective-permute-done.7
  114.3 1.7 pad_maximum_fusion.refs_2_
  116.0 2.9 %shard_map.82.__1_ = f32[16,768]{1,0:T(8,128)S(1)} custom-call(s32[1]{0:T(128)} %bitcast.12.at_ref, s32[1,768]{1,0:T(1,128)S(1)} %broadcast_in_dim.129.refs_0_, bf16[768,2048]{1,0:T(8,128)(2,1)S(1)} %copy-done.1, bf16[512,2048]{1,0:T(8,128)(2,1)S(1)} %pad_maximum_fusion.refs_2_, f32[16,768]{1,0:T(8,128)S(1)} %shard_map.81.refs_3_), custom_call_target="tpu_custom_call" | custom-call | flops 1 | bytes 1 | tf_op jit(solution)/shard_map/pallas_call | solution.py:27
  119.0 7.8 %collective-permute-start.8 = (f32[16,768]{1,0:T(8,128)S(1)}, f32[16,768]{1,0:T(8,128)S(1)}, u32[]{:S(2)}, u32[]{:S(2)}) collective-permute-start(f32[16,768]{1,0:T(8,128)S(1)} %add_add_fusion), channel_id=1, source_target_pairs={{0,1},{1,0},{2,3},{3,2},{4,5},{5,4},{6,7},{7,6},{8,9},{9,8},{10,11... | collective-permute-start | bytes 147464 | tf_op jit(solution)/shard_map/ppermute | solution.py:299
  126.8 31.8 %collective-permute-done.8 = f32[16,768]{1,0:T(8,128)S(1)} collective-permute-done((f32[16,768]{1,0:T(8,128)S(1)}, f32[16,768]{1,0:T(8,128)S(1)}, u32[]{:S(2)}, u32[]{:S(2)}) %collective-permute-start.8) | collective-permute-done | bytes 49184 | tf_op jit(solution)/shard_map/ppermute | solution.py:299
  158.6 0.6 add.106.__0_
  159.2 0.7 collective-permute-start.12
  159.9 4.1 %fusion.17 = (bf16[384,2048]{1,0:T(8,128)(2,1)}, bf16[384,2048]{1,0:T(8,128)(2,1)}) fusion(bf16[768,2048]{1,0:T(8,128)(2,1)} %shard_map.86.refs_0_.refs_4_), kind=kLoop, calls=%fused_computation.55 | loop fusion | bytes 6291456 | tf_op jit(solution)/shard_map/slice | solution.py:297
  164.0 1.3 collective-permute-start.14
  165.3 1.5 collective-permute-start.10
  166.9 4.1 %collective-permute-start.11 = (f32[16,768]{1,0:T(8,128)S(1)}, f32[16,768]{1,0:T(8,128)S(1)}, u32[]{:S(2)}, u32[]{:S(2)}) collective-permute-start(f32[16,768]{1,0:T(8,128)S(1)} %copy-done.8), channel_id=1, source_target_pairs={{0,2},{1,3},{2,0},{3,1},{4,6},{5,7},{6,4},{7,5},{8,10},{9,11},{10,... | collective-permute-start | bytes 147464 | tf_op jit(solution)/shard_map/ppermute | solution.py:302
  171.0 2.3 fusion.18
  173.3 14.0 %shard_map.87.refs_4_.refs_5_ = f32[768,2048]{1,0:T(8,128)} custom-call(s32[1]{0:T(128)} %bitcast.16.at_ref, bf16[768,2048]{1,0:T(8,128)(2,1)} %shard_map.86.refs_0_.refs_4_, bf16[768,2048]{1,0:T(8,128)(2,1)} %shard_map.84.__1_.refs_1_, bf16[8192,2048]{1,0:T(8,128)(2,1)} %refs_2_.5, f32[768,2048]{1,0:T(8,128)} %shard_map.79.__1_.refs_3_, ...), custom_call_target="tpu_custom_call" | custom-call | flops 1 | bytes 1 | tf_op jit(solution)/shard_map/pallas_call | solution.py:27
  187.2 0.7 compare_select_fusion
  188.0 0.8 copy-done.4
  188.8 8.9 %shard_map.88.refs_3_.refs_4_ = f32[768,2048]{1,0:T(8,128)} custom-call(s32[2]{0:T(128)S(1)} %broadcast_5_at_ref.2.at_ref, bf16[768,512]{1,0:T(8,128)(2,1)S(1)} %get-tuple-element.26.refs_0_, bf16[512,2048]{1,0:T(8,128)(2,1)S(1)} %bitcast.23, bf16[768,512]{1,0:T(8,128)(2,1)S(1)} %get-tuple-element.25.refs_2_, bf16[512,2048]{1,0:T(8,128)(2,1)} %shard_map.76.__1_.refs_3_, ...), custom_call_target="tpu_custom_call" | custom-call | flops 1 | bytes 1 | tf_op jit(solution)/shard_map/pallas_call | solution.py:27
  197.7 0.1 fusion.19
  197.8 7.0 %collective-permute-done.14.refs_1_ = bf16[384,2048]{1,0:T(8,128)(2,1)S(1)} collective-permute-done((bf16[384,2048]{1,0:T(8,128)(2,1)}, bf16[384,2048]{1,0:T(8,128)(2,1)S(1)}, u32[]{:S(2)}, u32[]{:S(2)}) %collective-permute-start.14) | collective-permute-done | bytes 1572896 | tf_op jit(solution)/shard_map/ppermute | solution.py:297
  204.8 8.4 %shard_map.89.refs_4_.refs_5_ = f32[384,2048]{1,0:T(8,128)} custom-call(s32[1]{0:T(128)} %bitcast.at_ref, bf16[384,2048]{1,0:T(8,128)(2,1)S(1)} %get-tuple-element.23.refs_0_, bf16[384,2048]{1,0:T(8,128)(2,1)S(1)} %collective-permute-done.14.refs_1_, bf16[8192,2048]{1,0:T(8,128)(2,1)} %refs_2_.5, f32[768,2048]{1,0:T(8,128)} %shard_map.88.refs_3_.refs_4_, ...), custom_call_target="tpu_custom_call" | custom-call | flops 1 | bytes 1 | tf_op jit(solution)/shard_map/pallas_call | solution.py:27
  213.2 6.0 %shard_map.90.refs_5_.refs_4_ = bf16[768,2048]{1,0:T(8,128)(2,1)} custom-call(s32[2]{0:T(128)S(1)} %broadcast_5_at_ref.2.at_ref, bf16[384,512]{1,0:T(8,128)(2,1)S(1)} %get-tuple-element.34.refs_0_, bf16[512,2048]{1,0:T(8,128)(2,1)S(1)} %collective-permute-done.12.refs_1_, bf16[384,512]{1,0:T(8,128)(2,1)S(1)} %get-tuple-element.29.refs_2_, ...), custom_call_target="tpu_custom_call" | custom-call | flops 1 | bytes 1 | tf_op jit(solution)/shard_map/pallas_call | solution.py:27
  219.2 6.5 %shard_map.91.refs_3_ = f32[384,2048]{1,0:T(8,128)} custom-call(s32[2]{0:T(128)S(1)} %broadcast_5_at_ref.2.at_ref, bf16[384,512]{1,0:T(8,128)(2,1)S(1)} %get-tuple-element.33.refs_0_, bf16[512,2048]{1,0:T(8,128)(2,1)S(1)} %collective-permute-done.12.refs_1_, bf16[384,512]{1,0:T(8,128)(2,1)S(1)} %get-tuple-element.30.refs_2_, ...), custom_call_target="tpu_custom_call" | custom-call | flops 1 | bytes 1 | tf_op jit(solution)/shard_map/pallas_call | solution.py:27
  225.7 10.6 %collective-permute-done.10.refs_1_ = bf16[384,2048]{1,0:T(8,128)(2,1)S(1)} collective-permute-done((bf16[384,2048]{1,0:T(8,128)(2,1)}, bf16[384,2048]{1,0:T(8,128)(2,1)S(1)}, u32[]{:S(2)}, u32[]{:S(2)}) %collective-permute-start.10) | collective-permute-done | bytes 1572896 | tf_op jit(solution)/shard_map/ppermute | solution.py:297
  236.2 7.9 %shard_map.92 = bf16[768,2048]{1,0:T(8,128)(2,1)} custom-call(s32[1]{0:T(128)} %bitcast.at_ref, bf16[384,2048]{1,0:T(8,128)(2,1)S(1)} %get-tuple-element.24.refs_0_, bf16[384,2048]{1,0:T(8,128)(2,1)S(1)} %collective-permute-done.10.refs_1_, bf16[8192,2048]{1,0:T(8,128)(2,1)} %refs_2_.5, ...), custom_call_target="tpu_custom_call", output_to_operand_aliasing={{}: (5, {})} | custom-call | flops 1 | bytes 1 | tf_op jit(solution)/shard_map/pallas_call | solution.py:27
  (39 shorter events, 0.1 us)
Async XLA Ops:
  4.3 9.0 %copy-start = (bf16[768,2048]{1,0:T(8,128)(2,1)S(1)}, bf16[768,2048]{1,0:T(8,128)(2,1)}, u32[]{:S(2)}) copy-start(bf16[768,2048]{1,0:T(8,128)(2,1)} %refs_1_.11) | copy-start | bytes 9437188
  9.6 96.6 %collective-permute-start.5 = (bf16[1024,2048]{1,0:T(8,128)(2,1)}, bf16[1024,2048]{1,0:T(8,128)(2,1)}, u32[]{:S(2)}, u32[]{:S(2)}) collective-permute-start(bf16[1024,2048]{1,0:T(8,128)(2,1)} %bitcast.9), channel_id=1, source_target_pairs={{0,8},{4,12},{8,0},{12,4},{1,9},{5,13},{9,1},{13,5},{2,10},{6,14},... | collective-permute-start | bytes 12582920 | tf_op jit(solution)/shard_map/ppermute | solution.py:238
  13.2 70.3 %collective-permute-start.1 = (bf16[768,2048]{1,0:T(8,128)(2,1)S(1)}, bf16[768,2048]{1,0:T(8,128)(2,1)}, u32[]{:S(2)}, u32[]{:S(2)}) collective-permute-start(bf16[768,2048]{1,0:T(8,128)(2,1)S(1)} %copy-done), channel_id=1, source_target_pairs={{0,1},{1,0},{2,3},{3,2},{4,5},{5,4},{6,7},{7,6},{8,9},{9,8},{10,11... | collective-permute-start | bytes 9437192 | tf_op jit(solution)/shard_map/ppermute | solution.py:276
  14.8 68.7 %collective-permute-start = (bf16[768,2048]{1,0:T(8,128)(2,1)S(1)}, bf16[768,2048]{1,0:T(8,128)(2,1)}, u32[]{:S(2)}, u32[]{:S(2)}) collective-permute-start(bf16[768,2048]{1,0:T(8,128)(2,1)S(1)} %copy-done), channel_id=1, source_target_pairs={{1,2},{2,1},{5,6},{6,5},{9,10},{10,9},{13,14},{14,13},{17,18},{18,... | collective-permute-start | bytes 9437192 | tf_op jit(solution)/shard_map/ppermute | solution.py:277
  30.2 1.3 copy-start.2
  31.5 4.5 %collective-permute-start.3 = (bf16[512,2048]{1,0:T(8,128)(2,1)}, bf16[512,2048]{1,0:T(8,128)(2,1)}, u32[]{:S(2)}, u32[]{:S(2)}) collective-permute-start(bf16[512,2048]{1,0:T(8,128)(2,1)} %bitcast.7), channel_id=1, source_target_pairs={{0,4},{4,0},{8,12},{12,8},{1,5},{5,1},{9,13},{13,9},{2,6},{6,2},{1... | collective-permute-start | bytes 6291464 | tf_op jit(solution)/shard_map/ppermute | solution.py:238
  31.5 14.0 %collective-permute-start.2 = (bf16[512,2048]{1,0:T(8,128)(2,1)}, bf16[512,2048]{1,0:T(8,128)(2,1)}, u32[]{:S(2)}, u32[]{:S(2)}) collective-permute-start(bf16[512,2048]{1,0:T(8,128)(2,1)} %bitcast.26), channel_id=1, source_target_pairs={{0,4},{4,0},{8,12},{12,8},{1,5},{5,1},{9,13},{13,9},{2,6},{6,2},{1... | collective-permute-start | bytes 6291464 | tf_op jit(solution)/shard_map/ppermute | solution.py:238
  36.0 1.6 copy-start.3
  44.8 0.6 copy-start.5
  83.5 3.9 %copy-start.1 = (bf16[768,2048]{1,0:T(8,128)(2,1)S(1)}, bf16[768,2048]{1,0:T(8,128)(2,1)}, u32[]{:S(2)}) copy-start(bf16[768,2048]{1,0:T(8,128)(2,1)} %refs_1_.11) | copy-start | bytes 9437188
  83.6 75.7 %collective-permute-start.9 = (bf16[768,2048]{1,0:T(8,128)(2,1)}, bf16[768,2048]{1,0:T(8,128)(2,1)}, u32[]{:S(2)}, u32[]{:S(2)}) collective-permute-start(bf16[768,2048]{1,0:T(8,128)(2,1)} %shard_map.78.refs_4_), channel_id=1, source_target_pairs={{1,0},{2,3},{5,4},{6,7},{9,8},{10,11},{13,12},{14,15},{17,16},{18,... | collective-permute-start | bytes 9437192 | tf_op jit(solution)/shard_map/ppermute | solution.py:279
  85.1 74.8 %collective-permute-start.4 = (bf16[768,2048]{1,0:T(8,128)(2,1)}, bf16[768,2048]{1,0:T(8,128)(2,1)}, u32[]{:S(2)}, u32[]{:S(2)}) collective-permute-start(bf16[768,2048]{1,0:T(8,128)(2,1)} %shard_map.77.__1_.refs_2_), channel_id=1, source_target_pairs={{1,2},{2,1},{5,6},{6,5},{9,10},{10,9},{13,14},{14,13},{17,18},{18,... | collective-permute-start | bytes 9437192 | tf_op jit(solution)/shard_map/ppermute | solution.py:278
  109.3 5.0 %collective-permute-start.6 = (bf16[256,2048]{1,0:T(8,128)(2,1)}, bf16[256,2048]{1,0:T(8,128)(2,1)}, u32[]{:S(2)}, u32[]{:S(2)}) collective-permute-start(bf16[256,2048]{1,0:T(8,128)(2,1)} %get-tuple-element.19), channel_id=1, source_target_pairs={{0,4},{4,0},{8,12},{12,8},{1,5},{5,1},{9,13},{13,9},{2,6},{6,2},{1... | collective-permute-start | bytes 3145736 | tf_op jit(solution)/shard_map/ppermute | solution.py:238
  109.3 5.0 %collective-permute-start.7 = (bf16[256,2048]{1,0:T(8,128)(2,1)}, bf16[256,2048]{1,0:T(8,128)(2,1)}, u32[]{:S(2)}, u32[]{:S(2)}) collective-permute-start(bf16[256,2048]{1,0:T(8,128)(2,1)} %get-tuple-element.20), channel_id=1, source_target_pairs={{0,4},{4,0},{8,12},{12,8},{1,5},{5,1},{9,13},{13,9},{2,6},{6,2},{1... | collective-permute-start | bytes 3145736 | tf_op jit(solution)/shard_map/ppermute | solution.py:238
  109.8 103.4 %collective-permute-start.13 = (bf16[512,2048]{1,0:T(8,128)(2,1)}, bf16[512,2048]{1,0:T(8,128)(2,1)}, u32[]{:S(2)}, u32[]{:S(2)}) collective-permute-start(bf16[512,2048]{1,0:T(8,128)(2,1)} %bitcast.14), channel_id=1, source_target_pairs={{0,12},{4,8},{8,4},{12,0},{1,13},{5,9},{9,5},{13,1},{2,14},{6,10},... | collective-permute-start | bytes 6291464 | tf_op jit(solution)/shard_map/ppermute | solution.py:238
  116.0 2.9 %copy-start.6 = (f32[16,768]{1,0:T(8,128)S(1)}, f32[16,768]{1,0:T(8,128)}, u32[]{:S(2)}) copy-start(f32[16,768]{1,0:T(8,128)} %copy-done.5) | copy-start | bytes 147460
  119.0 7.8 %copy-start.7 = (f32[16,768]{1,0:T(8,128)}, f32[16,768]{1,0:T(8,128)S(1)}, u32[]{:S(2)}) copy-start(f32[16,768]{1,0:T(8,128)S(1)} %shard_map.82.__1_) | copy-start | bytes 147460
  119.0 39.6 %collective-permute-start.8 = (f32[16,768]{1,0:T(8,128)S(1)}, f32[16,768]{1,0:T(8,128)S(1)}, u32[]{:S(2)}, u32[]{:S(2)}) collective-permute-start(f32[16,768]{1,0:T(8,128)S(1)} %add_add_fusion), channel_id=1, source_target_pairs={{0,1},{1,0},{2,3},{3,2},{4,5},{5,4},{6,7},{7,6},{8,9},{9,8},{10,11... | collective-permute-start | bytes 147464 | tf_op jit(solution)/shard_map/ppermute | solution.py:299
  159.2 54.0 %collective-permute-start.12 = (bf16[512,2048]{1,0:T(8,128)(2,1)}, bf16[512,2048]{1,0:T(8,128)(2,1)S(1)}, u32[]{:S(2)}, u32[]{:S(2)}) collective-permute-start(bf16[512,2048]{1,0:T(8,128)(2,1)} %shard_map.83.__1_), channel_id=1, source_target_pairs={{0,8},{4,12},{8,0},{12,4},{1,9},{5,13},{9,1},{13,5},{2,10},{6,14},... | collective-permute-start | bytes 6291464 | tf_op jit(solution)/shard_map/ppermute | solution.py:238
  159.9 6.9 %copy-start.8 = (f32[16,768]{1,0:T(8,128)S(1)}, f32[16,768]{1,0:T(8,128)}, u32[]{:S(2)}) copy-start(f32[16,768]{1,0:T(8,128)} %shard_map.85.__1_) | copy-start | bytes 147460
  164.0 40.8 %collective-permute-start.14 = (bf16[384,2048]{1,0:T(8,128)(2,1)}, bf16[384,2048]{1,0:T(8,128)(2,1)S(1)}, u32[]{:S(2)}, u32[]{:S(2)}) collective-permute-start(bf16[384,2048]{1,0:T(8,128)(2,1)} %get-tuple-element.21), channel_id=1, source_target_pairs={{1,0},{2,3},{5,4},{6,7},{9,8},{10,11},{13,12},{14,15},{17,16},{18,... | collective-permute-start | bytes 4718600 | tf_op jit(solution)/shard_map/ppermute | solution.py:297
  165.3 71.0 %collective-permute-start.10 = (bf16[384,2048]{1,0:T(8,128)(2,1)}, bf16[384,2048]{1,0:T(8,128)(2,1)S(1)}, u32[]{:S(2)}, u32[]{:S(2)}) collective-permute-start(bf16[384,2048]{1,0:T(8,128)(2,1)} %get-tuple-element.22), channel_id=1, source_target_pairs={{1,0},{2,3},{5,4},{6,7},{9,8},{10,11},{13,12},{14,15},{17,16},{18,... | collective-permute-start | bytes 4718600 | tf_op jit(solution)/shard_map/ppermute | solution.py:297
  166.9 20.4 %collective-permute-start.11 = (f32[16,768]{1,0:T(8,128)S(1)}, f32[16,768]{1,0:T(8,128)S(1)}, u32[]{:S(2)}, u32[]{:S(2)}) collective-permute-start(f32[16,768]{1,0:T(8,128)S(1)} %copy-done.8), channel_id=1, source_target_pairs={{0,2},{1,3},{2,0},{3,1},{4,6},{5,7},{6,4},{7,5},{8,10},{9,11},{10,... | collective-permute-start | bytes 147464 | tf_op jit(solution)/shard_map/ppermute | solution.py:302
  187.2 1.6 copy-start.4

commit v2 on v1

v2 whole, which is shorter than its diff:
```python
import functools

import jax
import jax.numpy as jnp
from jax import lax
from jax.experimental import pallas as pl
from jax.experimental.pallas import tpu as pltpu
from jax.sharding import PartitionSpec as P

F32 = jnp.float32
BF16 = jnp.bfloat16
ROOM = 48 * 1024 * 1024
TILE = 512


class Order:
    def __init__(self, first):
        self.last = first

    def call(self, kernel, at, args, specs, **rest):
        after = [] if rest.get("input_output_aliases") else [self.last]

        def body(at_ref, *refs):
            kernel(at_ref, *refs[: len(args)], *refs[len(args) + len(after) :])

        outs = pl.pallas_call(
            body,
            grid_spec=pltpu.PrefetchScalarGridSpec(
                num_scalar_prefetch=1,
                in_specs=list(specs) + [pl.BlockSpec(memory_space=pl.ANY)] * len(after),
                **rest.pop("grid_spec"),
            ),
            compiler_params=pltpu.CompilerParams(vmem_limit_bytes=ROOM),
            cost_estimate=pl.CostEstimate(flops=1, bytes_accessed=1, transcendentals=0),
            **rest,
        )(at, *args, *after)
        self.last = outs[0] if isinstance(outs, (list, tuple)) else outs
        return outs


    def hold(self, x):
        self.last = pl.pallas_call(
            lambda *_: None,
            out_shape=jax.ShapeDtypeStruct(x.shape, x.dtype),
            in_specs=[pl.BlockSpec(memory_space=pl.ANY)] * 2,
            out_specs=pl.BlockSpec(memory_space=pl.ANY),
            input_output_aliases={0: 0},
            cost_estimate=pl.CostEstimate(flops=1, bytes_accessed=1, transcendentals=0),
        )(x, self.last)
        return self.last


    def cut(self, x, sizes):
        def kernel(x_ref, _, *outs):
            start = 0
            for size, out in zip(sizes, outs):
                out[...] = x_ref[pl.ds(start, size)]
                start += size

        outs = pl.pallas_call(
            kernel,
            out_shape=[jax.ShapeDtypeStruct((size, x.shape[1]), x.dtype) for size in sizes],
            in_specs=[pl.BlockSpec(memory_space=pltpu.VMEM), pl.BlockSpec(memory_space=pl.ANY)],
            out_specs=[pl.BlockSpec(memory_space=pltpu.VMEM)] * len(sizes),
            compiler_params=pltpu.CompilerParams(vmem_limit_bytes=ROOM),
            cost_estimate=pl.CostEstimate(flops=1, bytes_accessed=1, transcendentals=0),
        )(x, self.last)
        self.last = outs[0]
        return outs


def fetch_kernel(lists_ref, *refs, stores, plan):
    outs, (held, in_sem, out_sem) = refs[stores:-3], refs[-3:]
    count = held.shape[1]
    steps = [(o, at, s, n) for o, pairs in enumerate(plan) for at, (s, n) in enumerate(pairs)]
    for i, (_, _, s, n) in enumerate(steps):
        @pl.loop(0, count)
        def _(j, i=i, s=s, n=n):
            pltpu.make_async_copy(
                refs[s].at[lists_ref[n, j]], held.at[i, j], in_sem.at[i]
            ).start()
    copies = []
    for i, (o, at, _, _) in enumerate(steps):
        pltpu.make_async_copy(held.at[i], held.at[i], in_sem.at[i]).wait()
        copies.append(
            pltpu.make_async_copy(
                held.at[i], outs[o].at[pl.ds(at * count, count)], out_sem.at[i]
            )
        )
        copies[-1].start()
    for copy in copies:
        copy.wait()


def fetch(order, lists, stores, plan):
    count = lists.shape[1]
    shape = stores[0].shape[1:]
    total = sum(map(len, plan))
    outs = order.call(
        functools.partial(fetch_kernel, stores=len(stores), plan=plan),
        lists,
        stores,
        [pl.BlockSpec(memory_space=pl.ANY)] * len(stores),
        out_shape=[jax.ShapeDtypeStruct((len(p) * count,) + shape, BF16) for p in plan],
        grid_spec=dict(
            grid=(1,),
            out_specs=[pl.BlockSpec(memory_space=pl.ANY)] * len(plan),
            scratch_shapes=[
                pltpu.VMEM((total, count) + shape, BF16),
                pltpu.SemaphoreType.DMA((total,)),
                pltpu.SemaphoreType.DMA((total,)),
            ],
        ),
    )
    return [o.reshape(o.shape[0] * shape[0], shape[1]) for o in outs]


def sum_kernel(at_ref, *refs, plan, has_total, has_out, rounded):
    refs = list(refs)
    factors = [([refs.pop(0) for _ in range(n)], refs.pop(0)) for n in plan]
    total = refs.pop(0) if has_total else None
    if has_out:
        refs.pop(0)
    out = refs.pop(0)
    value = total[...] if has_total else None
    for xs, w in factors:
        if len(xs) > 1:
            both = refs.pop(0)

            @pl.when(pl.program_id(0) == 0)
            def _(xs=xs, both=both):
                start = 0
                for x in xs[:-1]:
                    part = pl.ds(start, x.shape[0])
                    both[part] = x[...] + xs[-1][part]
                    start += x.shape[0]

            x = both
        else:
            x = xs[0]
        product = jnp.dot(x[...], w[...], preferred_element_type=F32)
        value = product if value is None else value + product
    out[...] = value.astype(BF16) if rounded else value


def add_products(order, terms, total=None, first=0, rows=None, whole=None, out=None, rounded=False):
    rows = rows or terms[0][0][-1].shape[0]
    width = terms[0][1].shape[1]
    tile = min(TILE, width)
    at = jnp.stack([jnp.asarray(t[2], jnp.int32) for t in terms])
    here = first // rows
    there = here if whole else 0
    specs, args, scratch = [], [], []
    for n, (xs, w, _) in enumerate(terms):
        depth = xs[0].shape[1]
        for x in xs:
            at_row = here if x is xs[-1] and x.shape[0] > rows else 0
            specs.append(
                pl.BlockSpec((min(rows, x.shape[0]), depth), lambda j, at, i=at_row: (i, 0))
            )
            args.append(x)
        specs.append(pl.BlockSpec((depth, tile), lambda j, at, n=n: (at[n], j)))
        args.append(w)
        if len(xs) > 1:
            scratch.append(pltpu.VMEM((rows, depth), BF16))
    if total is not None:
        specs.append(pl.BlockSpec((rows, tile), lambda j, at: (here, j)))
        args.append(total)
    aliases = {}
    if out is not None:
        aliases = {len(args) + 1: 0}
        specs.append(pl.BlockSpec(memory_space=pl.ANY))
        args.append(out)
    dtype = BF16 if rounded else F32
    return order.call(
        functools.partial(
            sum_kernel,
            plan=[len(t[0]) for t in terms],
            has_total=total is not None,
            has_out=out is not None,
            rounded=rounded,
        ),
        at,
        args,
        specs,
        out_shape=jax.ShapeDtypeStruct((whole or rows, width), dtype),
        grid_spec=dict(
            grid=(width // tile,),
            out_specs=pl.BlockSpec((rows, tile), lambda j, at: (there, j)),
            scratch_shapes=scratch,
        ),
        input_output_aliases=aliases,
    )


def expand_kernel(at_ref, low, codes, *refs, most, rank):
    blocks, (total, out, picks) = refs[:-3], refs[-3:]
    width = most * rank

    @pl.when(pl.program_id(0) == 0)
    def _():
        column = lax.broadcasted_iota(jnp.int32, (rank, width), 1)
        fold = column % rank == lax.broadcasted_iota(jnp.int32, (rank, width), 0)
        spread = lax.dot_general(
            low[...], fold.astype(BF16), (((0,), (0,)), ((), ())), preferred_element_type=F32
        )
        place = lax.broadcasted_iota(jnp.int32, (1, width), 1) // rank
        for n in range(len(blocks)):
            mine = codes[...] == at_ref[len(blocks) + n] * most + place
            picks[n] = jnp.where(mine, spread, 0.0).astype(BF16)

    value = total[...]
    for n, block in enumerate(blocks):
        value = value + jnp.dot(picks[n], block[...], preferred_element_type=F32)
    out[...] = value


def add_expanded(order, low, codes, factors, homes, total, most):
    rank, rows = low.shape
    width = total.shape[1]
    tile = min(TILE, width)
    at = jnp.stack([jnp.asarray(x, jnp.int32) for x in [i for _, i in factors] + homes])
    full = lambda j, at: (0, 0)
    return order.call(
        functools.partial(expand_kernel, most=most, rank=rank),
        at,
        [low, codes, *[w for w, _ in factors], total],
        [pl.BlockSpec((rank, rows), full), pl.BlockSpec((rows, 1), full)]
        + [
            pl.BlockSpec((most * rank, tile), lambda j, at, n=n: (at[n], j))
            for n in range(len(factors))
        ]
        + [pl.BlockSpec((rows, tile), lambda j, at: (0, j))],
        out_shape=jax.ShapeDtypeStruct((rows, width), F32),
        grid_spec=dict(
            grid=(width // tile,),
            out_specs=pl.BlockSpec((rows, tile), lambda j, at: (0, j)),
            scratch_shapes=[pltpu.VMEM((len(factors), rows, most * rank), BF16)],
        ),
    )


def shrink_kernel(at_ref, code, x, store, mates, out, held, sem, *, k, most, rank):
    for i in range(2):
        @pl.loop(0, most // 2)
        def _(j, i=i):
            j = j + i * (most // 2)
            pltpu.make_async_copy(
                store.at[at_ref[k, j]], held.at[pl.ds(j * rank, rank)], sem
            ).start()
    width = most * rank
    place = lax.broadcasted_iota(jnp.int32, (width, 1), 0) // rank
    fold = lax.broadcasted_iota(jnp.int32, (rank, width), 1) % rank == lax.broadcasted_iota(
        jnp.int32, (rank, width), 0
    )

    last = at_ref.shape[0] - 1

    def picked(block, which):
        product = lax.dot_general(
            block, x[...], (((1,), (1,)), ((), ())), preferred_element_type=F32
        )
        return jnp.where(at_ref[last, which] * most + place == code[...], product, 0.0)

    value = picked(mates[...], 1)
    pltpu.make_async_copy(held, held, sem).wait()
    out[...] = jnp.dot(
        fold.astype(F32),
        value + picked(held[...], 0),
        precision=lax.Precision.HIGHEST,
        preferred_element_type=F32,
    )


def shrink_part(order, lists, k, code, x, store, mates):
    rows, depth = code.shape[1], x.shape[1]
    most, rank = lists.shape[1], store.shape[1]
    full = lambda i, at: (0, 0)
    return order.call(
        functools.partial(shrink_kernel, k=k, most=most, rank=rank),
        lists,
        [code, x, store, mates],
        [
            pl.BlockSpec((1, rows), full),
            pl.BlockSpec((rows, depth), full),
            pl.BlockSpec(memory_space=pl.ANY),
            pl.BlockSpec((most * rank, depth), full),
        ],
        out_shape=jax.ShapeDtypeStruct((rank, rows), F32),
        grid_spec=dict(
            grid=(1,),
            out_specs=pl.BlockSpec((rank, rows), full),
            scratch_shapes=[
                pltpu.VMEM((most * rank, depth), BF16),
                pltpu.SemaphoreType.DMA(()),
            ],
        ),
    )


def body(
    tokens,
    query_base_weight,
    stored_shrink_factors,
    stored_expand_factors,
    segment_adapter,
    segment_length,
    adapter_storage_slot,
):
    groups = lax.axis_size("dp")
    lanes = lax.axis_size("tensor")
    me = lax.axis_index("dp")
    stored, rank, depth = stored_shrink_factors.shape
    used = segment_adapter.shape[1]
    most = used // 2
    rows = tokens.shape[0]
    count_all = adapter_storage_slot.shape[0]

    flat_ids = segment_adapter.reshape(-1)
    match = flat_ids[:, None] == jnp.arange(count_all, dtype=jnp.int32)[None, :]
    slot = jnp.sum(jnp.where(match, adapter_storage_slot[None, :], 0), axis=1)
    slot = slot.reshape(groups, used)
    home, local = slot // stored, slot % stored

    earlier = jnp.arange(used)[None, :] < jnp.arange(used)[:, None]
    same = home[:, :, None] == home[:, None, :]
    place = jnp.sum(jnp.where(same & earlier[None], 1, 0), axis=2)

    mine = (home == me)[:, :, None] & (place[:, :, None] == jnp.arange(most)[None, None, :])
    lists = jnp.sum(jnp.where(mine, local[:, :, None], 0), axis=1)
    to = me ^ jnp.arange(groups, dtype=jnp.int32)
    lists = jnp.sum(jnp.where((to[:, None] == jnp.arange(groups)[None])[:, :, None], lists[None], 0), axis=1)

    def send(block, k):
        return lax.ppermute(block, "dp", [(i, i ^ k) for i in range(groups)])

    here = (jnp.arange(groups) == me)[:, None]
    code_of = jnp.sum(jnp.where(here, home * most + place, 0), axis=0)
    ends = jnp.cumsum(segment_length[0])
    row_ids = jnp.arange(rows, dtype=jnp.int32)
    member = ((ends - segment_length[0])[None, :] <= row_ids[:, None]) & (
        row_ids[:, None] < ends[None, :]
    )
    code = jnp.sum(jnp.where(member, code_of[None, :], 0), axis=1)
    note = jnp.pad(code, (0, 16 * depth - rows)).reshape(16, depth).astype(BF16)
    noted = jnp.concatenate([tokens, note], axis=0)

    homes = jnp.where(jnp.arange(most) == 0, me, me ^ 1)[None]
    lists = jnp.concatenate([lists, homes])
    order = Order(lists)
    weight = query_base_weight
    line = lax.axis_index("tensor")
    shrinks, expands = stored_shrink_factors, stored_expand_factors
    across = send(noted, 2)
    plan = [[p] for p in [(0, 1), (0, 3), (1, 1), (1, 0), (1, 2), (1, 3)]]
    blocks = fetch(order, lists, [shrinks, expands], plan)
    mates = [send(x, 1) for x in blocks[:3]]
    far_b = [None, send(blocks[5], 3)]

    def shrink_of(k, code, x, mates):
        return shrink_part(order, lists, k, code[None], x, shrinks, mates)

    if lanes == 4:
        swap = [(0, 1), (1, 0), (2, 3), (3, 2)]
        middle = [(1, 2), (2, 1)]
        inward = [(0, 1), (3, 2)]
        outward = [(1, 0), (2, 3)]
        step = rows // 4
        near = lax.ppermute(tokens, "tensor", swap)
        cross = lax.ppermute(tokens, "tensor", middle)
        own = add_products(order, [([tokens], weight, line)])
        cross = order.hold(cross)
        out_near = lax.ppermute(cross, "tensor", outward)
        cuts = order.cut(near, [2 * step] * 2)
        far = [lax.ppermute(x, "tensor", middle) for x in cuts]
        across = order.hold(across)
        own = add_products(order, [([near], weight, line ^ 1)], own)
    part = shrink_of(0, code, tokens, mates[0])
    code_across = across[rows:].reshape(-1)[:rows].astype(F32).astype(jnp.int32)
    part = part + send(shrink_of(2, code_across, across, mates[1]), 2)
    if lanes == 4:
        far[0] = order.hold(far[0])
        out_far = [lax.ppermute(far[0], "tensor", outward)]
        far_b[1] = order.hold(far_b[1])
        part = order.hold(part)
        far_b[0] = send(order.hold(blocks[4]), 2)
        out_near = order.hold(out_near)
        part = order.hold(part + lax.ppermute(part, "tensor", inward))
        part = part + lax.ppermute(part, "tensor", middle)
        own = add_products(order, [([*far, out_near], weight, line ^ 2)], own)
        low = order.hold(part.astype(BF16))
        told = lax.ppermute(low, "tensor", outward)
        pieces = order.cut(far[1], [step] * 2)
        out_far.append(lax.ppermute(pieces[0], "tensor", outward))
        told = order.hold(told)
        out_far.append(lax.ppermute(order.hold(pieces[1]), "tensor", outward))
        low = jnp.where((line == 1) | (line == 2), low, told)
    else:
        far_b[0] = send(blocks[4], 2)
        low = lax.psum(part, "tensor").astype(BF16)
    factors = [(x, 0) for x in (blocks[3], mates[2], *far_b)]
    if lanes != 4:
        whole = lax.all_gather(tokens, "tensor", axis=1, tiled=True)
        own = jnp.dot(whole, weight, preferred_element_type=F32)
    total = add_expanded(order, low, code[:, None], factors, [me ^ k for k in range(groups)], own, most)
    if lanes != 4:
        return total.astype(BF16)
    out = None
    first = 0
    for x in out_far:
        last = [([x, cross], weight, line ^ 3)]
        out = add_products(order, last, total, first, x.shape[0], rows, out, True)
        first += x.shape[0]
    return out


def solution(mesh):
    in_specs = (
        P(("groups", "dp"), "tensor"),
        P(None, "tensor"),
        P("dp", None, "tensor"),
        P("dp", None, "tensor"),
        P("groups", None),
        P(("groups", "dp"), None),
        P("groups"),
    )
    out_specs = P(("groups", "dp"), "tensor")
    return jax.shard_map(body, mesh=mesh, in_specs=in_specs, out_specs=out_specs, check_vma=False)
```

time: 245 us -> 222 us (0.906)
  waiting for transfers between devices: 91.4 us -> 70.8 us
  starting transfers between devices: 27.8 us -> 23.5 us
  other arithmetic: 5.1 us -> 9.23 us
    ppermute x7 -> x10, waiting for transfers between devices: 87.5 us -> 44.5 us  [the longest x1 29 us: body(): near = lax.ppermute(tokens, 'tensor', swap)]
    ppermute x7, waiting for transfers between devices: 3.94 us -> 19.8 us  [send(): return lax.ppermute(block, 'dp', [(i, i ^ k) for i in range(groups)])]
    slice x4 -> x0, local copies, waits for them, and re-layouts: 9.58 us -> none  [the longest x1 4.07 us: onward(): return lax.ppermute(far[i * step:(i + 1) * step], 'tensor', outward)]
    unnamed x18 -> x30, local copies, waits for them, and re-layouts: 4.39 us -> 11.3 us
    ppermute x1, waiting for transfers between devices: 0.01 us -> 6.56 us  [body(): out_near = lax.ppermute(cross, 'tensor', outward)]
    pallas_call x0 -> x2, Pallas kernels: none -> 4.67 us  [cut(): pl.pallas_call(kernel, out_shape=[jax.ShapeDtypeStruct((size, x.shape[1])...]
    ppermute x7 -> x10, starting transfers between devices: 20.9 us -> 16.4 us  [the longest x1 5.71 us: body(): near = lax.ppermute(tokens, 'tensor', swap)]
    pallas_call x12 -> x10, Pallas kernels: 103 us -> 99.3 us  [call(): pl.pallas_call(body, grid_spec=pltpu.PrefetchScalarGridSpec(num_scalar_pr...]
  transfers between devices with their start and end apart: 15 -> 18, of which waited for: 5 -> 6; matrix products, arithmetic and copies ran while one was open for 5% -> 5% of each run, Pallas kernels for 37% -> 44%
where the time goes in v2:
time: 222 us; the launch traced here: 221 us
  Pallas kernels  104 us (47%)
  waiting for transfers between devices  70.8 us (32%)
  starting transfers between devices  23.5 us (11%)
  local copies, waits for them, and re-layouts  13.2 us (6%)
  other arithmetic  9.23 us (4%)
    pallas_call x10, Pallas kernels, call(): pl.pallas_call(body, grid_spec=pltpu.PrefetchScalarGridSpec(num_scalar_pr...  99.3 us
    ppermute x1, waiting for transfers between devices, body(): near = lax.ppermute(tokens, 'tensor', swap)  29 us
    ppermute x7, waiting for transfers between devices, send(): return lax.ppermute(block, 'dp', [(i, i ^ k) for i in range(groups)])  19.8 us
    ppermute x1, waiting for transfers between devices, body(): told = lax.ppermute(low, 'tensor', outward)  13.8 us
    unnamed x30, local copies, waits for them, and re-layouts  11.3 us
    ppermute x1, waiting for transfers between devices, body(): out_near = lax.ppermute(cross, 'tensor', outward)  6.56 us
    ppermute x7, starting transfers between devices, send(): return lax.ppermute(block, 'dp', [(i, i ^ k) for i in range(groups)])  5.73 us
    ppermute x1, starting transfers between devices, body(): near = lax.ppermute(tokens, 'tensor', swap)  5.71 us
  transfers between devices with their start and end apart: 18, of which 6 were waited for; matrix products, arithmetic and copies ran while one was open for 5% of the time, Pallas kernels for 44%

profile of v2, /device:TPU:0, one launch (start us, length us, event | category | flops | bytes accessed | tf_op | source)
XLA Modules:
  0.0 221.1 jit_solution(2055145298432478281)
XLA Ops:
  0.0 0.9 collective-permute-start.1
  0.9 5.7 %collective-permute-start = (bf16[768,2048]{1,0:T(8,128)(2,1)}, bf16[768,2048]{1,0:T(8,128)(2,1)}, u32[]{:S(2)}, u32[]{:S(2)}) collective-permute-start(bf16[768,2048]{1,0:T(8,128)(2,1)} %refs_1_.7), channel_id=1, source_target_pairs={{0,1},{1,0},{2,3},{3,2},{4,5},{5,4},{6,7},{7,6},{8,9},{9,8},{10,11... | collective-permute-start | bytes 9437192 | tf_op jit(solution)/shard_map/ppermute | solution.py:369
  6.6 0.8 eq.100
  7.4 1.0 select_reduce_fusion
  8.3 0.1 reshape.178
  8.4 0.8 copy.24
  9.2 0.1 reduce-window.4
  9.2 0.1 reduce
  9.4 0.7 fusion.3
  10.0 0.2 select_reduce_fusion.2
  10.3 0.1 select_reduce_fusion.5
  10.4 0.1 select_reduce_fusion.1
  10.6 4.0 %pad_maximum_fusion = bf16[784,2048]{1,0:T(8,128)(2,1)} fusion(bf16[16,2048]{1,0:T(8,128)(2,1)S(1)} %convert_element_type.13, bf16[768,2048]{1,0:T(8,128)(2,1)} %refs_1_.7), kind=kLoop, calls=%fused_computation | loop fusion | flops 6422528 | bytes 6422528 | tf_op jit(solution)/shard_map/concatenate | solution.py:346
  14.5 1.5 collective-permute-start.4
  16.0 0.1 select_reduce_fusion.3
  16.2 0.1 iota_compare_fusion.5
  16.3 0.1 select_reduce_fusion.4
  16.4 13.5 %shard_map.73 = (bf16[32,16,2048]{2,1,0:T(8,128)(2,1)}, bf16[32,16,2048]{2,1,0:T(8,128)(2,1)}, bf16[32,16,2048]{2,1,0:T(8,128)(2,1)}, bf16[32,16,2048]{2,1,0:T(8...) custom-call(s32[5,32]{1,0:T(8,128)S(1)} %pad_add_fusion.at_ref.refs_2_, ...), custom_call_target="tpu_custom_call" | custom-call | flops 1 | bytes 1 | tf_op jit(solution)/shard_map/pallas_call | solution.py:26
  29.9 0.1 collective-permute-start.3
  30.0 0.5 collective-permute-start.5
  30.4 1.9 copy-done.2
  32.3 10.5 %shard_map.74.__1_.refs_2_ = f32[768,2048]{1,0:T(8,128)} custom-call(s32[1]{0:T(128)} %bitcast.1.at_ref, bf16[768,2048]{1,0:T(8,128)(2,1)S(1)} %copy-done.2, bf16[8192,2048]{1,0:T(8,128)(2,1)} %refs_2_.9, bf16[32,16,2048]{2,1,0:T(8,128)(2,1)} %get-tuple-element.15.refs_2_), custom_call_target="tpu_custom_call" | custom-call | flops 1 | bytes 1 | tf_op jit(solution)/shard_map/pallas_call | solution.py:26
  42.8 1.7 copy-done
  44.5 1.3 collective-permute-start.10
  45.7 29.0 %collective-permute-done.x_ref.refs_0_ = bf16[768,2048]{1,0:T(8,128)(2,1)} collective-permute-done((bf16[768,2048]{1,0:T(8,128)(2,1)}, bf16[768,2048]{1,0:T(8,128)(2,1)}, u32[]{:S(2)}, u32[]{:S(2)}) %collective-permute-start) | collective-permute-done | bytes 3145760 | tf_op jit(solution)/shard_map/ppermute | solution.py:369
  74.8 3.7 %shard_map.76 = (bf16[384,2048]{1,0:T(8,128)(2,1)}, bf16[384,2048]{1,0:T(8,128)(2,1)}) custom-call(bf16[768,2048]{1,0:T(8,128)(2,1)} %collective-permute-done.x_ref.refs_0_, bf16[768,2048]{1,0:T(8,128)(2,1)} %shard_map.75._.refs_1_), custom_call_target="tpu_custom_call" | custom-call | flops 1 | bytes 1 | tf_op jit(solution)/shard_map/pallas_call | solution.py:60
  78.5 0.8 collective-permute-start.8
  79.2 8.1 %collective-permute-done.4.__0_ = bf16[784,2048]{1,0:T(8,128)(2,1)} collective-permute-done((bf16[784,2048]{1,0:T(8,128)(2,1)}, bf16[784,2048]{1,0:T(8,128)(2,1)}, u32[]{:S(2)}, u32[]{:S(2)}) %collective-permute-start.4) | collective-permute-done | bytes 3211296 | tf_op jit(solution)/shard_map/ppermute | solution.py:335
  87.3 0.9 collective-permute-start.2
  88.3 12.6 %shard_map.78.refs_4_ = f32[768,2048]{1,0:T(8,128)} custom-call(s32[1]{0:T(128)} %bitcast.5.at_ref, bf16[768,2048]{1,0:T(8,128)(2,1)} %collective-permute-done.x_ref.refs_0_, bf16[8192,2048]{1,0:T(8,128)(2,1)} %refs_2_.9, f32[768,2048]{1,0:T(8,128)} %shard_map.74.__1_.refs_2_, bf16[784,2048]{1,0:T(8,128)(2,1)} %shard_map.77.refs_3_.refs_1_), custom_call_target="tpu_custom_call" | custom-call | flops 1 | bytes 1 | tf_op jit(solution)/shard_map/pallas_call | solution.py:26
  100.9 7.4 %shard_map.79.refs_4_ = f32[16,768]{1,0:T(8,128)S(1)} custom-call(s32[5,32]{1,0:T(8,128)S(1)} %pad_add_fusion.at_ref.refs_2_, s32[1,768]{1,0:T(1,128)S(1)} %broadcast_in_dim.127.refs_0_, bf16[768,2048]{1,0:T(8,128)(2,1)S(1)} %copy-done.3, bf16[256,16,2048]{2,1,0:T(8,128)(2,1)} %refs_2_.6, bf16[512,2048]{1,0:T(8,128)(2,1)} %collective-permute-done.3.refs_3_, ...), custom_call_target="tpu_custom_call" | custom-call | flops 1 | bytes 1 | tf_op jit(solution)/shard_map/pallas_call | solution.py:26
  108.3 0.8 slice_bitcast_fusion
  109.2 8.4 %shard_map.80.__1_ = f32[16,768]{1,0:T(8,128)S(1)} custom-call(s32[5,32]{1,0:T(8,128)S(1)} %pad_add_fusion.at_ref.refs_2_, s32[1,768]{1,0:T(1,128)S(1)} %broadcast_in_dim.128.refs_0_, bf16[784,2048]{1,0:T(8,128)(2,1)} %shard_map.77.refs_3_.refs_1_, bf16[256,16,2048]{2,1,0:T(8,128)(2,1)} %refs_2_.6, bf16[512,2048]{1,0:T(8,128)(2,1)} %collective-permute-done.5.refs_3_, ...), custom_call_target="tpu_custom_call" | custom-call | flops 1 | bytes 1 | tf_op jit(solution)/shard_map/pallas_call | solution.py:26
  117.7 2.1 collective-permute-start.6
  119.7 11.7 %collective-permute-done.6 = f32[16,768]{1,0:T(8,128)S(1)} collective-permute-done((f32[16,768]{1,0:T(8,128)S(1)}, f32[16,768]{1,0:T(8,128)S(1)}, u32[]{:S(2)}, u32[]{:S(2)}) %collective-permute-start.6) | collective-permute-done | bytes 49184 | tf_op jit(solution)/shard_map/ppermute | solution.py:335
  131.4 0.6 add.38.__0_
  132.1 1.1 copy-done.4
  133.3 1.6 collective-permute-start.15
  134.8 2.2 collective-permute-start.9
  137.0 1.7 collective-permute-done.9
  138.8 1.3 collective-permute-start.17
  140.0 0.6 add.39.__0_
  140.7 6.6 %collective-permute-done.10.__0_ = bf16[768,2048]{1,0:T(8,128)(2,1)} collective-permute-done((bf16[768,2048]{1,0:T(8,128)(2,1)}, bf16[768,2048]{1,0:T(8,128)(2,1)}, u32[]{:S(2)}, u32[]{:S(2)}) %collective-permute-start.10) | collective-permute-done | bytes 3145760 | tf_op jit(solution)/shard_map/ppermute | solution.py:373
  147.2 0.7 collective-permute-start.11
  147.9 0.8 copy-done.9
  148.7 13.1 %shard_map.87.__1_.refs_6_ = f32[768,2048]{1,0:T(8,128)} custom-call(s32[1]{0:T(128)} %bitcast.9.at_ref, bf16[384,2048]{1,0:T(8,128)(2,1)S(1)} %copy-done.5, bf16[384,2048]{1,0:T(8,128)(2,1)S(1)} %collective-permute-done.2.refs_1_.x_ref, bf16[768,2048]{1,0:T(8,128)(2,1)} %shard_map.85.__1_.refs_2_, bf16[8192,2048]{1,0:T(8,128)(2,1)} %refs_2_.9, ...), custom_call_target="tpu_custom_call" | custom-call | flops 1 | bytes 1 | tf_op jit(solution)/shard_map/pallas_call | solution.py:26
  161.8 0.6 add_convert_fusion.__0_
  162.4 1.3 collective-permute-start.12
  163.7 0.7 copy-done.10
  164.4 1.0 shard_map.89
  165.4 0.9 copy-done.6
  166.3 1.3 collective-permute-start.16
  167.6 13.8 %collective-permute-done.12.__0_ = bf16[16,768]{1,0:T(8,128)(2,1)S(1)} collective-permute-done((bf16[16,768]{1,0:T(8,128)(2,1)}, bf16[16,768]{1,0:T(8,128)(2,1)S(1)}, u32[]{:S(2)}, u32[]{:S(2)}) %collective-permute-start.12) | collective-permute-done | bytes 24608 | tf_op jit(solution)/shard_map/ppermute | solution.py:392
  181.4 0.6 copy-done.13
  182.0 1.5 collective-permute-start.13
  183.5 0.2 broadcast_in_dim.130.refs_1_
  183.7 0.1 stack.37.at_ref
  183.8 0.7 broadcast_select_fusion.refs_0_
  184.5 1.1 copy-done.7
  185.6 1.6 copy-done.8
  187.2 12.8 %shard_map.92.refs_3_.refs_4_ = f32[768,2048]{1,0:T(8,128)} custom-call(s32[8]{0:T(128)S(1)} %stack.37.at_ref, bf16[16,768]{1,0:T(8,128)(2,1)S(1)} %broadcast_select_fusion.refs_0_, s32[768,1]{1,0:T(8,128)S(1)} %broadcast_in_dim.130.refs_1_, bf16[512,2048]{1,0:T(8,128)(2,1)S(1)} %bitcast.24, bf16[512,2048]{1,0:T(8,128)(2,1)} %collective-permute-done.14.refs_3_, ...), custom_call_target="tpu_custom_call" | custom-call | flops 1 | bytes 1 | tf_op jit(solution)/shard_map/pallas_call | solution.py:26
  200.1 8.5 %shard_map.93.refs_4_ = bf16[768,2048]{1,0:T(8,128)(2,1)} custom-call(s32[1]{0:T(128)} %bitcast.at_ref, bf16[384,2048]{1,0:T(8,128)(2,1)} %collective-permute-done.17.refs_0_, bf16[768,2048]{1,0:T(8,128)(2,1)S(1)} %copy-done.1, bf16[8192,2048]{1,0:T(8,128)(2,1)} %refs_2_.9, f32[768,2048]{1,0:T(8,128)} %shard_map.92.refs_3_.refs_4_, ...), custom_call_target="tpu_custom_call" | custom-call | flops 1 | bytes 1 | tf_op jit(solution)/shard_map/pallas_call | solution.py:26
  208.5 6.3 %shard_map.94.refs_4_ = bf16[768,2048]{1,0:T(8,128)(2,1)} custom-call(s32[1]{0:T(128)} %bitcast.at_ref, bf16[192,2048]{1,0:T(8,128)(2,1)S(1)} %collective-permute-done.16.refs_0_, bf16[768,2048]{1,0:T(8,128)(2,1)S(1)} %copy-done.1, bf16[8192,2048]{1,0:T(8,128)(2,1)} %refs_2_.9, ...), custom_call_target="tpu_custom_call", output_to_operand_aliasing={{}: (5, {})} | custom-call | flops 1 | bytes 1 | tf_op jit(solution)/shard_map/pallas_call | solution.py:26
  214.8 6.3 %shard_map.95 = bf16[768,2048]{1,0:T(8,128)(2,1)} custom-call(s32[1]{0:T(128)} %bitcast.at_ref, bf16[192,2048]{1,0:T(8,128)(2,1)S(1)} %collective-permute-done.13.refs_0_, bf16[768,2048]{1,0:T(8,128)(2,1)S(1)} %copy-done.1, bf16[8192,2048]{1,0:T(8,128)(2,1)} %refs_2_.9, f32[768,2048]{1,0:T(8,128)} %shard_map.92.refs_3_.refs_4_, ...), custom_call_target="tpu_custom_call", output_to_operand_aliasing={{}: (5, {})} | custom-call | flops 1 | bytes 1 | tf_op jit(solution)/shard_map/pallas_call | solution.py:26
  (59 shorter events, 0.3 us)
Async XLA Ops:
  0.0 42.8 %collective-permute-start.1 = (bf16[768,2048]{1,0:T(8,128)(2,1)}, bf16[768,2048]{1,0:T(8,128)(2,1)S(1)}, u32[]{:S(2)}, u32[]{:S(2)}) collective-permute-start(bf16[768,2048]{1,0:T(8,128)(2,1)} %refs_1_.7), channel_id=1, source_target_pairs={{1,2},{2,1},{5,6},{6,5},{9,10},{10,9},{13,14},{14,13},{17,18},{18,... | collective-permute-start | bytes 9437192 | tf_op jit(solution)/shard_map/ppermute | solution.py:370
  0.9 73.9 %collective-permute-start = (bf16[768,2048]{1,0:T(8,128)(2,1)}, bf16[768,2048]{1,0:T(8,128)(2,1)}, u32[]{:S(2)}, u32[]{:S(2)}) collective-permute-start(bf16[768,2048]{1,0:T(8,128)(2,1)} %refs_1_.7), channel_id=1, source_target_pairs={{0,1},{1,0},{2,3},{3,2},{4,5},{5,4},{6,7},{7,6},{8,9},{9,8},{10,11... | collective-permute-start | bytes 9437192 | tf_op jit(solution)/shard_map/ppermute | solution.py:369
  14.5 72.8 %collective-permute-start.4 = (bf16[784,2048]{1,0:T(8,128)(2,1)}, bf16[784,2048]{1,0:T(8,128)(2,1)}, u32[]{:S(2)}, u32[]{:S(2)}) collective-permute-start(bf16[784,2048]{1,0:T(8,128)(2,1)} %pad_maximum_fusion), channel_id=1, source_target_pairs={{0,8},{4,12},{8,0},{12,4},{1,9},{5,13},{9,1},{13,5},{2,10},{6,14},... | collective-permute-start | bytes 9633800 | tf_op jit(solution)/shard_map/ppermute | solution.py:335
  29.9 48.6 %collective-permute-start.3 = (bf16[512,2048]{1,0:T(8,128)(2,1)}, bf16[512,2048]{1,0:T(8,128)(2,1)}, u32[]{:S(2)}, u32[]{:S(2)}) collective-permute-start(bf16[512,2048]{1,0:T(8,128)(2,1)} %bitcast.4), channel_id=1, source_target_pairs={{0,4},{4,0},{8,12},{12,8},{1,5},{5,1},{9,13},{13,9},{2,6},{6,2},{1... | collective-permute-start | bytes 6291464 | tf_op jit(solution)/shard_map/ppermute | solution.py:335
  30.0 79.3 %collective-permute-start.5 = (bf16[512,2048]{1,0:T(8,128)(2,1)}, bf16[512,2048]{1,0:T(8,128)(2,1)}, u32[]{:S(2)}, u32[]{:S(2)}) collective-permute-start(bf16[512,2048]{1,0:T(8,128)(2,1)} %bitcast.6), channel_id=1, source_target_pairs={{0,4},{4,0},{8,12},{12,8},{1,5},{5,1},{9,13},{13,9},{2,6},{6,2},{1... | collective-permute-start | bytes 6291464 | tf_op jit(solution)/shard_map/ppermute | solution.py:335
  30.4 1.9 copy-start.2
  42.8 1.7 copy-start
  44.5 102.8 %collective-permute-start.10 = (bf16[768,2048]{1,0:T(8,128)(2,1)}, bf16[768,2048]{1,0:T(8,128)(2,1)}, u32[]{:S(2)}, u32[]{:S(2)}) collective-permute-start(bf16[768,2048]{1,0:T(8,128)(2,1)} %shard_map.75._.refs_1_), channel_id=1, source_target_pairs={{1,0},{2,3},{5,4},{6,7},{9,8},{10,11},{13,12},{14,15},{17,16},{18,... | collective-permute-start | bytes 9437192 | tf_op jit(solution)/shard_map/ppermute | solution.py:373
  74.7 58.5 %collective-permute-start.7 = (bf16[512,2048]{1,0:T(8,128)(2,1)}, bf16[512,2048]{1,0:T(8,128)(2,1)}, u32[]{:S(2)}, u32[]{:S(2)}) collective-permute-start(bf16[512,2048]{1,0:T(8,128)(2,1)} %bitcast.29), channel_id=1, source_target_pairs={{0,12},{4,8},{8,4},{12,0},{1,13},{5,9},{9,5},{13,1},{2,14},{6,10},... | collective-permute-start | bytes 6291464 | tf_op jit(solution)/shard_map/ppermute | solution.py:335
  78.5 53.6 %collective-permute-start.8 = (bf16[384,2048]{1,0:T(8,128)(2,1)}, bf16[384,2048]{1,0:T(8,128)(2,1)S(1)}, u32[]{:S(2)}, u32[]{:S(2)}) collective-permute-start(bf16[384,2048]{1,0:T(8,128)(2,1)} %get-tuple-element.17.__1_), channel_id=1, source_target_pairs={{1,2},{2,1},{5,6},{6,5},{9,10},{10,9},{13,14},{14,13},{17,18},{18,... | collective-permute-start | bytes 4718600 | tf_op jit(solution)/shard_map/ppermute | solution.py:375
  87.3 60.6 %collective-permute-start.2 = (bf16[384,2048]{1,0:T(8,128)(2,1)}, bf16[384,2048]{1,0:T(8,128)(2,1)S(1)}, u32[]{:S(2)}, u32[]{:S(2)}) collective-permute-start(bf16[384,2048]{1,0:T(8,128)(2,1)} %get-tuple-element.16), channel_id=1, source_target_pairs={{1,2},{2,1},{5,6},{6,5},{9,10},{10,9},{13,14},{14,13},{17,18},{18,... | collective-permute-start | bytes 4718600 | tf_op jit(solution)/shard_map/ppermute | solution.py:375
  88.3 12.6 %copy-start.3 = (bf16[768,2048]{1,0:T(8,128)(2,1)S(1)}, bf16[768,2048]{1,0:T(8,128)(2,1)}, u32[]{:S(2)}) copy-start(bf16[768,2048]{1,0:T(8,128)(2,1)} %refs_1_.7) | copy-start | bytes 9437188
  117.6 14.4 %copy-start.11 = (f32[16,768]{1,0:T(8,128)}, f32[16,768]{1,0:T(8,128)S(1)}, u32[]{:S(2)}) copy-start(f32[16,768]{1,0:T(8,128)S(1)} %shard_map.80.__1_) | copy-start | bytes 147460
  117.7 13.8 %collective-permute-start.6 = (f32[16,768]{1,0:T(8,128)S(1)}, f32[16,768]{1,0:T(8,128)S(1)}, u32[]{:S(2)}, u32[]{:S(2)}) collective-permute-start(f32[16,768]{1,0:T(8,128)S(1)} %shard_map.80.__1_), channel_id=1, source_target_pairs={{0,8},{4,12},{8,0},{12,4},{1,9},{5,13},{9,1},{13,5},{2,10},{6,14},... | collective-permute-start | bytes 147464 | tf_op jit(solution)/shard_map/ppermute | solution.py:335
  132.1 1.2 copy-start.4
  133.2 5.5 %copy-start.5 = (bf16[384,2048]{1,0:T(8,128)(2,1)S(1)}, bf16[384,2048]{1,0:T(8,128)(2,1)}, u32[]{:S(2)}) copy-start(bf16[384,2048]{1,0:T(8,128)(2,1)} %shard_map.81.__1_.refs_0_) | copy-start | bytes 4718596
  133.2 51.3 %collective-permute-start.14 = (bf16[512,2048]{1,0:T(8,128)(2,1)}, bf16[512,2048]{1,0:T(8,128)(2,1)}, u32[]{:S(2)}, u32[]{:S(2)}) collective-permute-start(bf16[512,2048]{1,0:T(8,128)(2,1)} %bitcast.28), channel_id=1, source_target_pairs={{0,4},{4,0},{8,12},{12,8},{1,5},{5,1},{9,13},{13,9},{2,6},{6,2},{1... | collective-permute-start | bytes 6291464 | tf_op jit(solution)/shard_map/ppermute | solution.py:335
  133.2 1.6 copy-start.12
  133.3 51.3 %collective-permute-start.15 = (bf16[512,2048]{1,0:T(8,128)(2,1)}, bf16[512,2048]{1,0:T(8,128)(2,1)}, u32[]{:S(2)}, u32[]{:S(2)}) collective-permute-start(bf16[512,2048]{1,0:T(8,128)(2,1)} %shard_map.84.__1_), channel_id=1, source_target_pairs={{0,8},{4,12},{8,0},{12,4},{1,9},{5,13},{9,1},{13,5},{2,10},{6,14},... | collective-permute-start | bytes 6291464 | tf_op jit(solution)/shard_map/ppermute | solution.py:335
  134.8 3.9 %collective-permute-start.9 = (f32[16,768]{1,0:T(8,128)S(1)}, f32[16,768]{1,0:T(8,128)S(1)}, u32[]{:S(2)}, u32[]{:S(2)}) collective-permute-start(f32[16,768]{1,0:T(8,128)S(1)} %copy-done.12), channel_id=1, source_target_pairs={{0,1},{3,2},{4,5},{7,6},{8,9},{11,10},{12,13},{15,14},{16,17},{19,... | collective-permute-start | bytes 147464 | tf_op jit(solution)/shard_map/ppermute | solution.py:388
  138.8 61.3 %collective-permute-start.17 = (bf16[384,2048]{1,0:T(8,128)(2,1)S(1)}, bf16[384,2048]{1,0:T(8,128)(2,1)}, u32[]{:S(2)}, u32[]{:S(2)}) collective-permute-start(bf16[384,2048]{1,0:T(8,128)(2,1)S(1)} %copy-done.5), channel_id=1, source_target_pairs={{1,0},{2,3},{5,4},{6,7},{9,8},{10,11},{13,12},{14,15},{17,16},{18,... | collective-permute-start | bytes 4718600 | tf_op jit(solution)/shard_map/ppermute | solution.py:383
  147.2 14.5 %collective-permute-start.11 = (f32[16,768]{1,0:T(8,128)}, f32[16,768]{1,0:T(8,128)S(1)}, u32[]{:S(2)}, u32[]{:S(2)}) collective-permute-start(f32[16,768]{1,0:T(8,128)} %shard_map.86.refs_5_), channel_id=1, source_target_pairs={{1,2},{2,1},{5,6},{6,5},{9,10},{10,9},{13,14},{14,13},{17,18},{18,... | collective-permute-start | bytes 147464 | tf_op jit(solution)/shard_map/ppermute | solution.py:389
  147.9 0.8 copy-start.9
  162.4 19.0 %collective-permute-start.12 = (bf16[16,768]{1,0:T(8,128)(2,1)}, bf16[16,768]{1,0:T(8,128)(2,1)S(1)}, u32[]{:S(2)}, u32[]{:S(2)}) collective-permute-start(bf16[16,768]{1,0:T(8,128)(2,1)} %shard_map.88._), channel_id=1, source_target_pairs={{1,0},{2,3},{5,4},{6,7},{9,8},{10,11},{13,12},{14,15},{17,16},{18,... | collective-permute-start | bytes 73736 | tf_op jit(solution)/shard_map/ppermute | solution.py:392
  163.7 0.7 copy-start.10
  165.4 0.9 copy-start.6
  166.3 42.2 %collective-permute-start.16 = (bf16[192,2048]{1,0:T(8,128)(2,1)}, bf16[192,2048]{1,0:T(8,128)(2,1)S(1)}, u32[]{:S(2)}, u32[]{:S(2)}) collective-permute-start(bf16[192,2048]{1,0:T(8,128)(2,1)} %get-tuple-element.22.__1_), channel_id=1, source_target_pairs={{1,0},{2,3},{5,4},{6,7},{9,8},{10,11},{13,12},{14,15},{17,16},{18,... | collective-permute-start | bytes 2359304 | tf_op jit(solution)/shard_map/ppermute | solution.py:394
  181.4 0.6 copy-start.13
  182.0 32.9 %collective-permute-start.13 = (bf16[192,2048]{1,0:T(8,128)(2,1)}, bf16[192,2048]{1,0:T(8,128)(2,1)S(1)}, u32[]{:S(2)}, u32[]{:S(2)}) collective-permute-start(bf16[192,2048]{1,0:T(8,128)(2,1)} %shard_map.91.refs_7_), channel_id=1, source_target_pairs={{1,0},{2,3},{5,4},{6,7},{9,8},{10,11},{13,12},{14,15},{17,16},{18,... | collective-permute-start | bytes 2359304 | tf_op jit(solution)/shard_map/ppermute | solution.py:396
  184.5 1.1 copy-start.7
  185.6 1.6 copy-start.8
  187.2 12.8 %copy-start.1 = (bf16[768,2048]{1,0:T(8,128)(2,1)S(1)}, bf16[768,2048]{1,0:T(8,128)(2,1)}, u32[]{:S(2)}) copy-start(bf16[768,2048]{1,0:T(8,128)(2,1)} %shard_map.75._.refs_1_) | copy-start | bytes 9437188

commit v3 on v2

--- a/solution.py
+++ b/solution.py
@@ -9,7 +9,7 @@
 
 F32 = jnp.float32
 BF16 = jnp.bfloat16
-ROOM = 48 * 1024 * 1024
+ROOM = 36 * 1024 * 1024
 TILE = 512
 
 
@@ -17,7 +17,7 @@
     def __init__(self, first):
         self.last = first
 
-    def call(self, kernel, at, args, specs, **rest):
+    def call(self, kernel, at, args, specs, room=ROOM, **rest):
         after = [] if rest.get("input_output_aliases") else [self.last]
 
         def body(at_ref, *refs):
@@ -30,7 +30,7 @@
                 in_specs=list(specs) + [pl.BlockSpec(memory_space=pl.ANY)] * len(after),
                 **rest.pop("grid_spec"),
             ),
-            compiler_params=pltpu.CompilerParams(vmem_limit_bytes=ROOM),
+            compiler_params=pltpu.CompilerParams(vmem_limit_bytes=room),
             cost_estimate=pl.CostEstimate(flops=1, bytes_accessed=1, transcendentals=0),
             **rest,
         )(at, *args, *after)
@@ -143,10 +143,10 @@
     out[...] = value.astype(BF16) if rounded else value
 
 
-def add_products(order, terms, total=None, first=0, rows=None, whole=None, out=None, rounded=False):
+def add_products(order, terms, total=None, first=0, rows=None, whole=None, out=None, rounded=False, room=ROOM):
     rows = rows or terms[0][0][-1].shape[0]
     width = terms[0][1].shape[1]
-    tile = min(TILE, width)
+    tile = min(2 * TILE if rounded else TILE, width)
     at = jnp.stack([jnp.asarray(t[2], jnp.int32) for t in terms])
     here = first // rows
     there = here if whole else 0
@@ -183,6 +183,7 @@
         at,
         args,
         specs,
+        room,
         out_shape=jax.ShapeDtypeStruct((whole or rows, width), dtype),
         grid_spec=dict(
             grid=(width // tile,),
@@ -237,6 +238,23 @@
             out_specs=pl.BlockSpec((rows, tile), lambda j, at: (0, j)),
             scratch_shapes=[pltpu.VMEM((len(factors), rows, most * rank), BF16)],
         ),
+    )
+
+
+def block_of(order, matrix, at, depth):
+    width = matrix.shape[1]
+    tile = depth // 4
+
+    def kernel(at_ref, x, out):
+        out[...] = x[...]
+
+    return order.call(
+        kernel,
+        jnp.asarray(at, jnp.int32)[None],
+        [matrix],
+        [pl.BlockSpec((tile, width), lambda i, at: (4 * at[0] + i, 0))],
+        out_shape=jax.ShapeDtypeStruct((depth, width), matrix.dtype),
+        grid_spec=dict(grid=(4,), out_specs=pl.BlockSpec((tile, width), lambda i, at: (i, 0))),
     )
 
 
@@ -368,7 +386,7 @@
         step = rows // 4
         near = lax.ppermute(tokens, "tensor", swap)
         cross = lax.ppermute(tokens, "tensor", middle)
-        own = add_products(order, [([tokens], weight, line)])
+        own = add_products(order, [([tokens], weight, line)], room=62 * 1024 * 1024)
         cross = order.hold(cross)
         out_near = lax.ppermute(cross, "tensor", outward)
         cuts = order.cut(near, [2 * step] * 2)
@@ -392,6 +410,7 @@
         told = lax.ppermute(low, "tensor", outward)
         pieces = order.cut(far[1], [step] * 2)
         out_far.append(lax.ppermute(pieces[0], "tensor", outward))
+        last = block_of(order, weight, line ^ 3, depth)
         told = order.hold(told)
         out_far.append(lax.ppermute(order.hold(pieces[1]), "tensor", outward))
         low = jnp.where((line == 1) | (line == 2), low, told)
@@ -408,8 +427,7 @@
     out = None
     first = 0
     for x in out_far:
-        last = [([x, cross], weight, line ^ 3)]
-        out = add_products(order, last, total, first, x.shape[0], rows, out, True)
+        out = add_products(order, [([x, cross], last, 0)], total, first, x.shape[0], rows, out, True)
         first += x.shape[0]
     return out
 

time: 222 us -> 218 us (0.982)
  waiting for transfers between devices: 70.8 us -> 59.7 us
  local copies, waits for them, and re-layouts: 13.2 us -> 21 us
  Pallas kernels: 104 us -> 97.5 us
  starting transfers between devices: 23.5 us -> 28.6 us
    ppermute x1, waiting for transfers between devices: 13.8 us -> 0.01 us  [body(): told = lax.ppermute(low, 'tensor', outward)]
    pallas_call x10 -> x11, Pallas kernels: 99.3 us -> 91.4 us  [call(): pl.pallas_call(body, grid_spec=pltpu.PrefetchScalarGridSpec(num_scalar_pr...]
    unnamed x30 -> x44, local copies, waits for them, and re-layouts: 11.3 us -> 19.1 us
    ppermute x1, waiting for transfers between devices: 0.01 us -> 4.6 us  [body(): out_far.append(lax.ppermute(order.hold(pieces[1]), 'tensor', outward))]
    ppermute x7, starting transfers between devices: 5.73 us -> 8.56 us  [send(): return lax.ppermute(block, 'dp', [(i, i ^ k) for i in range(groups)])]
  transfers between devices with their start and end apart: 18 -> 18, of which waited for: 6 -> 6; matrix products, arithmetic and copies ran while one was open for 5% -> 6% of each run, Pallas kernels for 44% -> 43%
where the time goes in v3:
time: 218 us; the launch traced here: 216 us
  Pallas kernels  97.5 us (45%)
  waiting for transfers between devices  59.7 us (27%)
  starting transfers between devices  28.6 us (13%)
  local copies, waits for them, and re-layouts  21 us (10%)
  other arithmetic  9.25 us (4%)
    pallas_call x11, Pallas kernels, call(): pl.pallas_call(body, grid_spec=pltpu.PrefetchScalarGridSpec(num_scalar_pr...  91.4 us
    ppermute x1, waiting for transfers between devices, body(): near = lax.ppermute(tokens, 'tensor', swap)  29 us
    unnamed x44, local copies, waits for them, and re-layouts  19.1 us
    ppermute x7, waiting for transfers between devices, send(): return lax.ppermute(block, 'dp', [(i, i ^ k) for i in range(groups)])  18.4 us
    ppermute x7, starting transfers between devices, send(): return lax.ppermute(block, 'dp', [(i, i ^ k) for i in range(groups)])  8.56 us
    pallas_call x2, Pallas kernels, cut(): pl.pallas_call(kernel, out_shape=[jax.ShapeDtypeStruct((size, x.shape[1])...  6.02 us
    ppermute x1, waiting for transfers between devices, body(): out_near = lax.ppermute(cross, 'tensor', outward)  5.93 us
    ppermute x1, waiting for transfers between devices, body(): out_far.append(lax.ppermute(order.hold(pieces[1]), 'tensor', outward))  4.6 us
  transfers between devices with their start and end apart: 18, of which 6 were waited for; matrix products, arithmetic and copies ran while one was open for 6% of the time, Pallas kernels for 43%

profile of v3, /device:TPU:0, one launch (start us, length us, event | category | flops | bytes accessed | tf_op | source)
XLA Modules:
  0.0 216.5 jit_solution(420867239870916635)
XLA Ops:
  0.0 2.3 %collective-permute-start.1 = (bf16[768,2048]{1,0:T(8,128)(2,1)}, bf16[768,2048]{1,0:T(8,128)(2,1)}, u32[]{:S(2)}, u32[]{:S(2)}) collective-permute-start(bf16[768,2048]{1,0:T(8,128)(2,1)} %refs_1_.7), channel_id=1, source_target_pairs={{1,2},{2,1},{5,6},{6,5},{9,10},{10,9},{13,14},{14,13},{17,18},{18,... | collective-permute-start | bytes 9437192 | tf_op jit(solution)/shard_map/ppermute | solution.py:388
  2.3 4.3 %collective-permute-start = (bf16[768,2048]{1,0:T(8,128)(2,1)}, bf16[768,2048]{1,0:T(8,128)(2,1)}, u32[]{:S(2)}, u32[]{:S(2)}) collective-permute-start(bf16[768,2048]{1,0:T(8,128)(2,1)} %refs_1_.7), channel_id=1, source_target_pairs={{0,1},{1,0},{2,3},{3,2},{4,5},{5,4},{6,7},{7,6},{8,9},{9,8},{10,11... | collective-permute-start | bytes 9437192 | tf_op jit(solution)/shard_map/ppermute | solution.py:387
  6.6 0.8 eq.100
  7.4 1.0 select_reduce_fusion
  8.4 0.8 copy.24
  9.2 0.1 reduce-window.4
  9.2 0.1 reduce
  9.4 0.7 fusion.3
  10.0 0.2 select_reduce_fusion.2
  10.4 0.1 select_reduce_fusion.1
  10.6 4.0 %pad_maximum_fusion = bf16[784,2048]{1,0:T(8,128)(2,1)} fusion(bf16[16,2048]{1,0:T(8,128)(2,1)S(1)} %convert_element_type.13, bf16[768,2048]{1,0:T(8,128)(2,1)} %refs_1_.7), kind=kLoop, calls=%fused_computation | loop fusion | flops 6422528 | bytes 6422528 | tf_op jit(solution)/shard_map/concatenate | solution.py:364
  14.6 1.5 collective-permute-start.4
  16.1 0.1 select_reduce_fusion.3
  16.3 0.1 select_reduce_fusion.4
  16.4 7.3 %shard_map.73 = (bf16[32,16,2048]{2,1,0:T(8,128)(2,1)}, bf16[32,16,2048]{2,1,0:T(8,128)(2,1)}, bf16[32,16,2048]{2,1,0:T(8,128)(2,1)S(1)}, bf16[32,16,2048]{2,1,0...) custom-call(s32[5,32]{1,0:T(8,128)S(1)} %pad_add_fusion.at_ref.refs_2_, ...), custom_call_target="tpu_custom_call" | custom-call | flops 1 | bytes 1 | tf_op jit(solution)/shard_map/pallas_call | solution.py:26
  23.7 1.3 copy-done.6
  25.1 1.3 copy-done.9
  26.4 1.4 copy-done.15
  27.7 1.4 copy-done.16
  29.1 3.8 %collective-permute-start.3 = (bf16[512,2048]{1,0:T(8,128)(2,1)}, bf16[512,2048]{1,0:T(8,128)(2,1)}, u32[]{:S(2)}, u32[]{:S(2)}) collective-permute-start(bf16[512,2048]{1,0:T(8,128)(2,1)} %bitcast.3), channel_id=1, source_target_pairs={{0,4},{4,0},{8,12},{12,8},{1,5},{5,1},{9,13},{13,9},{2,6},{6,2},{1... | collective-permute-start | bytes 6291464 | tf_op jit(solution)/shard_map/ppermute | solution.py:353
  32.9 11.4 %shard_map.74.__1_.refs_2_ = f32[768,2048]{1,0:T(8,128)} custom-call(s32[1]{0:T(128)} %bitcast.at_ref, bf16[768,2048]{1,0:T(8,128)(2,1)} %refs_1_.7, bf16[8192,2048]{1,0:T(8,128)(2,1)} %refs_0_.5, bf16[32,16,2048]{2,1,0:T(8,128)(2,1)} %get-tuple-element.15.refs_2_), custom_call_target="tpu_custom_call" | custom-call | flops 1 | bytes 1 | tf_op jit(solution)/shard_map/pallas_call | solution.py:26
  44.4 1.3 collective-permute-start.10
  45.7 29.0 %collective-permute-done.x_ref.refs_0_ = bf16[768,2048]{1,0:T(8,128)(2,1)} collective-permute-done((bf16[768,2048]{1,0:T(8,128)(2,1)}, bf16[768,2048]{1,0:T(8,128)(2,1)}, u32[]{:S(2)}, u32[]{:S(2)}) %collective-permute-start) | collective-permute-done | bytes 3145760 | tf_op jit(solution)/shard_map/ppermute | solution.py:387
  74.8 3.6 %shard_map.76 = (bf16[384,2048]{1,0:T(8,128)(2,1)}, bf16[384,2048]{1,0:T(8,128)(2,1)}) custom-call(bf16[768,2048]{1,0:T(8,128)(2,1)} %collective-permute-done.x_ref.refs_0_, bf16[768,2048]{1,0:T(8,128)(2,1)} %shard_map.75._.refs_1_), custom_call_target="tpu_custom_call" | custom-call | flops 1 | bytes 1 | tf_op jit(solution)/shard_map/pallas_call | solution.py:60
  78.4 1.9 collective-permute-start.8
  80.3 7.0 %collective-permute-done.4.__0_ = bf16[784,2048]{1,0:T(8,128)(2,1)} collective-permute-done((bf16[784,2048]{1,0:T(8,128)(2,1)}, bf16[784,2048]{1,0:T(8,128)(2,1)}, u32[]{:S(2)}, u32[]{:S(2)}) %collective-permute-start.4) | collective-permute-done | bytes 3211296 | tf_op jit(solution)/shard_map/ppermute | solution.py:353
  87.3 1.8 collective-permute-start.2
  89.2 11.0 %shard_map.78.refs_4_ = f32[768,2048]{1,0:T(8,128)S(1)} custom-call(s32[1]{0:T(128)} %bitcast.4.at_ref, bf16[768,2048]{1,0:T(8,128)(2,1)} %collective-permute-done.x_ref.refs_0_, bf16[8192,2048]{1,0:T(8,128)(2,1)} %refs_0_.5, f32[768,2048]{1,0:T(8,128)} %shard_map.74.__1_.refs_2_, bf16[784,2048]{1,0:T(8,128)(2,1)} %shard_map.77.refs_3_.refs_1_), custom_call_target="tpu_custom_call" | custom-call | flops 1 | bytes 1 | tf_op jit(solution)/shard_map/pallas_call | solution.py:26
  100.2 9.0 %shard_map.79.refs_4_ = f32[16,768]{1,0:T(8,128)S(1)} custom-call(s32[5,32]{1,0:T(8,128)S(1)} %pad_add_fusion.at_ref.refs_2_, s32[1,768]{1,0:T(1,128)S(1)} %broadcast_in_dim.130.refs_0_, bf16[768,2048]{1,0:T(8,128)(2,1)S(1)} %copy-done.3, bf16[256,16,2048]{2,1,0:T(8,128)(2,1)} %refs_2_.3, bf16[512,2048]{1,0:T(8,128)(2,1)} %collective-permute-done.3.refs_3_, ...), custom_call_target="tpu_custom_call" | custom-call | flops 1 | bytes 1 | tf_op jit(solution)/shard_map/pallas_call | solution.py:26
  109.2 0.8 slice_bitcast_fusion
  110.1 8.4 %shard_map.80.__1_ = f32[16,768]{1,0:T(8,128)S(1)} custom-call(s32[5,32]{1,0:T(8,128)S(1)} %pad_add_fusion.at_ref.refs_2_, s32[1,768]{1,0:T(1,128)S(1)} %broadcast_in_dim.131.refs_0_, bf16[784,2048]{1,0:T(8,128)(2,1)} %shard_map.77.refs_3_.refs_1_, bf16[256,16,2048]{2,1,0:T(8,128)(2,1)} %refs_2_.3, bf16[512,2048]{1,0:T(8,128)(2,1)} %collective-permute-done.5.refs_3_, ...), custom_call_target="tpu_custom_call" | custom-call | flops 1 | bytes 1 | tf_op jit(solution)/shard_map/pallas_call | solution.py:26
  118.5 1.6 collective-permute-start.6
  120.1 11.4 %collective-permute-done.6 = f32[16,768]{1,0:T(8,128)S(1)} collective-permute-done((f32[16,768]{1,0:T(8,128)S(1)}, f32[16,768]{1,0:T(8,128)S(1)}, u32[]{:S(2)}, u32[]{:S(2)}) %collective-permute-start.6) | collective-permute-done | bytes 49184 | tf_op jit(solution)/shard_map/ppermute | solution.py:353
  131.4 0.6 add.38.__0_
  132.2 1.6 collective-permute-start.15
  133.8 2.2 %collective-permute-start.9 = (f32[16,768]{1,0:T(8,128)S(1)}, f32[16,768]{1,0:T(8,128)S(1)}, u32[]{:S(2)}, u32[]{:S(2)}) collective-permute-start(f32[16,768]{1,0:T(8,128)S(1)} %copy-done.17), channel_id=1, source_target_pairs={{0,1},{3,2},{4,5},{7,6},{8,9},{11,10},{12,13},{15,14},{16,17},{19,... | collective-permute-start | bytes 147464 | tf_op jit(solution)/shard_map/ppermute | solution.py:406
  136.0 1.7 collective-permute-done.9
  137.7 1.3 collective-permute-start.17
  139.0 0.6 add.39.__0_
  139.6 5.9 %collective-permute-done.10.__0_ = bf16[768,2048]{1,0:T(8,128)(2,1)S(1)} collective-permute-done((bf16[768,2048]{1,0:T(8,128)(2,1)}, bf16[768,2048]{1,0:T(8,128)(2,1)S(1)}, u32[]{:S(2)}, u32[]{:S(2)}) %collective-permute-start.10) | collective-permute-done | bytes 3145760 | tf_op jit(solution)/shard_map/ppermute | solution.py:391
  145.6 1.7 copy-done.4
  147.2 0.8 collective-permute-start.11
  148.0 1.1 copy-done.5
  149.1 0.8 copy-done.11
  149.9 11.4 %shard_map.87.__1_.refs_6_ = f32[768,2048]{1,0:T(8,128)S(1)} custom-call(s32[1]{0:T(128)} %bitcast.8.at_ref, bf16[384,2048]{1,0:T(8,128)(2,1)} %shard_map.81.__1_.refs_0_, bf16[384,2048]{1,0:T(8,128)(2,1)} %collective-permute-done.2.refs_1_.x_ref, bf16[768,2048]{1,0:T(8,128)(2,1)S(1)} %copy-done.5, bf16[8192,2048]{1,0:T(8,128)(2,1)} %refs_0_.5, ...), custom_call_target="tpu_custom_call" | custom-call | flops 1 | bytes 1 | tf_op jit(solution)/shard_map/pallas_call | solution.py:26
  161.3 2.7 %copy-done.1 = f32[768,2048]{1,0:T(8,128)} copy-done((f32[768,2048]{1,0:T(8,128)}, f32[768,2048]{1,0:T(8,128)S(1)}, u32[]{:S(2)}) %copy-start.1) | copy-done | bytes 6291480
  164.0 0.6 add_convert_fusion.__0_
  164.6 1.3 collective-permute-start.12
  165.9 0.7 copy-done.12
  166.7 2.4 %shard_map.89 = (bf16[192,2048]{1,0:T(8,128)(2,1)}, bf16[192,2048]{1,0:T(8,128)(2,1)S(1)}) custom-call(bf16[384,2048]{1,0:T(8,128)(2,1)} %collective-permute-done.2.refs_1_.x_ref, bf16[16,768]{1,0:T(8,128)(2,1)S(1)} %copy-done.12), custom_call_target="tpu_custom_call" | custom-call | flops 1 | bytes 1 | tf_op jit(solution)/shard_map/pallas_call | solution.py:60
  169.1 0.9 copy-done.7
  170.0 1.3 collective-permute-start.16
  171.2 4.3 %shard_map.90.__1_.refs_2_ = bf16[2048,2048]{1,0:T(8,128)(2,1)S(1)} custom-call(s32[1]{0:T(128)} %bitcast.9.at_ref, bf16[8192,2048]{1,0:T(8,128)(2,1)} %refs_0_.5, bf16[192,2048]{1,0:T(8,128)(2,1)} %get-tuple-element.22.refs_1_), custom_call_target="tpu_custom_call" | custom-call | flops 1 | bytes 1 | tf_op jit(solution)/shard_map/pallas_call | solution.py:26
  175.5 3.2 %copy-done = bf16[2048,2048]{1,0:T(8,128)(2,1)} copy-done((bf16[2048,2048]{1,0:T(8,128)(2,1)}, bf16[2048,2048]{1,0:T(8,128)(2,1)S(1)}, u32[]{:S(2)}) %copy-start) | copy-done | bytes 8388632
  178.8 0.6 copy-done.18
  179.4 1.6 collective-permute-start.13
  181.0 0.2 broadcast_in_dim.134.refs_1_
  181.3 0.7 broadcast_select_fusion.refs_0_
  182.1 1.1 copy-done.8
  183.2 11.4 %shard_map.93.refs_3_.refs_4_ = f32[768,2048]{1,0:T(8,128)S(1)} custom-call(s32[8]{0:T(128)S(1)} %stack.31.at_ref, bf16[16,768]{1,0:T(8,128)(2,1)S(1)} %broadcast_select_fusion.refs_0_, s32[768,1]{1,0:T(8,128)S(1)} %broadcast_in_dim.134.refs_1_, bf16[512,2048]{1,0:T(8,128)(2,1)S(1)} %bitcast.27, bf16[512,2048]{1,0:T(8,128)(2,1)} %collective-permute-done.14.refs_3_, ...), custom_call_target="tpu_custom_call" | custom-call | flops 1 | bytes 1 | tf_op jit(solution)/shard_map/pallas_call | solution.py:26
  194.6 8.2 %shard_map.94.refs_4_ = bf16[768,2048]{1,0:T(8,128)(2,1)} custom-call(s32[1]{0:T(128)} %constant.39.clone.1.at_ref, bf16[384,2048]{1,0:T(8,128)(2,1)} %collective-permute-done.17.refs_0_, bf16[768,2048]{1,0:T(8,128)(2,1)} %shard_map.75._.refs_1_, bf16[2048,2048]{1,0:T(8,128)(2,1)} %copy-done, f32[768,2048]{1,0:T(8,128)S(1)} %shard_map.93.refs_3_.refs_4_, ...), custom_call_target="tpu_custom_call" | custom-call | flops 1 | bytes 1 | tf_op jit(solution)/shard_map/pallas_call | solution.py:26
  202.8 4.4 %shard_map.95.refs_4_ = bf16[768,2048]{1,0:T(8,128)(2,1)} custom-call(s32[1]{0:T(128)} %constant.39.clone.1.at_ref, bf16[192,2048]{1,0:T(8,128)(2,1)S(1)} %collective-permute-done.16.refs_0_, bf16[768,2048]{1,0:T(8,128)(2,1)} %shard_map.75._.refs_1_, bf16[2048,2048]{1,0:T(8,128)(2,1)S(1)} %bitcast.25, ...), custom_call_target="tpu_custom_call", output_to_operand_aliasing={{}: (5, {})} | custom-call | flops 1 | bytes 1 | tf_op jit(solution)/shard_map/pallas_call | solution.py:26
  207.2 4.6 %collective-permute-done.13.refs_0_ = bf16[192,2048]{1,0:T(8,128)(2,1)} collective-permute-done((bf16[192,2048]{1,0:T(8,128)(2,1)}, bf16[192,2048]{1,0:T(8,128)(2,1)}, u32[]{:S(2)}, u32[]{:S(2)}) %collective-permute-start.13) | collective-permute-done | bytes 786464 | tf_op jit(solution)/shard_map/ppermute | solution.py:415
  211.8 4.6 %shard_map.96 = bf16[768,2048]{1,0:T(8,128)(2,1)} custom-call(s32[1]{0:T(128)} %constant.39.clone.1.at_ref, bf16[192,2048]{1,0:T(8,128)(2,1)} %collective-permute-done.13.refs_0_, bf16[768,2048]{1,0:T(8,128)(2,1)} %shard_map.75._.refs_1_, bf16[2048,2048]{1,0:T(8,128)(2,1)S(1)} %bitcast.25, ...), custom_call_target="tpu_custom_call", output_to_operand_aliasing={{}: (5, {})} | custom-call | flops 1 | bytes 1 | tf_op jit(solution)/shard_map/pallas_call | solution.py:26
  (75 shorter events, 0.7 us)
Async XLA Ops:
  0.0 44.4 %collective-permute-start.1 = (bf16[768,2048]{1,0:T(8,128)(2,1)}, bf16[768,2048]{1,0:T(8,128)(2,1)}, u32[]{:S(2)}, u32[]{:S(2)}) collective-permute-start(bf16[768,2048]{1,0:T(8,128)(2,1)} %refs_1_.7), channel_id=1, source_target_pairs={{1,2},{2,1},{5,6},{6,5},{9,10},{10,9},{13,14},{14,13},{17,18},{18,... | collective-permute-start | bytes 9437192 | tf_op jit(solution)/shard_map/ppermute | solution.py:388
  2.3 72.4 %collective-permute-start = (bf16[768,2048]{1,0:T(8,128)(2,1)}, bf16[768,2048]{1,0:T(8,128)(2,1)}, u32[]{:S(2)}, u32[]{:S(2)}) collective-permute-start(bf16[768,2048]{1,0:T(8,128)(2,1)} %refs_1_.7), channel_id=1, source_target_pairs={{0,1},{1,0},{2,3},{3,2},{4,5},{5,4},{6,7},{7,6},{8,9},{9,8},{10,11... | collective-permute-start | bytes 9437192 | tf_op jit(solution)/shard_map/ppermute | solution.py:387
  14.6 72.8 %collective-permute-start.4 = (bf16[784,2048]{1,0:T(8,128)(2,1)}, bf16[784,2048]{1,0:T(8,128)(2,1)}, u32[]{:S(2)}, u32[]{:S(2)}) collective-permute-start(bf16[784,2048]{1,0:T(8,128)(2,1)} %pad_maximum_fusion), channel_id=1, source_target_pairs={{0,8},{4,12},{8,0},{12,4},{1,9},{5,13},{9,1},{13,5},{2,10},{6,14},... | collective-permute-start | bytes 9633800 | tf_op jit(solution)/shard_map/ppermute | solution.py:353
  23.7 1.3 copy-start.6
  25.1 1.3 copy-start.9
  26.4 1.4 copy-start.15
  27.7 1.4 copy-start.16
  29.1 49.3 %collective-permute-start.3 = (bf16[512,2048]{1,0:T(8,128)(2,1)}, bf16[512,2048]{1,0:T(8,128)(2,1)}, u32[]{:S(2)}, u32[]{:S(2)}) collective-permute-start(bf16[512,2048]{1,0:T(8,128)(2,1)} %bitcast.3), channel_id=1, source_target_pairs={{0,4},{4,0},{8,12},{12,8},{1,5},{5,1},{9,13},{13,9},{2,6},{6,2},{1... | collective-permute-start | bytes 6291464 | tf_op jit(solution)/shard_map/ppermute | solution.py:353
  32.9 77.1 %collective-permute-start.5 = (bf16[512,2048]{1,0:T(8,128)(2,1)}, bf16[512,2048]{1,0:T(8,128)(2,1)}, u32[]{:S(2)}, u32[]{:S(2)}) collective-permute-start(bf16[512,2048]{1,0:T(8,128)(2,1)} %bitcast.5), channel_id=1, source_target_pairs={{0,4},{4,0},{8,12},{12,8},{1,5},{5,1},{9,13},{13,9},{2,6},{6,2},{1... | collective-permute-start | bytes 6291464 | tf_op jit(solution)/shard_map/ppermute | solution.py:353
  44.4 101.2 %collective-permute-start.10 = (bf16[768,2048]{1,0:T(8,128)(2,1)}, bf16[768,2048]{1,0:T(8,128)(2,1)S(1)}, u32[]{:S(2)}, u32[]{:S(2)}) collective-permute-start(bf16[768,2048]{1,0:T(8,128)(2,1)} %shard_map.75._.refs_1_), channel_id=1, source_target_pairs={{1,0},{2,3},{5,4},{6,7},{9,8},{10,11},{13,12},{14,15},{17,16},{18,... | collective-permute-start | bytes 9437192 | tf_op jit(solution)/shard_map/ppermute | solution.py:391
  74.7 57.4 %collective-permute-start.7 = (bf16[512,2048]{1,0:T(8,128)(2,1)}, bf16[512,2048]{1,0:T(8,128)(2,1)}, u32[]{:S(2)}, u32[]{:S(2)}) collective-permute-start(bf16[512,2048]{1,0:T(8,128)(2,1)} %bitcast.29), channel_id=1, source_target_pairs={{0,12},{4,8},{8,4},{12,0},{1,13},{5,9},{9,5},{13,1},{2,14},{6,10},... | collective-permute-start | bytes 6291464 | tf_op jit(solution)/shard_map/ppermute | solution.py:353
  78.4 53.7 %collective-permute-start.8 = (bf16[384,2048]{1,0:T(8,128)(2,1)}, bf16[384,2048]{1,0:T(8,128)(2,1)}, u32[]{:S(2)}, u32[]{:S(2)}) collective-permute-start(bf16[384,2048]{1,0:T(8,128)(2,1)} %get-tuple-element.17.__1_), channel_id=1, source_target_pairs={{1,2},{2,1},{5,6},{6,5},{9,10},{10,9},{13,14},{14,13},{17,18},{18,... | collective-permute-start | bytes 4718600 | tf_op jit(solution)/shard_map/ppermute | solution.py:393
  87.3 60.7 %collective-permute-start.2 = (bf16[384,2048]{1,0:T(8,128)(2,1)}, bf16[384,2048]{1,0:T(8,128)(2,1)}, u32[]{:S(2)}, u32[]{:S(2)}) collective-permute-start(bf16[384,2048]{1,0:T(8,128)(2,1)} %get-tuple-element.16), channel_id=1, source_target_pairs={{1,2},{2,1},{5,6},{6,5},{9,10},{10,9},{13,14},{14,13},{17,18},{18,... | collective-permute-start | bytes 4718600 | tf_op jit(solution)/shard_map/ppermute | solution.py:393
  89.2 11.0 %copy-start.3 = (bf16[768,2048]{1,0:T(8,128)(2,1)S(1)}, bf16[768,2048]{1,0:T(8,128)(2,1)}, u32[]{:S(2)}) copy-start(bf16[768,2048]{1,0:T(8,128)(2,1)} %refs_1_.7) | copy-start | bytes 9437188
  100.2 9.0 %copy-start.2 = (f32[768,2048]{1,0:T(8,128)}, f32[768,2048]{1,0:T(8,128)S(1)}, u32[]{:S(2)}) copy-start(f32[768,2048]{1,0:T(8,128)S(1)} %shard_map.78.refs_4_) | copy-start | bytes 18874372
  118.5 13.6 %copy-start.14 = (f32[16,768]{1,0:T(8,128)}, f32[16,768]{1,0:T(8,128)S(1)}, u32[]{:S(2)}) copy-start(f32[16,768]{1,0:T(8,128)S(1)} %shard_map.80.__1_) | copy-start | bytes 147460
  118.5 12.9 %collective-permute-start.6 = (f32[16,768]{1,0:T(8,128)S(1)}, f32[16,768]{1,0:T(8,128)S(1)}, u32[]{:S(2)}, u32[]{:S(2)}) collective-permute-start(f32[16,768]{1,0:T(8,128)S(1)} %shard_map.80.__1_), channel_id=1, source_target_pairs={{0,8},{4,12},{8,0},{12,4},{1,9},{5,13},{9,1},{13,5},{2,10},{6,14},... | collective-permute-start | bytes 147464 | tf_op jit(solution)/shard_map/ppermute | solution.py:353
  132.1 49.9 %collective-permute-start.14 = (bf16[512,2048]{1,0:T(8,128)(2,1)}, bf16[512,2048]{1,0:T(8,128)(2,1)}, u32[]{:S(2)}, u32[]{:S(2)}) collective-permute-start(bf16[512,2048]{1,0:T(8,128)(2,1)} %bitcast.28), channel_id=1, source_target_pairs={{0,4},{4,0},{8,12},{12,8},{1,5},{5,1},{9,13},{13,9},{2,6},{6,2},{1... | collective-permute-start | bytes 6291464 | tf_op jit(solution)/shard_map/ppermute | solution.py:353
  132.2 1.6 copy-start.17
  132.2 49.8 %collective-permute-start.15 = (bf16[512,2048]{1,0:T(8,128)(2,1)}, bf16[512,2048]{1,0:T(8,128)(2,1)}, u32[]{:S(2)}, u32[]{:S(2)}) collective-permute-start(bf16[512,2048]{1,0:T(8,128)(2,1)} %shard_map.84.__1_), channel_id=1, source_target_pairs={{0,8},{4,12},{8,0},{12,4},{1,9},{5,13},{9,1},{13,5},{2,10},{6,14},... | collective-permute-start | bytes 6291464 | tf_op jit(solution)/shard_map/ppermute | solution.py:353
  133.8 3.9 %collective-permute-start.9 = (f32[16,768]{1,0:T(8,128)S(1)}, f32[16,768]{1,0:T(8,128)S(1)}, u32[]{:S(2)}, u32[]{:S(2)}) collective-permute-start(f32[16,768]{1,0:T(8,128)S(1)} %copy-done.17), channel_id=1, source_target_pairs={{0,1},{3,2},{4,5},{7,6},{8,9},{11,10},{12,13},{15,14},{16,17},{19,... | collective-permute-start | bytes 147464 | tf_op jit(solution)/shard_map/ppermute | solution.py:406
  137.7 56.9 %collective-permute-start.17 = (bf16[384,2048]{1,0:T(8,128)(2,1)}, bf16[384,2048]{1,0:T(8,128)(2,1)}, u32[]{:S(2)}, u32[]{:S(2)}) collective-permute-start(bf16[384,2048]{1,0:T(8,128)(2,1)} %shard_map.81.__1_.refs_0_), channel_id=1, source_target_pairs={{1,0},{2,3},{5,4},{6,7},{9,8},{10,11},{13,12},{14,15},{17,16},{18,... | collective-permute-start | bytes 4718600 | tf_op jit(solution)/shard_map/ppermute | solution.py:401
  145.6 1.7 copy-start.4
  147.2 1.9 copy-start.5
  147.2 16.8 %collective-permute-start.11 = (f32[16,768]{1,0:T(8,128)}, f32[16,768]{1,0:T(8,128)S(1)}, u32[]{:S(2)}, u32[]{:S(2)}) collective-permute-start(f32[16,768]{1,0:T(8,128)} %shard_map.86.refs_5_), channel_id=1, source_target_pairs={{1,2},{2,1},{5,6},{6,5},{9,10},{10,9},{13,14},{14,13},{17,18},{18,... | collective-permute-start | bytes 147464 | tf_op jit(solution)/shard_map/ppermute | solution.py:407
  149.1 0.8 copy-start.11
  161.3 2.7 %copy-start.1 = (f32[768,2048]{1,0:T(8,128)}, f32[768,2048]{1,0:T(8,128)S(1)}, u32[]{:S(2)}) copy-start(f32[768,2048]{1,0:T(8,128)S(1)} %shard_map.87.__1_.refs_6_) | copy-start | bytes 18874372
  164.6 14.1 %collective-permute-start.12 = (bf16[16,768]{1,0:T(8,128)(2,1)}, bf16[16,768]{1,0:T(8,128)(2,1)S(1)}, u32[]{:S(2)}, u32[]{:S(2)}) collective-permute-start(bf16[16,768]{1,0:T(8,128)(2,1)} %shard_map.88._), channel_id=1, source_target_pairs={{1,0},{2,3},{5,4},{6,7},{9,8},{10,11},{13,12},{14,15},{17,16},{18,... | collective-permute-start | bytes 73736 | tf_op jit(solution)/shard_map/ppermute | solution.py:410
  165.9 0.7 copy-start.12
  169.1 0.9 copy-start.7
  170.0 32.8 %collective-permute-start.16 = (bf16[192,2048]{1,0:T(8,128)(2,1)}, bf16[192,2048]{1,0:T(8,128)(2,1)S(1)}, u32[]{:S(2)}, u32[]{:S(2)}) collective-permute-start(bf16[192,2048]{1,0:T(8,128)(2,1)} %get-tuple-element.22.refs_1_), channel_id=1, source_target_pairs={{1,0},{2,3},{5,4},{6,7},{9,8},{10,11},{13,12},{14,15},{17,16},{18,... | collective-permute-start | bytes 2359304 | tf_op jit(solution)/shard_map/ppermute | solution.py:412
  175.5 3.2 %copy-start = (bf16[2048,2048]{1,0:T(8,128)(2,1)}, bf16[2048,2048]{1,0:T(8,128)(2,1)S(1)}, u32[]{:S(2)}) copy-start(bf16[2048,2048]{1,0:T(8,128)(2,1)S(1)} %shard_map.90.__1_.refs_2_) | copy-start | bytes 25165828
  178.8 2.5 %copy-start.13 = (bf16[16,768]{1,0:T(8,128)(2,1)S(1)}, bf16[16,768]{1,0:T(8,128)(2,1)}, u32[]{:S(2)}) copy-start(bf16[16,768]{1,0:T(8,128)(2,1)} %shard_map.88._) | copy-start | bytes 73732
  178.8 0.6 copy-start.18
  179.4 2.7 %copy-start.10 = (bf16[32,16,2048]{2,1,0:T(8,128)(2,1)S(1)}, bf16[32,16,2048]{2,1,0:T(8,128)(2,1)}, u32[]{:S(2)}) copy-start(bf16[32,16,2048]{2,1,0:T(8,128)(2,1)} %copy-done.9) | copy-start | bytes 6291460
  179.4 32.4 %collective-permute-start.13 = (bf16[192,2048]{1,0:T(8,128)(2,1)}, bf16[192,2048]{1,0:T(8,128)(2,1)}, u32[]{:S(2)}, u32[]{:S(2)}) collective-permute-start(bf16[192,2048]{1,0:T(8,128)(2,1)} %shard_map.92.refs_7_), channel_id=1, source_target_pairs={{1,0},{2,3},{5,4},{6,7},{9,8},{10,11},{13,12},{14,15},{17,16},{18,... | collective-permute-start | bytes 2359304 | tf_op jit(solution)/shard_map/ppermute | solution.py:415
  182.0 1.1 copy-start.8
  183.2 19.6 %slice-start = ((s8[8388608]{0:T(1024)(128)(4,1)}), s8[4194304]{0:T(1024)(128)(4,1)S(1)}, s32[]{:S(2)}) async-start(s8[8388608]{0:T(1024)(128)(4,1)} %bitcast.24), calls=%async_computation | async-start | bytes 8388608
  194.6 8.2 %slice-start.1 = ((s8[8388608]{0:T(1024)(128)(4,1)}), s8[4194304]{0:T(1024)(128)(4,1)S(1)}, s32[]{:S(2)}) async-start(s8[8388608]{0:T(1024)(128)(4,1)} %bitcast.24), calls=%async_computation.1 | async-start | bytes 8388608

commit v4 on v3

--- a/solution.py
+++ b/solution.py
@@ -146,7 +146,7 @@
 def add_products(order, terms, total=None, first=0, rows=None, whole=None, out=None, rounded=False, room=ROOM):
     rows = rows or terms[0][0][-1].shape[0]
     width = terms[0][1].shape[1]
-    tile = min(2 * TILE if rounded else TILE, width)
+    tile = min(4 * TILE if rounded and rows <= 192 else 2 * TILE if rounded else TILE, width)
     at = jnp.stack([jnp.asarray(t[2], jnp.int32) for t in terms])
     here = first // rows
     there = here if whole else 0

time: 218 us -> 217 us (level)
  Pallas kernels: 97.5 us -> 101 us
  starting transfers between devices: 28.6 us -> 25.1 us
    ppermute x7, starting transfers between devices: 8.56 us -> 5.12 us  [send(): return lax.ppermute(block, 'dp', [(i, i ^ k) for i in range(groups)])]
    pallas_call x11, Pallas kernels: 91.4 us -> 94.7 us  [call(): pl.pallas_call(body, grid_spec=pltpu.PrefetchScalarGridSpec(num_scalar_pr...]
  transfers between devices with their start and end apart: 18 -> 18, of which waited for: 6 -> 6; matrix products, arithmetic and copies ran while one was open for 6% -> 6% of each run, Pallas kernels for 43% -> 45%
where the time goes in v4:
time: 217 us; the launch traced here: 216 us
  Pallas kernels  101 us (47%)
  waiting for transfers between devices  59.3 us (27%)
  starting transfers between devices  25.1 us (12%)
  local copies, waits for them, and re-layouts  21 us (10%)
  other arithmetic  9.25 us (4%)
    pallas_call x11, Pallas kernels, call(): pl.pallas_call(body, grid_spec=pltpu.PrefetchScalarGridSpec(num_scalar_pr...  94.7 us
    ppermute x1, waiting for transfers between devices, body(): near = lax.ppermute(tokens, 'tensor', swap)  28.2 us
    unnamed x44, local copies, waits for them, and re-layouts  19.1 us
    ppermute x7, waiting for transfers between devices, send(): return lax.ppermute(block, 'dp', [(i, i ^ k) for i in range(groups)])  18.2 us
    pallas_call x2, Pallas kernels, cut(): pl.pallas_call(kernel, out_shape=[jax.ShapeDtypeStruct((size, x.shape[1])...  6.02 us
    ppermute x1, waiting for transfers between devices, body(): out_near = lax.ppermute(cross, 'tensor', outward)  5.93 us
    ppermute x1, waiting for transfers between devices, body(): out_far.append(lax.ppermute(order.hold(pieces[1]), 'tensor', outward))  5.21 us
    ppermute x7, starting transfers between devices, send(): return lax.ppermute(block, 'dp', [(i, i ^ k) for i in range(groups)])  5.12 us
  transfers between devices with their start and end apart: 18, of which 6 were waited for; matrix products, arithmetic and copies ran while one was open for 6% of the time, Pallas kernels for 45%

profile of v4, /device:TPU:0, one launch (start us, length us, event | category | flops | bytes accessed | tf_op | source)
XLA Modules:
  0.0 215.9 jit_solution(549298320256629378)
XLA Ops:
  0.0 2.3 %collective-permute-start.1 = (bf16[768,2048]{1,0:T(8,128)(2,1)}, bf16[768,2048]{1,0:T(8,128)(2,1)}, u32[]{:S(2)}, u32[]{:S(2)}) collective-permute-start(bf16[768,2048]{1,0:T(8,128)(2,1)} %refs_1_.7), channel_id=1, source_target_pairs={{1,2},{2,1},{5,6},{6,5},{9,10},{10,9},{13,14},{14,13},{17,18},{18,... | collective-permute-start | bytes 9437192 | tf_op jit(solution)/shard_map/ppermute | solution.py:388
  2.3 4.3 %collective-permute-start = (bf16[768,2048]{1,0:T(8,128)(2,1)}, bf16[768,2048]{1,0:T(8,128)(2,1)}, u32[]{:S(2)}, u32[]{:S(2)}) collective-permute-start(bf16[768,2048]{1,0:T(8,128)(2,1)} %refs_1_.7), channel_id=1, source_target_pairs={{0,1},{1,0},{2,3},{3,2},{4,5},{5,4},{6,7},{7,6},{8,9},{9,8},{10,11... | collective-permute-start | bytes 9437192 | tf_op jit(solution)/shard_map/ppermute | solution.py:387
  6.6 0.8 eq.100
  7.4 1.0 select_reduce_fusion
  8.4 0.8 copy.24
  9.2 0.1 reduce-window.4
  9.2 0.1 reduce
  9.4 0.7 fusion.3
  10.0 0.2 select_reduce_fusion.2
  10.4 0.1 select_reduce_fusion.1
  10.6 4.0 %pad_maximum_fusion = bf16[784,2048]{1,0:T(8,128)(2,1)} fusion(bf16[16,2048]{1,0:T(8,128)(2,1)S(1)} %convert_element_type.13, bf16[768,2048]{1,0:T(8,128)(2,1)} %refs_1_.7), kind=kLoop, calls=%fused_computation | loop fusion | flops 6422528 | bytes 6422528 | tf_op jit(solution)/shard_map/concatenate | solution.py:364
  14.6 1.5 collective-permute-start.4
  16.1 0.1 select_reduce_fusion.3
  16.3 0.1 select_reduce_fusion.4
  16.4 11.4 %shard_map.73 = (bf16[32,16,2048]{2,1,0:T(8,128)(2,1)}, bf16[32,16,2048]{2,1,0:T(8,128)(2,1)}, bf16[32,16,2048]{2,1,0:T(8,128)(2,1)S(1)}, bf16[32,16,2048]{2,1,0...) custom-call(s32[5,32]{1,0:T(8,128)S(1)} %pad_add_fusion.at_ref.refs_2_, ...), custom_call_target="tpu_custom_call" | custom-call | flops 1 | bytes 1 | tf_op jit(solution)/shard_map/pallas_call | solution.py:26
  27.8 1.3 copy-done.6
  29.2 1.3 copy-done.9
  30.5 1.4 copy-done.15
  31.8 1.4 copy-done.16
  33.2 0.5 collective-permute-start.5
  33.8 11.4 %shard_map.74.__1_.refs_2_ = f32[768,2048]{1,0:T(8,128)} custom-call(s32[1]{0:T(128)} %bitcast.at_ref, bf16[768,2048]{1,0:T(8,128)(2,1)} %refs_1_.7, bf16[8192,2048]{1,0:T(8,128)(2,1)} %refs_0_.5, bf16[32,16,2048]{2,1,0:T(8,128)(2,1)} %get-tuple-element.15.refs_2_), custom_call_target="tpu_custom_call" | custom-call | flops 1 | bytes 1 | tf_op jit(solution)/shard_map/pallas_call | solution.py:26
  45.2 1.3 collective-permute-start.10
  46.5 28.2 %collective-permute-done.x_ref.refs_0_ = bf16[768,2048]{1,0:T(8,128)(2,1)} collective-permute-done((bf16[768,2048]{1,0:T(8,128)(2,1)}, bf16[768,2048]{1,0:T(8,128)(2,1)}, u32[]{:S(2)}, u32[]{:S(2)}) %collective-permute-start) | collective-permute-done | bytes 3145760 | tf_op jit(solution)/shard_map/ppermute | solution.py:387
  74.8 3.6 %shard_map.76 = (bf16[384,2048]{1,0:T(8,128)(2,1)}, bf16[384,2048]{1,0:T(8,128)(2,1)}) custom-call(bf16[768,2048]{1,0:T(8,128)(2,1)} %collective-permute-done.x_ref.refs_0_, bf16[768,2048]{1,0:T(8,128)(2,1)} %shard_map.75._.refs_1_), custom_call_target="tpu_custom_call" | custom-call | flops 1 | bytes 1 | tf_op jit(solution)/shard_map/pallas_call | solution.py:60
  78.4 1.9 collective-permute-start.8
  80.3 7.0 %collective-permute-done.4.__0_ = bf16[784,2048]{1,0:T(8,128)(2,1)} collective-permute-done((bf16[784,2048]{1,0:T(8,128)(2,1)}, bf16[784,2048]{1,0:T(8,128)(2,1)}, u32[]{:S(2)}, u32[]{:S(2)}) %collective-permute-start.4) | collective-permute-done | bytes 3211296 | tf_op jit(solution)/shard_map/ppermute | solution.py:353
  87.3 1.8 collective-permute-start.2
  89.2 11.0 %shard_map.78.refs_4_ = f32[768,2048]{1,0:T(8,128)S(1)} custom-call(s32[1]{0:T(128)} %bitcast.4.at_ref, bf16[768,2048]{1,0:T(8,128)(2,1)} %collective-permute-done.x_ref.refs_0_, bf16[8192,2048]{1,0:T(8,128)(2,1)} %refs_0_.5, f32[768,2048]{1,0:T(8,128)} %shard_map.74.__1_.refs_2_, bf16[784,2048]{1,0:T(8,128)(2,1)} %shard_map.77.refs_3_.refs_1_), custom_call_target="tpu_custom_call" | custom-call | flops 1 | bytes 1 | tf_op jit(solution)/shard_map/pallas_call | solution.py:26
  100.2 9.2 %shard_map.79.refs_4_ = f32[16,768]{1,0:T(8,128)S(1)} custom-call(s32[5,32]{1,0:T(8,128)S(1)} %pad_add_fusion.at_ref.refs_2_, s32[1,768]{1,0:T(1,128)S(1)} %broadcast_in_dim.130.refs_0_, bf16[768,2048]{1,0:T(8,128)(2,1)S(1)} %copy-done.3, bf16[256,16,2048]{2,1,0:T(8,128)(2,1)} %refs_2_.3, bf16[512,2048]{1,0:T(8,128)(2,1)} %collective-permute-done.3.refs_3_, ...), custom_call_target="tpu_custom_call" | custom-call | flops 1 | bytes 1 | tf_op jit(solution)/shard_map/pallas_call | solution.py:26
  109.4 0.8 slice_bitcast_fusion
  110.2 8.6 %shard_map.80.__1_ = f32[16,768]{1,0:T(8,128)S(1)} custom-call(s32[5,32]{1,0:T(8,128)S(1)} %pad_add_fusion.at_ref.refs_2_, s32[1,768]{1,0:T(1,128)S(1)} %broadcast_in_dim.131.refs_0_, bf16[784,2048]{1,0:T(8,128)(2,1)} %shard_map.77.refs_3_.refs_1_, bf16[256,16,2048]{2,1,0:T(8,128)(2,1)} %refs_2_.3, bf16[512,2048]{1,0:T(8,128)(2,1)} %collective-permute-done.5.refs_3_, ...), custom_call_target="tpu_custom_call" | custom-call | flops 1 | bytes 1 | tf_op jit(solution)/shard_map/pallas_call | solution.py:26
  118.8 1.4 collective-permute-start.6
  120.3 11.2 %collective-permute-done.6 = f32[16,768]{1,0:T(8,128)S(1)} collective-permute-done((f32[16,768]{1,0:T(8,128)S(1)}, f32[16,768]{1,0:T(8,128)S(1)}, u32[]{:S(2)}, u32[]{:S(2)}) %collective-permute-start.6) | collective-permute-done | bytes 49184 | tf_op jit(solution)/shard_map/ppermute | solution.py:353
  131.4 0.6 add.38.__0_
  132.2 1.6 collective-permute-start.15
  133.8 2.2 %collective-permute-start.9 = (f32[16,768]{1,0:T(8,128)S(1)}, f32[16,768]{1,0:T(8,128)S(1)}, u32[]{:S(2)}, u32[]{:S(2)}) collective-permute-start(f32[16,768]{1,0:T(8,128)S(1)} %copy-done.17), channel_id=1, source_target_pairs={{0,1},{3,2},{4,5},{7,6},{8,9},{11,10},{12,13},{15,14},{16,17},{19,... | collective-permute-start | bytes 147464 | tf_op jit(solution)/shard_map/ppermute | solution.py:406
  136.0 1.7 collective-permute-done.9
  137.7 1.3 collective-permute-start.17
  139.0 0.6 add.39.__0_
  139.6 5.9 %collective-permute-done.10.__0_ = bf16[768,2048]{1,0:T(8,128)(2,1)S(1)} collective-permute-done((bf16[768,2048]{1,0:T(8,128)(2,1)}, bf16[768,2048]{1,0:T(8,128)(2,1)S(1)}, u32[]{:S(2)}, u32[]{:S(2)}) %collective-permute-start.10) | collective-permute-done | bytes 3145760 | tf_op jit(solution)/shard_map/ppermute | solution.py:391
  145.6 1.7 copy-done.4
  147.2 0.8 collective-permute-start.11
  148.0 1.1 copy-done.5
  149.1 0.8 copy-done.11
  149.9 11.4 %shard_map.87.__1_.refs_6_ = f32[768,2048]{1,0:T(8,128)S(1)} custom-call(s32[1]{0:T(128)} %bitcast.8.at_ref, bf16[384,2048]{1,0:T(8,128)(2,1)} %shard_map.81.__1_.refs_0_, bf16[384,2048]{1,0:T(8,128)(2,1)} %collective-permute-done.2.refs_1_.x_ref, bf16[768,2048]{1,0:T(8,128)(2,1)S(1)} %copy-done.5, bf16[8192,2048]{1,0:T(8,128)(2,1)} %refs_0_.5, ...), custom_call_target="tpu_custom_call" | custom-call | flops 1 | bytes 1 | tf_op jit(solution)/shard_map/pallas_call | solution.py:26
  161.3 2.7 %copy-done.1 = f32[768,2048]{1,0:T(8,128)} copy-done((f32[768,2048]{1,0:T(8,128)}, f32[768,2048]{1,0:T(8,128)S(1)}, u32[]{:S(2)}) %copy-start.1) | copy-done | bytes 6291480
  164.0 0.6 add_convert_fusion.__0_
  164.6 1.3 collective-permute-start.12
  165.9 0.7 copy-done.12
  166.7 2.4 %shard_map.89 = (bf16[192,2048]{1,0:T(8,128)(2,1)}, bf16[192,2048]{1,0:T(8,128)(2,1)S(1)}) custom-call(bf16[384,2048]{1,0:T(8,128)(2,1)} %collective-permute-done.2.refs_1_.x_ref, bf16[16,768]{1,0:T(8,128)(2,1)S(1)} %copy-done.12), custom_call_target="tpu_custom_call" | custom-call | flops 1 | bytes 1 | tf_op jit(solution)/shard_map/pallas_call | solution.py:60
  169.1 0.9 copy-done.7
  170.0 1.3 collective-permute-start.16
  171.2 4.3 %shard_map.90.__1_.refs_2_ = bf16[2048,2048]{1,0:T(8,128)(2,1)S(1)} custom-call(s32[1]{0:T(128)} %bitcast.9.at_ref, bf16[8192,2048]{1,0:T(8,128)(2,1)} %refs_0_.5, bf16[192,2048]{1,0:T(8,128)(2,1)} %get-tuple-element.22.refs_1_), custom_call_target="tpu_custom_call" | custom-call | flops 1 | bytes 1 | tf_op jit(solution)/shard_map/pallas_call | solution.py:26
  175.5 3.2 %copy-done = bf16[2048,2048]{1,0:T(8,128)(2,1)} copy-done((bf16[2048,2048]{1,0:T(8,128)(2,1)}, bf16[2048,2048]{1,0:T(8,128)(2,1)S(1)}, u32[]{:S(2)}) %copy-start) | copy-done | bytes 8388632
  178.8 0.6 copy-done.18
  179.4 1.6 collective-permute-start.13
  181.0 0.2 broadcast_in_dim.134.refs_1_
  181.3 0.7 broadcast_select_fusion.refs_0_
  182.1 1.1 copy-done.8
  183.2 11.4 %shard_map.93.refs_3_.refs_4_ = f32[768,2048]{1,0:T(8,128)S(1)} custom-call(s32[8]{0:T(128)S(1)} %stack.31.at_ref, bf16[16,768]{1,0:T(8,128)(2,1)S(1)} %broadcast_select_fusion.refs_0_, s32[768,1]{1,0:T(8,128)S(1)} %broadcast_in_dim.134.refs_1_, bf16[512,2048]{1,0:T(8,128)(2,1)S(1)} %bitcast.27, bf16[512,2048]{1,0:T(8,128)(2,1)} %collective-permute-done.14.refs_3_, ...), custom_call_target="tpu_custom_call" | custom-call | flops 1 | bytes 1 | tf_op jit(solution)/shard_map/pallas_call | solution.py:26
  194.6 8.2 %shard_map.94.refs_4_ = bf16[768,2048]{1,0:T(8,128)(2,1)} custom-call(s32[1]{0:T(128)} %constant.39.clone.1.at_ref, bf16[384,2048]{1,0:T(8,128)(2,1)} %collective-permute-done.17.refs_0_, bf16[768,2048]{1,0:T(8,128)(2,1)} %shard_map.75._.refs_1_, bf16[2048,2048]{1,0:T(8,128)(2,1)} %copy-done, f32[768,2048]{1,0:T(8,128)S(1)} %shard_map.93.refs_3_.refs_4_, ...), custom_call_target="tpu_custom_call" | custom-call | flops 1 | bytes 1 | tf_op jit(solution)/shard_map/pallas_call | solution.py:26
  202.8 3.8 %shard_map.95.refs_4_ = bf16[768,2048]{1,0:T(8,128)(2,1)} custom-call(s32[1]{0:T(128)} %constant.39.clone.1.at_ref, bf16[192,2048]{1,0:T(8,128)(2,1)S(1)} %collective-permute-done.16.refs_0_, bf16[768,2048]{1,0:T(8,128)(2,1)} %shard_map.75._.refs_1_, bf16[2048,2048]{1,0:T(8,128)(2,1)S(1)} %bitcast.25, ...), custom_call_target="tpu_custom_call", output_to_operand_aliasing={{}: (5, {})} | custom-call | flops 1 | bytes 1 | tf_op jit(solution)/shard_map/pallas_call | solution.py:26
  206.6 5.2 %collective-permute-done.13.refs_0_ = bf16[192,2048]{1,0:T(8,128)(2,1)} collective-permute-done((bf16[192,2048]{1,0:T(8,128)(2,1)}, bf16[192,2048]{1,0:T(8,128)(2,1)}, u32[]{:S(2)}, u32[]{:S(2)}) %collective-permute-start.13) | collective-permute-done | bytes 786464 | tf_op jit(solution)/shard_map/ppermute | solution.py:415
  211.8 4.1 %shard_map.96 = bf16[768,2048]{1,0:T(8,128)(2,1)} custom-call(s32[1]{0:T(128)} %constant.39.clone.1.at_ref, bf16[192,2048]{1,0:T(8,128)(2,1)} %collective-permute-done.13.refs_0_, bf16[768,2048]{1,0:T(8,128)(2,1)} %shard_map.75._.refs_1_, bf16[2048,2048]{1,0:T(8,128)(2,1)S(1)} %bitcast.25, ...), custom_call_target="tpu_custom_call", output_to_operand_aliasing={{}: (5, {})} | custom-call | flops 1 | bytes 1 | tf_op jit(solution)/shard_map/pallas_call | solution.py:26
  (75 shorter events, 0.7 us)
Async XLA Ops:
  0.0 45.2 %collective-permute-start.1 = (bf16[768,2048]{1,0:T(8,128)(2,1)}, bf16[768,2048]{1,0:T(8,128)(2,1)}, u32[]{:S(2)}, u32[]{:S(2)}) collective-permute-start(bf16[768,2048]{1,0:T(8,128)(2,1)} %refs_1_.7), channel_id=1, source_target_pairs={{1,2},{2,1},{5,6},{6,5},{9,10},{10,9},{13,14},{14,13},{17,18},{18,... | collective-permute-start | bytes 9437192 | tf_op jit(solution)/shard_map/ppermute | solution.py:388
  2.3 72.4 %collective-permute-start = (bf16[768,2048]{1,0:T(8,128)(2,1)}, bf16[768,2048]{1,0:T(8,128)(2,1)}, u32[]{:S(2)}, u32[]{:S(2)}) collective-permute-start(bf16[768,2048]{1,0:T(8,128)(2,1)} %refs_1_.7), channel_id=1, source_target_pairs={{0,1},{1,0},{2,3},{3,2},{4,5},{5,4},{6,7},{7,6},{8,9},{9,8},{10,11... | collective-permute-start | bytes 9437192 | tf_op jit(solution)/shard_map/ppermute | solution.py:387
  14.6 72.8 %collective-permute-start.4 = (bf16[784,2048]{1,0:T(8,128)(2,1)}, bf16[784,2048]{1,0:T(8,128)(2,1)}, u32[]{:S(2)}, u32[]{:S(2)}) collective-permute-start(bf16[784,2048]{1,0:T(8,128)(2,1)} %pad_maximum_fusion), channel_id=1, source_target_pairs={{0,8},{4,12},{8,0},{12,4},{1,9},{5,13},{9,1},{13,5},{2,10},{6,14},... | collective-permute-start | bytes 9633800 | tf_op jit(solution)/shard_map/ppermute | solution.py:353
  27.8 1.3 copy-start.6
  29.2 1.3 copy-start.9
  30.5 1.4 copy-start.15
  31.8 1.4 copy-start.16
  33.2 45.2 %collective-permute-start.3 = (bf16[512,2048]{1,0:T(8,128)(2,1)}, bf16[512,2048]{1,0:T(8,128)(2,1)}, u32[]{:S(2)}, u32[]{:S(2)}) collective-permute-start(bf16[512,2048]{1,0:T(8,128)(2,1)} %bitcast.3), channel_id=1, source_target_pairs={{0,4},{4,0},{8,12},{12,8},{1,5},{5,1},{9,13},{13,9},{2,6},{6,2},{1... | collective-permute-start | bytes 6291464 | tf_op jit(solution)/shard_map/ppermute | solution.py:353
  33.2 77.0 %collective-permute-start.5 = (bf16[512,2048]{1,0:T(8,128)(2,1)}, bf16[512,2048]{1,0:T(8,128)(2,1)}, u32[]{:S(2)}, u32[]{:S(2)}) collective-permute-start(bf16[512,2048]{1,0:T(8,128)(2,1)} %bitcast.5), channel_id=1, source_target_pairs={{0,4},{4,0},{8,12},{12,8},{1,5},{5,1},{9,13},{13,9},{2,6},{6,2},{1... | collective-permute-start | bytes 6291464 | tf_op jit(solution)/shard_map/ppermute | solution.py:353
  45.2 100.4 %collective-permute-start.10 = (bf16[768,2048]{1,0:T(8,128)(2,1)}, bf16[768,2048]{1,0:T(8,128)(2,1)S(1)}, u32[]{:S(2)}, u32[]{:S(2)}) collective-permute-start(bf16[768,2048]{1,0:T(8,128)(2,1)} %shard_map.75._.refs_1_), channel_id=1, source_target_pairs={{1,0},{2,3},{5,4},{6,7},{9,8},{10,11},{13,12},{14,15},{17,16},{18,... | collective-permute-start | bytes 9437192 | tf_op jit(solution)/shard_map/ppermute | solution.py:391
  74.7 57.4 %collective-permute-start.7 = (bf16[512,2048]{1,0:T(8,128)(2,1)}, bf16[512,2048]{1,0:T(8,128)(2,1)}, u32[]{:S(2)}, u32[]{:S(2)}) collective-permute-start(bf16[512,2048]{1,0:T(8,128)(2,1)} %bitcast.29), channel_id=1, source_target_pairs={{0,12},{4,8},{8,4},{12,0},{1,13},{5,9},{9,5},{13,1},{2,14},{6,10},... | collective-permute-start | bytes 6291464 | tf_op jit(solution)/shard_map/ppermute | solution.py:353
  78.4 53.7 %collective-permute-start.8 = (bf16[384,2048]{1,0:T(8,128)(2,1)}, bf16[384,2048]{1,0:T(8,128)(2,1)}, u32[]{:S(2)}, u32[]{:S(2)}) collective-permute-start(bf16[384,2048]{1,0:T(8,128)(2,1)} %get-tuple-element.17.__1_), channel_id=1, source_target_pairs={{1,2},{2,1},{5,6},{6,5},{9,10},{10,9},{13,14},{14,13},{17,18},{18,... | collective-permute-start | bytes 4718600 | tf_op jit(solution)/shard_map/ppermute | solution.py:393
  87.3 60.7 %collective-permute-start.2 = (bf16[384,2048]{1,0:T(8,128)(2,1)}, bf16[384,2048]{1,0:T(8,128)(2,1)}, u32[]{:S(2)}, u32[]{:S(2)}) collective-permute-start(bf16[384,2048]{1,0:T(8,128)(2,1)} %get-tuple-element.16), channel_id=1, source_target_pairs={{1,2},{2,1},{5,6},{6,5},{9,10},{10,9},{13,14},{14,13},{17,18},{18,... | collective-permute-start | bytes 4718600 | tf_op jit(solution)/shard_map/ppermute | solution.py:393
  89.2 11.0 %copy-start.3 = (bf16[768,2048]{1,0:T(8,128)(2,1)S(1)}, bf16[768,2048]{1,0:T(8,128)(2,1)}, u32[]{:S(2)}) copy-start(bf16[768,2048]{1,0:T(8,128)(2,1)} %refs_1_.7) | copy-start | bytes 9437188
  100.2 9.2 %copy-start.2 = (f32[768,2048]{1,0:T(8,128)}, f32[768,2048]{1,0:T(8,128)S(1)}, u32[]{:S(2)}) copy-start(f32[768,2048]{1,0:T(8,128)S(1)} %shard_map.78.refs_4_) | copy-start | bytes 18874372
  118.8 13.2 %copy-start.14 = (f32[16,768]{1,0:T(8,128)}, f32[16,768]{1,0:T(8,128)S(1)}, u32[]{:S(2)}) copy-start(f32[16,768]{1,0:T(8,128)S(1)} %shard_map.80.__1_) | copy-start | bytes 147460
  118.8 12.6 %collective-permute-start.6 = (f32[16,768]{1,0:T(8,128)S(1)}, f32[16,768]{1,0:T(8,128)S(1)}, u32[]{:S(2)}, u32[]{:S(2)}) collective-permute-start(f32[16,768]{1,0:T(8,128)S(1)} %shard_map.80.__1_), channel_id=1, source_target_pairs={{0,8},{4,12},{8,0},{12,4},{1,9},{5,13},{9,1},{13,5},{2,10},{6,14},... | collective-permute-start | bytes 147464 | tf_op jit(solution)/shard_map/ppermute | solution.py:353
  132.1 49.9 %collective-permute-start.14 = (bf16[512,2048]{1,0:T(8,128)(2,1)}, bf16[512,2048]{1,0:T(8,128)(2,1)}, u32[]{:S(2)}, u32[]{:S(2)}) collective-permute-start(bf16[512,2048]{1,0:T(8,128)(2,1)} %bitcast.28), channel_id=1, source_target_pairs={{0,4},{4,0},{8,12},{12,8},{1,5},{5,1},{9,13},{13,9},{2,6},{6,2},{1... | collective-permute-start | bytes 6291464 | tf_op jit(solution)/shard_map/ppermute | solution.py:353
  132.2 1.6 copy-start.17
  132.2 49.8 %collective-permute-start.15 = (bf16[512,2048]{1,0:T(8,128)(2,1)}, bf16[512,2048]{1,0:T(8,128)(2,1)}, u32[]{:S(2)}, u32[]{:S(2)}) collective-permute-start(bf16[512,2048]{1,0:T(8,128)(2,1)} %shard_map.84.__1_), channel_id=1, source_target_pairs={{0,8},{4,12},{8,0},{12,4},{1,9},{5,13},{9,1},{13,5},{2,10},{6,14},... | collective-permute-start | bytes 6291464 | tf_op jit(solution)/shard_map/ppermute | solution.py:353
  133.8 3.9 %collective-permute-start.9 = (f32[16,768]{1,0:T(8,128)S(1)}, f32[16,768]{1,0:T(8,128)S(1)}, u32[]{:S(2)}, u32[]{:S(2)}) collective-permute-start(f32[16,768]{1,0:T(8,128)S(1)} %copy-done.17), channel_id=1, source_target_pairs={{0,1},{3,2},{4,5},{7,6},{8,9},{11,10},{12,13},{15,14},{16,17},{19,... | collective-permute-start | bytes 147464 | tf_op jit(solution)/shard_map/ppermute | solution.py:406
  137.7 56.9 %collective-permute-start.17 = (bf16[384,2048]{1,0:T(8,128)(2,1)}, bf16[384,2048]{1,0:T(8,128)(2,1)}, u32[]{:S(2)}, u32[]{:S(2)}) collective-permute-start(bf16[384,2048]{1,0:T(8,128)(2,1)} %shard_map.81.__1_.refs_0_), channel_id=1, source_target_pairs={{1,0},{2,3},{5,4},{6,7},{9,8},{10,11},{13,12},{14,15},{17,16},{18,... | collective-permute-start | bytes 4718600 | tf_op jit(solution)/shard_map/ppermute | solution.py:401
  145.6 1.7 copy-start.4
  147.2 1.9 copy-start.5
  147.2 16.8 %collective-permute-start.11 = (f32[16,768]{1,0:T(8,128)}, f32[16,768]{1,0:T(8,128)S(1)}, u32[]{:S(2)}, u32[]{:S(2)}) collective-permute-start(f32[16,768]{1,0:T(8,128)} %shard_map.86.refs_5_), channel_id=1, source_target_pairs={{1,2},{2,1},{5,6},{6,5},{9,10},{10,9},{13,14},{14,13},{17,18},{18,... | collective-permute-start | bytes 147464 | tf_op jit(solution)/shard_map/ppermute | solution.py:407
  149.1 0.8 copy-start.11
  161.3 2.7 %copy-start.1 = (f32[768,2048]{1,0:T(8,128)}, f32[768,2048]{1,0:T(8,128)S(1)}, u32[]{:S(2)}) copy-start(f32[768,2048]{1,0:T(8,128)S(1)} %shard_map.87.__1_.refs_6_) | copy-start | bytes 18874372
  164.6 14.1 %collective-permute-start.12 = (bf16[16,768]{1,0:T(8,128)(2,1)}, bf16[16,768]{1,0:T(8,128)(2,1)S(1)}, u32[]{:S(2)}, u32[]{:S(2)}) collective-permute-start(bf16[16,768]{1,0:T(8,128)(2,1)} %shard_map.88._), channel_id=1, source_target_pairs={{1,0},{2,3},{5,4},{6,7},{9,8},{10,11},{13,12},{14,15},{17,16},{18,... | collective-permute-start | bytes 73736 | tf_op jit(solution)/shard_map/ppermute | solution.py:410
  165.9 0.7 copy-start.12
  169.1 0.9 copy-start.7
  170.0 32.8 %collective-permute-start.16 = (bf16[192,2048]{1,0:T(8,128)(2,1)}, bf16[192,2048]{1,0:T(8,128)(2,1)S(1)}, u32[]{:S(2)}, u32[]{:S(2)}) collective-permute-start(bf16[192,2048]{1,0:T(8,128)(2,1)} %get-tuple-element.22.refs_1_), channel_id=1, source_target_pairs={{1,0},{2,3},{5,4},{6,7},{9,8},{10,11},{13,12},{14,15},{17,16},{18,... | collective-permute-start | bytes 2359304 | tf_op jit(solution)/shard_map/ppermute | solution.py:412
  175.5 3.2 %copy-start = (bf16[2048,2048]{1,0:T(8,128)(2,1)}, bf16[2048,2048]{1,0:T(8,128)(2,1)S(1)}, u32[]{:S(2)}) copy-start(bf16[2048,2048]{1,0:T(8,128)(2,1)S(1)} %shard_map.90.__1_.refs_2_) | copy-start | bytes 25165828
  178.8 2.5 %copy-start.13 = (bf16[16,768]{1,0:T(8,128)(2,1)S(1)}, bf16[16,768]{1,0:T(8,128)(2,1)}, u32[]{:S(2)}) copy-start(bf16[16,768]{1,0:T(8,128)(2,1)} %shard_map.88._) | copy-start | bytes 73732
  178.8 0.6 copy-start.18
  179.4 2.7 %copy-start.10 = (bf16[32,16,2048]{2,1,0:T(8,128)(2,1)S(1)}, bf16[32,16,2048]{2,1,0:T(8,128)(2,1)}, u32[]{:S(2)}) copy-start(bf16[32,16,2048]{2,1,0:T(8,128)(2,1)} %copy-done.9) | copy-start | bytes 6291460
  179.4 32.4 %collective-permute-start.13 = (bf16[192,2048]{1,0:T(8,128)(2,1)}, bf16[192,2048]{1,0:T(8,128)(2,1)}, u32[]{:S(2)}, u32[]{:S(2)}) collective-permute-start(bf16[192,2048]{1,0:T(8,128)(2,1)} %shard_map.92.refs_7_), channel_id=1, source_target_pairs={{1,0},{2,3},{5,4},{6,7},{9,8},{10,11},{13,12},{14,15},{17,16},{18,... | collective-permute-start | bytes 2359304 | tf_op jit(solution)/shard_map/ppermute | solution.py:415
  182.0 1.1 copy-start.8
  183.2 19.6 %slice-start = ((s8[8388608]{0:T(1024)(128)(4,1)}), s8[4194304]{0:T(1024)(128)(4,1)S(1)}, s32[]{:S(2)}) async-start(s8[8388608]{0:T(1024)(128)(4,1)} %bitcast.24), calls=%async_computation | async-start | bytes 8388608
  194.6 8.2 %slice-start.1 = ((s8[8388608]{0:T(1024)(128)(4,1)}), s8[4194304]{0:T(1024)(128)(4,1)S(1)}, s32[]{:S(2)}) async-start(s8[8388608]{0:T(1024)(128)(4,1)} %bitcast.24), calls=%async_computation.1 | async-start | bytes 8388608

commit v5 on v4

--- a/solution.py
+++ b/solution.py
@@ -370,6 +370,8 @@
     line = lax.axis_index("tensor")
     shrinks, expands = stored_shrink_factors, stored_expand_factors
     across = send(noted, 2)
+    if lanes == 4:
+        own = add_products(order, [([tokens], weight, line)], room=62 * 1024 * 1024)
     plan = [[p] for p in [(0, 1), (0, 3), (1, 1), (1, 0), (1, 2), (1, 3)]]
     blocks = fetch(order, lists, [shrinks, expands], plan)
     mates = [send(x, 1) for x in blocks[:3]]
@@ -386,7 +388,6 @@
         step = rows // 4
         near = lax.ppermute(tokens, "tensor", swap)
         cross = lax.ppermute(tokens, "tensor", middle)
-        own = add_products(order, [([tokens], weight, line)], room=62 * 1024 * 1024)
         cross = order.hold(cross)
         out_near = lax.ppermute(cross, "tensor", outward)
         cuts = order.cut(near, [2 * step] * 2)

time: 217 us -> 217 us (level)
    unnamed x44 -> x46, local copies, waits for them, and re-layouts: 19.1 us -> 19.2 us
where the time goes in v5:
time: 217 us; the launch traced here: 216 us
  Pallas kernels  101 us (47%)
  waiting for transfers between devices  58.6 us (27%)
  starting transfers between devices  25.3 us (12%)
  local copies, waits for them, and re-layouts  21 us (10%)
  other arithmetic  9.85 us (5%)
    pallas_call x11, Pallas kernels, call(): pl.pallas_call(body, grid_spec=pltpu.PrefetchScalarGridSpec(num_scalar_pr...  94.7 us
    ppermute x1, waiting for transfers between devices, body(): near = lax.ppermute(tokens, 'tensor', swap)  27.3 us
    unnamed x46, local copies, waits for them, and re-layouts  19.2 us
    ppermute x7, waiting for transfers between devices, send(): return lax.ppermute(block, 'dp', [(i, i ^ k) for i in range(groups)])  18.4 us
    pallas_call x2, Pallas kernels, cut(): pl.pallas_call(kernel, out_shape=[jax.ShapeDtypeStruct((size, x.shape[1])...  6.01 us
    ppermute x1, waiting for transfers between devices, body(): out_near = lax.ppermute(cross, 'tensor', outward)  5.93 us
    ppermute x7, starting transfers between devices, send(): return lax.ppermute(block, 'dp', [(i, i ^ k) for i in range(groups)])  5.25 us
    ppermute x1, waiting for transfers between devices, body(): out_far.append(lax.ppermute(order.hold(pieces[1]), 'tensor', outward))  5.21 us
  transfers between devices with their start and end apart: 18, of which 6 were waited for; matrix products, arithmetic and copies ran while one was open for 6% of the time, Pallas kernels for 45%

profile of v5, /device:TPU:0, one launch (start us, length us, event | category | flops | bytes accessed | tf_op | source)
XLA Modules:
  0.0 215.9 jit_solution(6668001857051836025)
XLA Ops:
  0.0 2.3 %collective-permute-start.1 = (bf16[768,2048]{1,0:T(8,128)(2,1)}, bf16[768,2048]{1,0:T(8,128)(2,1)}, u32[]{:S(2)}, u32[]{:S(2)}) collective-permute-start(bf16[768,2048]{1,0:T(8,128)(2,1)} %refs_1_.7), channel_id=1, source_target_pairs={{1,2},{2,1},{5,6},{6,5},{9,10},{10,9},{13,14},{14,13},{17,18},{18,... | collective-permute-start | bytes 9437192 | tf_op jit(solution)/shard_map/ppermute | solution.py:390
  2.3 4.3 %collective-permute-start = (bf16[768,2048]{1,0:T(8,128)(2,1)}, bf16[768,2048]{1,0:T(8,128)(2,1)}, u32[]{:S(2)}, u32[]{:S(2)}) collective-permute-start(bf16[768,2048]{1,0:T(8,128)(2,1)} %refs_1_.7), channel_id=1, source_target_pairs={{0,1},{1,0},{2,3},{3,2},{4,5},{5,4},{6,7},{7,6},{8,9},{9,8},{10,11... | collective-permute-start | bytes 9437192 | tf_op jit(solution)/shard_map/ppermute | solution.py:389
  6.6 0.8 eq.100
  7.4 1.0 select_reduce_fusion
  8.4 0.8 copy.24
  9.2 0.1 reduce-window.4
  9.2 0.1 reduce
  9.4 0.7 fusion.3
  10.0 0.2 select_reduce_fusion.2
  10.4 0.1 select_reduce_fusion.1
  10.6 4.0 %pad_maximum_fusion = bf16[784,2048]{1,0:T(8,128)(2,1)} fusion(bf16[16,2048]{1,0:T(8,128)(2,1)S(1)} %convert_element_type.13, bf16[768,2048]{1,0:T(8,128)(2,1)} %refs_1_.7), kind=kLoop, calls=%fused_computation | loop fusion | flops 6422528 | bytes 6422528 | tf_op jit(solution)/shard_map/concatenate | solution.py:364
  14.6 1.5 collective-permute-start.4
  16.1 0.1 select_reduce_fusion.3
  16.4 0.6 pad_add_fusion.refs_2_.at_ref
  17.0 11.4 %shard_map.73.refs_2_ = f32[768,2048]{1,0:T(8,128)} custom-call(s32[1]{0:T(128)} %bitcast.at_ref, bf16[768,2048]{1,0:T(8,128)(2,1)} %refs_1_.7, bf16[8192,2048]{1,0:T(8,128)(2,1)} %refs_0_.5, s32[5,32]{1,0:T(8,128)} %pad_add_fusion.refs_2_.at_ref), custom_call_target="tpu_custom_call" | custom-call | flops 1 | bytes 1 | tf_op jit(solution)/shard_map/pallas_call | solution.py:26
  28.4 11.8 %shard_map.74 = (bf16[32,16,2048]{2,1,0:T(8,128)(2,1)}, bf16[32,16,2048]{2,1,0:T(8,128)(2,1)}, bf16[32,16,2048]{2,1,0:T(8,128)(2,1)S(1)}, bf16[32,16,2048]{2,1,0...) custom-call(s32[5,32]{1,0:T(8,128)S(1)} %copy-done.15, ...), custom_call_target="tpu_custom_call" | custom-call | flops 1 | bytes 1 | tf_op jit(solution)/shard_map/pallas_call | solution.py:26
  40.2 1.3 copy-done.6
  41.6 1.3 copy-done.9
  42.9 1.4 copy-done.16
  44.2 1.4 copy-done.17
  45.6 0.5 collective-permute-start.5
  46.1 1.3 collective-permute-start.10
  47.4 27.3 %collective-permute-done.x_ref.refs_0_ = bf16[768,2048]{1,0:T(8,128)(2,1)} collective-permute-done((bf16[768,2048]{1,0:T(8,128)(2,1)}, bf16[768,2048]{1,0:T(8,128)(2,1)}, u32[]{:S(2)}, u32[]{:S(2)}) %collective-permute-start) | collective-permute-done | bytes 3145760 | tf_op jit(solution)/shard_map/ppermute | solution.py:389
  74.8 3.6 %shard_map.76 = (bf16[384,2048]{1,0:T(8,128)(2,1)}, bf16[384,2048]{1,0:T(8,128)(2,1)}) custom-call(bf16[768,2048]{1,0:T(8,128)(2,1)} %collective-permute-done.x_ref.refs_0_, bf16[768,2048]{1,0:T(8,128)(2,1)} %shard_map.75._.refs_1_), custom_call_target="tpu_custom_call" | custom-call | flops 1 | bytes 1 | tf_op jit(solution)/shard_map/pallas_call | solution.py:60
  78.4 1.9 collective-permute-start.8
  80.3 7.0 %collective-permute-done.4.__0_ = bf16[784,2048]{1,0:T(8,128)(2,1)} collective-permute-done((bf16[784,2048]{1,0:T(8,128)(2,1)}, bf16[784,2048]{1,0:T(8,128)(2,1)}, u32[]{:S(2)}, u32[]{:S(2)}) %collective-permute-start.4) | collective-permute-done | bytes 3211296 | tf_op jit(solution)/shard_map/ppermute | solution.py:353
  87.3 1.8 collective-permute-start.2
  89.2 11.0 %shard_map.78.refs_4_ = f32[768,2048]{1,0:T(8,128)S(1)} custom-call(s32[1]{0:T(128)} %bitcast.4.at_ref, bf16[768,2048]{1,0:T(8,128)(2,1)} %collective-permute-done.x_ref.refs_0_, bf16[8192,2048]{1,0:T(8,128)(2,1)} %refs_0_.5, f32[768,2048]{1,0:T(8,128)} %shard_map.73.refs_2_, bf16[784,2048]{1,0:T(8,128)(2,1)} %shard_map.77.refs_3_.refs_1_), custom_call_target="tpu_custom_call" | custom-call | flops 1 | bytes 1 | tf_op jit(solution)/shard_map/pallas_call | solution.py:26
  100.2 9.0 %shard_map.79.refs_4_ = f32[16,768]{1,0:T(8,128)S(1)} custom-call(s32[5,32]{1,0:T(8,128)S(1)} %copy-done.15, s32[1,768]{1,0:T(1,128)S(1)} %broadcast_in_dim.130.refs_0_, bf16[768,2048]{1,0:T(8,128)(2,1)S(1)} %copy-done.3, bf16[256,16,2048]{2,1,0:T(8,128)(2,1)} %refs_2_.3, bf16[512,2048]{1,0:T(8,128)(2,1)} %collective-permute-done.3.refs_3_, ...), custom_call_target="tpu_custom_call" | custom-call | flops 1 | bytes 1 | tf_op jit(solution)/shard_map/pallas_call | solution.py:26
  109.2 0.8 slice_bitcast_fusion
  110.1 8.4 %shard_map.80.__1_ = f32[16,768]{1,0:T(8,128)S(1)} custom-call(s32[5,32]{1,0:T(8,128)S(1)} %copy-done.15, s32[1,768]{1,0:T(1,128)S(1)} %broadcast_in_dim.131.refs_0_, bf16[784,2048]{1,0:T(8,128)(2,1)} %shard_map.77.refs_3_.refs_1_, bf16[256,16,2048]{2,1,0:T(8,128)(2,1)} %refs_2_.3, bf16[512,2048]{1,0:T(8,128)(2,1)} %collective-permute-done.5.refs_3_, ...), custom_call_target="tpu_custom_call" | custom-call | flops 1 | bytes 1 | tf_op jit(solution)/shard_map/pallas_call | solution.py:26
  118.5 1.6 collective-permute-start.6
  120.1 11.4 %collective-permute-done.6 = f32[16,768]{1,0:T(8,128)S(1)} collective-permute-done((f32[16,768]{1,0:T(8,128)S(1)}, f32[16,768]{1,0:T(8,128)S(1)}, u32[]{:S(2)}, u32[]{:S(2)}) %collective-permute-start.6) | collective-permute-done | bytes 49184 | tf_op jit(solution)/shard_map/ppermute | solution.py:353
  131.5 0.6 add.38.__0_
  132.2 1.6 collective-permute-start.15
  133.8 2.2 %collective-permute-start.9 = (f32[16,768]{1,0:T(8,128)S(1)}, f32[16,768]{1,0:T(8,128)S(1)}, u32[]{:S(2)}, u32[]{:S(2)}) collective-permute-start(f32[16,768]{1,0:T(8,128)S(1)} %copy-done.18), channel_id=1, source_target_pairs={{0,1},{3,2},{4,5},{7,6},{8,9},{11,10},{12,13},{15,14},{16,17},{19,... | collective-permute-start | bytes 147464 | tf_op jit(solution)/shard_map/ppermute | solution.py:407
  136.0 1.7 collective-permute-done.9
  137.7 1.3 collective-permute-start.17
  139.0 0.6 add.39.__0_
  139.6 5.9 %collective-permute-done.10.__0_ = bf16[768,2048]{1,0:T(8,128)(2,1)S(1)} collective-permute-done((bf16[768,2048]{1,0:T(8,128)(2,1)}, bf16[768,2048]{1,0:T(8,128)(2,1)S(1)}, u32[]{:S(2)}, u32[]{:S(2)}) %collective-permute-start.10) | collective-permute-done | bytes 3145760 | tf_op jit(solution)/shard_map/ppermute | solution.py:392
  145.6 1.7 copy-done.4
  147.2 0.8 collective-permute-start.11
  148.0 1.1 copy-done.5
  149.1 0.8 copy-done.11
  149.9 11.4 %shard_map.87.__1_.refs_6_ = f32[768,2048]{1,0:T(8,128)S(1)} custom-call(s32[1]{0:T(128)} %bitcast.8.at_ref, bf16[384,2048]{1,0:T(8,128)(2,1)} %shard_map.81.__1_.refs_0_, bf16[384,2048]{1,0:T(8,128)(2,1)} %collective-permute-done.2.refs_1_.x_ref, bf16[768,2048]{1,0:T(8,128)(2,1)S(1)} %copy-done.5, bf16[8192,2048]{1,0:T(8,128)(2,1)} %refs_0_.5, ...), custom_call_target="tpu_custom_call" | custom-call | flops 1 | bytes 1 | tf_op jit(solution)/shard_map/pallas_call | solution.py:26
  161.3 2.7 %copy-done.1 = f32[768,2048]{1,0:T(8,128)} copy-done((f32[768,2048]{1,0:T(8,128)}, f32[768,2048]{1,0:T(8,128)S(1)}, u32[]{:S(2)}) %copy-start.1) | copy-done | bytes 6291480
  164.0 0.6 add_convert_fusion.__0_
  164.6 1.3 collective-permute-start.12
  165.9 0.7 copy-done.12
  166.7 2.4 %shard_map.89 = (bf16[192,2048]{1,0:T(8,128)(2,1)}, bf16[192,2048]{1,0:T(8,128)(2,1)S(1)}) custom-call(bf16[384,2048]{1,0:T(8,128)(2,1)} %collective-permute-done.2.refs_1_.x_ref, bf16[16,768]{1,0:T(8,128)(2,1)S(1)} %copy-done.12), custom_call_target="tpu_custom_call" | custom-call | flops 1 | bytes 1 | tf_op jit(solution)/shard_map/pallas_call | solution.py:60
  169.0 0.9 copy-done.7
  169.9 1.3 collective-permute-start.16
  171.2 4.3 %shard_map.90.__1_.refs_2_ = bf16[2048,2048]{1,0:T(8,128)(2,1)S(1)} custom-call(s32[1]{0:T(128)} %bitcast.9.at_ref, bf16[8192,2048]{1,0:T(8,128)(2,1)} %refs_0_.5, bf16[192,2048]{1,0:T(8,128)(2,1)} %get-tuple-element.22.refs_1_), custom_call_target="tpu_custom_call" | custom-call | flops 1 | bytes 1 | tf_op jit(solution)/shard_map/pallas_call | solution.py:26
  175.5 3.2 %copy-done = bf16[2048,2048]{1,0:T(8,128)(2,1)} copy-done((bf16[2048,2048]{1,0:T(8,128)(2,1)}, bf16[2048,2048]{1,0:T(8,128)(2,1)S(1)}, u32[]{:S(2)}) %copy-start) | copy-done | bytes 8388632
  178.8 0.6 copy-done.19
  179.4 1.6 collective-permute-start.13
  181.0 0.2 broadcast_in_dim.134.refs_1_
  181.3 0.7 broadcast_select_fusion.refs_0_
  182.1 1.1 copy-done.8
  183.2 11.4 %shard_map.93.refs_3_.refs_4_ = f32[768,2048]{1,0:T(8,128)S(1)} custom-call(s32[8]{0:T(128)S(1)} %stack.31.at_ref, bf16[16,768]{1,0:T(8,128)(2,1)S(1)} %broadcast_select_fusion.refs_0_, s32[768,1]{1,0:T(8,128)S(1)} %broadcast_in_dim.134.refs_1_, bf16[512,2048]{1,0:T(8,128)(2,1)S(1)} %bitcast.27, bf16[512,2048]{1,0:T(8,128)(2,1)} %collective-permute-done.14.refs_3_, ...), custom_call_target="tpu_custom_call" | custom-call | flops 1 | bytes 1 | tf_op jit(solution)/shard_map/pallas_call | solution.py:26
  194.6 8.2 %shard_map.94.refs_4_ = bf16[768,2048]{1,0:T(8,128)(2,1)} custom-call(s32[1]{0:T(128)} %constant.39.clone.1.at_ref, bf16[384,2048]{1,0:T(8,128)(2,1)} %collective-permute-done.17.refs_0_, bf16[768,2048]{1,0:T(8,128)(2,1)} %shard_map.75._.refs_1_, bf16[2048,2048]{1,0:T(8,128)(2,1)} %copy-done, f32[768,2048]{1,0:T(8,128)S(1)} %shard_map.93.refs_3_.refs_4_, ...), custom_call_target="tpu_custom_call" | custom-call | flops 1 | bytes 1 | tf_op jit(solution)/shard_map/pallas_call | solution.py:26
  202.8 3.8 %shard_map.95.refs_4_ = bf16[768,2048]{1,0:T(8,128)(2,1)} custom-call(s32[1]{0:T(128)} %constant.39.clone.1.at_ref, bf16[192,2048]{1,0:T(8,128)(2,1)S(1)} %collective-permute-done.16.refs_0_, bf16[768,2048]{1,0:T(8,128)(2,1)} %shard_map.75._.refs_1_, bf16[2048,2048]{1,0:T(8,128)(2,1)S(1)} %bitcast.25, ...), custom_call_target="tpu_custom_call", output_to_operand_aliasing={{}: (5, {})} | custom-call | flops 1 | bytes 1 | tf_op jit(solution)/shard_map/pallas_call | solution.py:26
  206.6 5.2 %collective-permute-done.13.refs_0_ = bf16[192,2048]{1,0:T(8,128)(2,1)} collective-permute-done((bf16[192,2048]{1,0:T(8,128)(2,1)}, bf16[192,2048]{1,0:T(8,128)(2,1)}, u32[]{:S(2)}, u32[]{:S(2)}) %collective-permute-start.13) | collective-permute-done | bytes 786464 | tf_op jit(solution)/shard_map/ppermute | solution.py:416
  211.8 4.1 %shard_map.96 = bf16[768,2048]{1,0:T(8,128)(2,1)} custom-call(s32[1]{0:T(128)} %constant.39.clone.1.at_ref, bf16[192,2048]{1,0:T(8,128)(2,1)} %collective-permute-done.13.refs_0_, bf16[768,2048]{1,0:T(8,128)(2,1)} %shard_map.75._.refs_1_, bf16[2048,2048]{1,0:T(8,128)(2,1)S(1)} %bitcast.25, ...), custom_call_target="tpu_custom_call", output_to_operand_aliasing={{}: (5, {})} | custom-call | flops 1 | bytes 1 | tf_op jit(solution)/shard_map/pallas_call | solution.py:26
  (77 shorter events, 0.8 us)
Async XLA Ops:
  0.0 46.1 %collective-permute-start.1 = (bf16[768,2048]{1,0:T(8,128)(2,1)}, bf16[768,2048]{1,0:T(8,128)(2,1)}, u32[]{:S(2)}, u32[]{:S(2)}) collective-permute-start(bf16[768,2048]{1,0:T(8,128)(2,1)} %refs_1_.7), channel_id=1, source_target_pairs={{1,2},{2,1},{5,6},{6,5},{9,10},{10,9},{13,14},{14,13},{17,18},{18,... | collective-permute-start | bytes 9437192 | tf_op jit(solution)/shard_map/ppermute | solution.py:390
  2.3 72.4 %collective-permute-start = (bf16[768,2048]{1,0:T(8,128)(2,1)}, bf16[768,2048]{1,0:T(8,128)(2,1)}, u32[]{:S(2)}, u32[]{:S(2)}) collective-permute-start(bf16[768,2048]{1,0:T(8,128)(2,1)} %refs_1_.7), channel_id=1, source_target_pairs={{0,1},{1,0},{2,3},{3,2},{4,5},{5,4},{6,7},{7,6},{8,9},{9,8},{10,11... | collective-permute-start | bytes 9437192 | tf_op jit(solution)/shard_map/ppermute | solution.py:389
  14.6 72.8 %collective-permute-start.4 = (bf16[784,2048]{1,0:T(8,128)(2,1)}, bf16[784,2048]{1,0:T(8,128)(2,1)}, u32[]{:S(2)}, u32[]{:S(2)}) collective-permute-start(bf16[784,2048]{1,0:T(8,128)(2,1)} %pad_maximum_fusion), channel_id=1, source_target_pairs={{0,8},{4,12},{8,0},{12,4},{1,9},{5,13},{9,1},{13,5},{2,10},{6,14},... | collective-permute-start | bytes 9633800 | tf_op jit(solution)/shard_map/ppermute | solution.py:353
  17.0 11.4 %copy-start.15 = (s32[5,32]{1,0:T(8,128)S(1)}, s32[5,32]{1,0:T(8,128)}, u32[]{:S(2)}) copy-start(s32[5,32]{1,0:T(8,128)} %pad_add_fusion.refs_2_.at_ref) | copy-start | bytes 1924
  40.2 1.4 copy-start.6
  41.6 1.3 copy-start.9
  42.9 1.4 copy-start.16
  44.2 1.4 copy-start.17
  45.6 32.8 %collective-permute-start.3 = (bf16[512,2048]{1,0:T(8,128)(2,1)}, bf16[512,2048]{1,0:T(8,128)(2,1)}, u32[]{:S(2)}, u32[]{:S(2)}) collective-permute-start(bf16[512,2048]{1,0:T(8,128)(2,1)} %bitcast.3), channel_id=1, source_target_pairs={{0,4},{4,0},{8,12},{12,8},{1,5},{5,1},{9,13},{13,9},{2,6},{6,2},{1... | collective-permute-start | bytes 6291464 | tf_op jit(solution)/shard_map/ppermute | solution.py:353
  45.6 64.5 %collective-permute-start.5 = (bf16[512,2048]{1,0:T(8,128)(2,1)}, bf16[512,2048]{1,0:T(8,128)(2,1)}, u32[]{:S(2)}, u32[]{:S(2)}) collective-permute-start(bf16[512,2048]{1,0:T(8,128)(2,1)} %bitcast.5), channel_id=1, source_target_pairs={{0,4},{4,0},{8,12},{12,8},{1,5},{5,1},{9,13},{13,9},{2,6},{6,2},{1... | collective-permute-start | bytes 6291464 | tf_op jit(solution)/shard_map/ppermute | solution.py:353
  46.1 99.4 %collective-permute-start.10 = (bf16[768,2048]{1,0:T(8,128)(2,1)}, bf16[768,2048]{1,0:T(8,128)(2,1)S(1)}, u32[]{:S(2)}, u32[]{:S(2)}) collective-permute-start(bf16[768,2048]{1,0:T(8,128)(2,1)} %shard_map.75._.refs_1_), channel_id=1, source_target_pairs={{1,0},{2,3},{5,4},{6,7},{9,8},{10,11},{13,12},{14,15},{17,16},{18,... | collective-permute-start | bytes 9437192 | tf_op jit(solution)/shard_map/ppermute | solution.py:392
  74.7 57.4 %collective-permute-start.7 = (bf16[512,2048]{1,0:T(8,128)(2,1)}, bf16[512,2048]{1,0:T(8,128)(2,1)}, u32[]{:S(2)}, u32[]{:S(2)}) collective-permute-start(bf16[512,2048]{1,0:T(8,128)(2,1)} %bitcast.29), channel_id=1, source_target_pairs={{0,12},{4,8},{8,4},{12,0},{1,13},{5,9},{9,5},{13,1},{2,14},{6,10},... | collective-permute-start | bytes 6291464 | tf_op jit(solution)/shard_map/ppermute | solution.py:353
  78.4 53.7 %collective-permute-start.8 = (bf16[384,2048]{1,0:T(8,128)(2,1)}, bf16[384,2048]{1,0:T(8,128)(2,1)}, u32[]{:S(2)}, u32[]{:S(2)}) collective-permute-start(bf16[384,2048]{1,0:T(8,128)(2,1)} %get-tuple-element.17.__1_), channel_id=1, source_target_pairs={{1,2},{2,1},{5,6},{6,5},{9,10},{10,9},{13,14},{14,13},{17,18},{18,... | collective-permute-start | bytes 4718600 | tf_op jit(solution)/shard_map/ppermute | solution.py:394
  87.3 60.7 %collective-permute-start.2 = (bf16[384,2048]{1,0:T(8,128)(2,1)}, bf16[384,2048]{1,0:T(8,128)(2,1)}, u32[]{:S(2)}, u32[]{:S(2)}) collective-permute-start(bf16[384,2048]{1,0:T(8,128)(2,1)} %get-tuple-element.16), channel_id=1, source_target_pairs={{1,2},{2,1},{5,6},{6,5},{9,10},{10,9},{13,14},{14,13},{17,18},{18,... | collective-permute-start | bytes 4718600 | tf_op jit(solution)/shard_map/ppermute | solution.py:394
  89.2 11.0 %copy-start.3 = (bf16[768,2048]{1,0:T(8,128)(2,1)S(1)}, bf16[768,2048]{1,0:T(8,128)(2,1)}, u32[]{:S(2)}) copy-start(bf16[768,2048]{1,0:T(8,128)(2,1)} %refs_1_.7) | copy-start | bytes 9437188
  100.2 9.0 %copy-start.2 = (f32[768,2048]{1,0:T(8,128)}, f32[768,2048]{1,0:T(8,128)S(1)}, u32[]{:S(2)}) copy-start(f32[768,2048]{1,0:T(8,128)S(1)} %shard_map.78.refs_4_) | copy-start | bytes 18874372
  118.5 13.6 %copy-start.14 = (f32[16,768]{1,0:T(8,128)}, f32[16,768]{1,0:T(8,128)S(1)}, u32[]{:S(2)}) copy-start(f32[16,768]{1,0:T(8,128)S(1)} %shard_map.80.__1_) | copy-start | bytes 147460
  118.5 12.9 %collective-permute-start.6 = (f32[16,768]{1,0:T(8,128)S(1)}, f32[16,768]{1,0:T(8,128)S(1)}, u32[]{:S(2)}, u32[]{:S(2)}) collective-permute-start(f32[16,768]{1,0:T(8,128)S(1)} %shard_map.80.__1_), channel_id=1, source_target_pairs={{0,8},{4,12},{8,0},{12,4},{1,9},{5,13},{9,1},{13,5},{2,10},{6,14},... | collective-permute-start | bytes 147464 | tf_op jit(solution)/shard_map/ppermute | solution.py:353
  132.1 49.9 %collective-permute-start.14 = (bf16[512,2048]{1,0:T(8,128)(2,1)}, bf16[512,2048]{1,0:T(8,128)(2,1)}, u32[]{:S(2)}, u32[]{:S(2)}) collective-permute-start(bf16[512,2048]{1,0:T(8,128)(2,1)} %bitcast.28), channel_id=1, source_target_pairs={{0,4},{4,0},{8,12},{12,8},{1,5},{5,1},{9,13},{13,9},{2,6},{6,2},{1... | collective-permute-start | bytes 6291464 | tf_op jit(solution)/shard_map/ppermute | solution.py:353
  132.2 1.6 copy-start.18
  132.2 49.8 %collective-permute-start.15 = (bf16[512,2048]{1,0:T(8,128)(2,1)}, bf16[512,2048]{1,0:T(8,128)(2,1)}, u32[]{:S(2)}, u32[]{:S(2)}) collective-permute-start(bf16[512,2048]{1,0:T(8,128)(2,1)} %shard_map.84.__1_), channel_id=1, source_target_pairs={{0,8},{4,12},{8,0},{12,4},{1,9},{5,13},{9,1},{13,5},{2,10},{6,14},... | collective-permute-start | bytes 6291464 | tf_op jit(solution)/shard_map/ppermute | solution.py:353
  133.8 3.9 %collective-permute-start.9 = (f32[16,768]{1,0:T(8,128)S(1)}, f32[16,768]{1,0:T(8,128)S(1)}, u32[]{:S(2)}, u32[]{:S(2)}) collective-permute-start(f32[16,768]{1,0:T(8,128)S(1)} %copy-done.18), channel_id=1, source_target_pairs={{0,1},{3,2},{4,5},{7,6},{8,9},{11,10},{12,13},{15,14},{16,17},{19,... | collective-permute-start | bytes 147464 | tf_op jit(solution)/shard_map/ppermute | solution.py:407
  137.7 56.9 %collective-permute-start.17 = (bf16[384,2048]{1,0:T(8,128)(2,1)}, bf16[384,2048]{1,0:T(8,128)(2,1)}, u32[]{:S(2)}, u32[]{:S(2)}) collective-permute-start(bf16[384,2048]{1,0:T(8,128)(2,1)} %shard_map.81.__1_.refs_0_), channel_id=1, source_target_pairs={{1,0},{2,3},{5,4},{6,7},{9,8},{10,11},{13,12},{14,15},{17,16},{18,... | collective-permute-start | bytes 4718600 | tf_op jit(solution)/shard_map/ppermute | solution.py:402
  145.6 1.7 copy-start.4
  147.2 1.9 copy-start.5
  147.2 16.8 %collective-permute-start.11 = (f32[16,768]{1,0:T(8,128)}, f32[16,768]{1,0:T(8,128)S(1)}, u32[]{:S(2)}, u32[]{:S(2)}) collective-permute-start(f32[16,768]{1,0:T(8,128)} %shard_map.86.refs_5_), channel_id=1, source_target_pairs={{1,2},{2,1},{5,6},{6,5},{9,10},{10,9},{13,14},{14,13},{17,18},{18,... | collective-permute-start | bytes 147464 | tf_op jit(solution)/shard_map/ppermute | solution.py:408
  149.1 0.8 copy-start.11
  161.3 2.7 %copy-start.1 = (f32[768,2048]{1,0:T(8,128)}, f32[768,2048]{1,0:T(8,128)S(1)}, u32[]{:S(2)}) copy-start(f32[768,2048]{1,0:T(8,128)S(1)} %shard_map.87.__1_.refs_6_) | copy-start | bytes 18874372
  164.6 14.1 %collective-permute-start.12 = (bf16[16,768]{1,0:T(8,128)(2,1)}, bf16[16,768]{1,0:T(8,128)(2,1)S(1)}, u32[]{:S(2)}, u32[]{:S(2)}) collective-permute-start(bf16[16,768]{1,0:T(8,128)(2,1)} %shard_map.88._), channel_id=1, source_target_pairs={{1,0},{2,3},{5,4},{6,7},{9,8},{10,11},{13,12},{14,15},{17,16},{18,... | collective-permute-start | bytes 73736 | tf_op jit(solution)/shard_map/ppermute | solution.py:411
  165.9 0.7 copy-start.12
  169.0 0.9 copy-start.7
  169.9 32.8 %collective-permute-start.16 = (bf16[192,2048]{1,0:T(8,128)(2,1)}, bf16[192,2048]{1,0:T(8,128)(2,1)S(1)}, u32[]{:S(2)}, u32[]{:S(2)}) collective-permute-start(bf16[192,2048]{1,0:T(8,128)(2,1)} %get-tuple-element.22.refs_1_), channel_id=1, source_target_pairs={{1,0},{2,3},{5,4},{6,7},{9,8},{10,11},{13,12},{14,15},{17,16},{18,... | collective-permute-start | bytes 2359304 | tf_op jit(solution)/shard_map/ppermute | solution.py:413
  175.5 3.3 %copy-start = (bf16[2048,2048]{1,0:T(8,128)(2,1)}, bf16[2048,2048]{1,0:T(8,128)(2,1)S(1)}, u32[]{:S(2)}) copy-start(bf16[2048,2048]{1,0:T(8,128)(2,1)S(1)} %shard_map.90.__1_.refs_2_) | copy-start | bytes 25165828
  178.7 2.5 %copy-start.13 = (bf16[16,768]{1,0:T(8,128)(2,1)S(1)}, bf16[16,768]{1,0:T(8,128)(2,1)}, u32[]{:S(2)}) copy-start(bf16[16,768]{1,0:T(8,128)(2,1)} %shard_map.88._) | copy-start | bytes 73732
  178.8 0.6 copy-start.19
  179.4 2.7 %copy-start.10 = (bf16[32,16,2048]{2,1,0:T(8,128)(2,1)S(1)}, bf16[32,16,2048]{2,1,0:T(8,128)(2,1)}, u32[]{:S(2)}) copy-start(bf16[32,16,2048]{2,1,0:T(8,128)(2,1)} %copy-done.9) | copy-start | bytes 6291460
  179.4 32.5 %collective-permute-start.13 = (bf16[192,2048]{1,0:T(8,128)(2,1)}, bf16[192,2048]{1,0:T(8,128)(2,1)}, u32[]{:S(2)}, u32[]{:S(2)}) collective-permute-start(bf16[192,2048]{1,0:T(8,128)(2,1)} %shard_map.92.refs_7_), channel_id=1, source_target_pairs={{1,0},{2,3},{5,4},{6,7},{9,8},{10,11},{13,12},{14,15},{17,16},{18,... | collective-permute-start | bytes 2359304 | tf_op jit(solution)/shard_map/ppermute | solution.py:416
  182.0 1.1 copy-start.8
  183.2 19.6 %slice-start = ((s8[8388608]{0:T(1024)(128)(4,1)}), s8[4194304]{0:T(1024)(128)(4,1)S(1)}, s32[]{:S(2)}) async-start(s8[8388608]{0:T(1024)(128)(4,1)} %bitcast.24), calls=%async_computation | async-start | bytes 8388608
  194.6 8.2 %slice-start.1 = ((s8[8388608]{0:T(1024)(128)(4,1)}), s8[4194304]{0:T(1024)(128)(4,1)S(1)}, s32[]{:S(2)}) async-start(s8[8388608]{0:T(1024)(128)(4,1)} %bitcast.24), calls=%async_computation.1 | async-start | bytes 8388608

commit v6 on v5

--- a/solution.py
+++ b/solution.py
@@ -219,7 +219,7 @@
 def add_expanded(order, low, codes, factors, homes, total, most):
     rank, rows = low.shape
     width = total.shape[1]
-    tile = min(TILE, width)
+    tile = min(2 * TILE, width)
     at = jnp.stack([jnp.asarray(x, jnp.int32) for x in [i for _, i in factors] + homes])
     full = lambda j, at: (0, 0)
     return order.call(

time: 217 us -> 217 us (level)
  Pallas kernels: 101 us -> 97.3 us
    pallas_call x11, Pallas kernels: 94.7 us -> 91.3 us  [call(): pl.pallas_call(body, grid_spec=pltpu.PrefetchScalarGridSpec(num_scalar_pr...]
  transfers between devices with their start and end apart: 18 -> 18, of which waited for: 6 -> 6; matrix products, arithmetic and copies ran while one was open for 6% -> 6% of each run, Pallas kernels for 45% -> 43%
where the time goes in v6:
time: 217 us; the launch traced here: 216 us
  Pallas kernels  97.3 us (45%)
  waiting for transfers between devices  59.8 us (28%)
  starting transfers between devices  27.4 us (13%)
  local copies, waits for them, and re-layouts  21 us (10%)
  other arithmetic  9.85 us (5%)
    pallas_call x11, Pallas kernels, call(): pl.pallas_call(body, grid_spec=pltpu.PrefetchScalarGridSpec(num_scalar_pr...  91.3 us
    ppermute x1, waiting for transfers between devices, body(): near = lax.ppermute(tokens, 'tensor', swap)  29.3 us
    unnamed x46, local copies, waits for them, and re-layouts  19.1 us
    ppermute x7, waiting for transfers between devices, send(): return lax.ppermute(block, 'dp', [(i, i ^ k) for i in range(groups)])  18.2 us
    ppermute x7, starting transfers between devices, send(): return lax.ppermute(block, 'dp', [(i, i ^ k) for i in range(groups)])  7.38 us
    pallas_call x2, Pallas kernels, cut(): pl.pallas_call(kernel, out_shape=[jax.ShapeDtypeStruct((size, x.shape[1])...  6.01 us
    ppermute x1, waiting for transfers between devices, body(): out_near = lax.ppermute(cross, 'tensor', outward)  5.93 us
    ppermute x1, waiting for transfers between devices, body(): out_far.append(lax.ppermute(order.hold(pieces[1]), 'tensor', outward))  4.7 us
  transfers between devices with their start and end apart: 18, of which 6 were waited for; matrix products, arithmetic and copies ran while one was open for 6% of the time, Pallas kernels for 43%

profile of v6, /device:TPU:0, one launch (start us, length us, event | category | flops | bytes accessed | tf_op | source)
XLA Modules:
  0.0 215.9 jit_solution(7768410375831152398)
XLA Ops:
  0.0 2.3 %collective-permute-start.1 = (bf16[768,2048]{1,0:T(8,128)(2,1)}, bf16[768,2048]{1,0:T(8,128)(2,1)}, u32[]{:S(2)}, u32[]{:S(2)}) collective-permute-start(bf16[768,2048]{1,0:T(8,128)(2,1)} %refs_1_.7), channel_id=1, source_target_pairs={{1,2},{2,1},{5,6},{6,5},{9,10},{10,9},{13,14},{14,13},{17,18},{18,... | collective-permute-start | bytes 9437192 | tf_op jit(solution)/shard_map/ppermute | solution.py:390
  2.3 4.3 %collective-permute-start = (bf16[768,2048]{1,0:T(8,128)(2,1)}, bf16[768,2048]{1,0:T(8,128)(2,1)}, u32[]{:S(2)}, u32[]{:S(2)}) collective-permute-start(bf16[768,2048]{1,0:T(8,128)(2,1)} %refs_1_.7), channel_id=1, source_target_pairs={{0,1},{1,0},{2,3},{3,2},{4,5},{5,4},{6,7},{7,6},{8,9},{9,8},{10,11... | collective-permute-start | bytes 9437192 | tf_op jit(solution)/shard_map/ppermute | solution.py:389
  6.6 0.8 eq.100
  7.4 1.0 select_reduce_fusion
  8.4 0.8 copy.24
  9.2 0.1 reduce-window.4
  9.2 0.1 reduce
  9.4 0.7 fusion.3
  10.0 0.2 select_reduce_fusion.2
  10.4 0.1 select_reduce_fusion.1
  10.6 4.0 %pad_maximum_fusion = bf16[784,2048]{1,0:T(8,128)(2,1)} fusion(bf16[16,2048]{1,0:T(8,128)(2,1)S(1)} %convert_element_type.13, bf16[768,2048]{1,0:T(8,128)(2,1)} %refs_1_.7), kind=kLoop, calls=%fused_computation | loop fusion | flops 6422528 | bytes 6422528 | tf_op jit(solution)/shard_map/concatenate | solution.py:364
  14.6 1.5 collective-permute-start.4
  16.1 0.1 select_reduce_fusion.3
  16.4 0.6 pad_add_fusion.refs_2_.at_ref
  17.0 11.4 %shard_map.73.refs_2_ = f32[768,2048]{1,0:T(8,128)} custom-call(s32[1]{0:T(128)} %bitcast.at_ref, bf16[768,2048]{1,0:T(8,128)(2,1)} %refs_1_.7, bf16[8192,2048]{1,0:T(8,128)(2,1)} %refs_0_.5, s32[5,32]{1,0:T(8,128)} %pad_add_fusion.refs_2_.at_ref), custom_call_target="tpu_custom_call" | custom-call | flops 1 | bytes 1 | tf_op jit(solution)/shard_map/pallas_call | solution.py:26
  28.4 7.9 %shard_map.74 = (bf16[32,16,2048]{2,1,0:T(8,128)(2,1)}, bf16[32,16,2048]{2,1,0:T(8,128)(2,1)}, bf16[32,16,2048]{2,1,0:T(8,128)(2,1)S(1)}, bf16[32,16,2048]{2,1,0...) custom-call(s32[5,32]{1,0:T(8,128)S(1)} %copy-done.15, ...), custom_call_target="tpu_custom_call" | custom-call | flops 1 | bytes 1 | tf_op jit(solution)/shard_map/pallas_call | solution.py:26
  36.3 1.3 copy-done.6
  37.7 1.3 copy-done.9
  39.0 1.4 copy-done.16
  40.3 1.4 copy-done.17
  41.7 2.4 %collective-permute-start.3 = (bf16[512,2048]{1,0:T(8,128)(2,1)}, bf16[512,2048]{1,0:T(8,128)(2,1)}, u32[]{:S(2)}, u32[]{:S(2)}) collective-permute-start(bf16[512,2048]{1,0:T(8,128)(2,1)} %bitcast.3), channel_id=1, source_target_pairs={{0,4},{4,0},{8,12},{12,8},{1,5},{5,1},{9,13},{13,9},{2,6},{6,2},{1... | collective-permute-start | bytes 6291464 | tf_op jit(solution)/shard_map/ppermute | solution.py:353
  44.2 1.3 collective-permute-start.10
  45.5 29.3 %collective-permute-done.x_ref.refs_0_ = bf16[768,2048]{1,0:T(8,128)(2,1)} collective-permute-done((bf16[768,2048]{1,0:T(8,128)(2,1)}, bf16[768,2048]{1,0:T(8,128)(2,1)}, u32[]{:S(2)}, u32[]{:S(2)}) %collective-permute-start) | collective-permute-done | bytes 3145760 | tf_op jit(solution)/shard_map/ppermute | solution.py:389
  74.8 3.6 %shard_map.76 = (bf16[384,2048]{1,0:T(8,128)(2,1)}, bf16[384,2048]{1,0:T(8,128)(2,1)}) custom-call(bf16[768,2048]{1,0:T(8,128)(2,1)} %collective-permute-done.x_ref.refs_0_, bf16[768,2048]{1,0:T(8,128)(2,1)} %shard_map.75._.refs_1_), custom_call_target="tpu_custom_call" | custom-call | flops 1 | bytes 1 | tf_op jit(solution)/shard_map/pallas_call | solution.py:60
  78.4 1.9 collective-permute-start.8
  80.3 7.0 %collective-permute-done.4.__0_ = bf16[784,2048]{1,0:T(8,128)(2,1)} collective-permute-done((bf16[784,2048]{1,0:T(8,128)(2,1)}, bf16[784,2048]{1,0:T(8,128)(2,1)}, u32[]{:S(2)}, u32[]{:S(2)}) %collective-permute-start.4) | collective-permute-done | bytes 3211296 | tf_op jit(solution)/shard_map/ppermute | solution.py:353
  87.3 1.8 collective-permute-start.2
  89.2 11.0 %shard_map.78.refs_4_ = f32[768,2048]{1,0:T(8,128)S(1)} custom-call(s32[1]{0:T(128)} %bitcast.4.at_ref, bf16[768,2048]{1,0:T(8,128)(2,1)} %collective-permute-done.x_ref.refs_0_, bf16[8192,2048]{1,0:T(8,128)(2,1)} %refs_0_.5, f32[768,2048]{1,0:T(8,128)} %shard_map.73.refs_2_, bf16[784,2048]{1,0:T(8,128)(2,1)} %shard_map.77.refs_3_.refs_1_), custom_call_target="tpu_custom_call" | custom-call | flops 1 | bytes 1 | tf_op jit(solution)/shard_map/pallas_call | solution.py:26
  100.2 9.0 %shard_map.79.refs_4_ = f32[16,768]{1,0:T(8,128)S(1)} custom-call(s32[5,32]{1,0:T(8,128)S(1)} %copy-done.15, s32[1,768]{1,0:T(1,128)S(1)} %broadcast_in_dim.130.refs_0_, bf16[768,2048]{1,0:T(8,128)(2,1)S(1)} %copy-done.3, bf16[256,16,2048]{2,1,0:T(8,128)(2,1)} %refs_2_.3, bf16[512,2048]{1,0:T(8,128)(2,1)} %collective-permute-done.3.refs_3_, ...), custom_call_target="tpu_custom_call" | custom-call | flops 1 | bytes 1 | tf_op jit(solution)/shard_map/pallas_call | solution.py:26
  109.2 0.8 slice_bitcast_fusion
  110.1 8.4 %shard_map.80.__1_ = f32[16,768]{1,0:T(8,128)S(1)} custom-call(s32[5,32]{1,0:T(8,128)S(1)} %copy-done.15, s32[1,768]{1,0:T(1,128)S(1)} %broadcast_in_dim.131.refs_0_, bf16[784,2048]{1,0:T(8,128)(2,1)} %shard_map.77.refs_3_.refs_1_, bf16[256,16,2048]{2,1,0:T(8,128)(2,1)} %refs_2_.3, bf16[512,2048]{1,0:T(8,128)(2,1)} %collective-permute-done.5.refs_3_, ...), custom_call_target="tpu_custom_call" | custom-call | flops 1 | bytes 1 | tf_op jit(solution)/shard_map/pallas_call | solution.py:26
  118.5 1.8 collective-permute-start.6
  120.3 11.2 %collective-permute-done.6 = f32[16,768]{1,0:T(8,128)S(1)} collective-permute-done((f32[16,768]{1,0:T(8,128)S(1)}, f32[16,768]{1,0:T(8,128)S(1)}, u32[]{:S(2)}, u32[]{:S(2)}) %collective-permute-start.6) | collective-permute-done | bytes 49184 | tf_op jit(solution)/shard_map/ppermute | solution.py:353
  131.5 0.6 add.38.__0_
  132.2 1.6 collective-permute-start.15
  133.8 2.2 %collective-permute-start.9 = (f32[16,768]{1,0:T(8,128)S(1)}, f32[16,768]{1,0:T(8,128)S(1)}, u32[]{:S(2)}, u32[]{:S(2)}) collective-permute-start(f32[16,768]{1,0:T(8,128)S(1)} %copy-done.18), channel_id=1, source_target_pairs={{0,1},{3,2},{4,5},{7,6},{8,9},{11,10},{12,13},{15,14},{16,17},{19,... | collective-permute-start | bytes 147464 | tf_op jit(solution)/shard_map/ppermute | solution.py:407
  136.0 1.7 collective-permute-done.9
  137.7 1.3 collective-permute-start.17
  139.0 0.6 add.39.__0_
  139.6 5.9 %collective-permute-done.10.__0_ = bf16[768,2048]{1,0:T(8,128)(2,1)S(1)} collective-permute-done((bf16[768,2048]{1,0:T(8,128)(2,1)}, bf16[768,2048]{1,0:T(8,128)(2,1)S(1)}, u32[]{:S(2)}, u32[]{:S(2)}) %collective-permute-start.10) | collective-permute-done | bytes 3145760 | tf_op jit(solution)/shard_map/ppermute | solution.py:392
  145.6 1.7 copy-done.4
  147.2 0.8 collective-permute-start.11
  148.0 1.1 copy-done.5
  149.1 0.8 copy-done.11
  149.9 11.4 %shard_map.87.__1_.refs_6_ = f32[768,2048]{1,0:T(8,128)S(1)} custom-call(s32[1]{0:T(128)} %bitcast.8.at_ref, bf16[384,2048]{1,0:T(8,128)(2,1)} %shard_map.81.__1_.refs_0_, bf16[384,2048]{1,0:T(8,128)(2,1)} %collective-permute-done.2.refs_1_.x_ref, bf16[768,2048]{1,0:T(8,128)(2,1)S(1)} %copy-done.5, bf16[8192,2048]{1,0:T(8,128)(2,1)} %refs_0_.5, ...), custom_call_target="tpu_custom_call" | custom-call | flops 1 | bytes 1 | tf_op jit(solution)/shard_map/pallas_call | solution.py:26
  161.3 2.7 %copy-done.1 = f32[768,2048]{1,0:T(8,128)} copy-done((f32[768,2048]{1,0:T(8,128)}, f32[768,2048]{1,0:T(8,128)S(1)}, u32[]{:S(2)}) %copy-start.1) | copy-done | bytes 6291480
  164.0 0.6 add_convert_fusion.__0_
  164.6 1.3 collective-permute-start.12
  165.9 0.7 copy-done.12
  166.7 2.4 %shard_map.89 = (bf16[192,2048]{1,0:T(8,128)(2,1)}, bf16[192,2048]{1,0:T(8,128)(2,1)S(1)}) custom-call(bf16[384,2048]{1,0:T(8,128)(2,1)} %collective-permute-done.2.refs_1_.x_ref, bf16[16,768]{1,0:T(8,128)(2,1)S(1)} %copy-done.12), custom_call_target="tpu_custom_call" | custom-call | flops 1 | bytes 1 | tf_op jit(solution)/shard_map/pallas_call | solution.py:60
  169.0 0.9 copy-done.7
  169.9 1.3 collective-permute-start.16
  171.2 4.3 %shard_map.90.__1_.refs_2_ = bf16[2048,2048]{1,0:T(8,128)(2,1)S(1)} custom-call(s32[1]{0:T(128)} %bitcast.9.at_ref, bf16[8192,2048]{1,0:T(8,128)(2,1)} %refs_0_.5, bf16[192,2048]{1,0:T(8,128)(2,1)} %get-tuple-element.22.refs_1_), custom_call_target="tpu_custom_call" | custom-call | flops 1 | bytes 1 | tf_op jit(solution)/shard_map/pallas_call | solution.py:26
  175.5 3.2 %copy-done = bf16[2048,2048]{1,0:T(8,128)(2,1)} copy-done((bf16[2048,2048]{1,0:T(8,128)(2,1)}, bf16[2048,2048]{1,0:T(8,128)(2,1)S(1)}, u32[]{:S(2)}) %copy-start) | copy-done | bytes 8388632
  178.8 0.6 copy-done.19
  179.4 1.6 collective-permute-start.13
  181.0 0.2 broadcast_in_dim.134.refs_1_
  181.3 0.7 broadcast_select_fusion.refs_0_
  182.1 1.1 copy-done.8
  183.2 11.9 %shard_map.93.refs_3_.refs_4_ = f32[768,2048]{1,0:T(8,128)S(1)} custom-call(s32[8]{0:T(128)S(1)} %stack.31.at_ref, bf16[16,768]{1,0:T(8,128)(2,1)S(1)} %broadcast_select_fusion.refs_0_, s32[768,1]{1,0:T(8,128)S(1)} %broadcast_in_dim.134.refs_1_, bf16[512,2048]{1,0:T(8,128)(2,1)S(1)} %bitcast.27, bf16[512,2048]{1,0:T(8,128)(2,1)} %collective-permute-done.14.refs_3_, ...), custom_call_target="tpu_custom_call" | custom-call | flops 1 | bytes 1 | tf_op jit(solution)/shard_map/pallas_call | solution.py:26
  195.1 8.2 %shard_map.94.refs_4_ = bf16[768,2048]{1,0:T(8,128)(2,1)} custom-call(s32[1]{0:T(128)} %constant.39.clone.1.at_ref, bf16[384,2048]{1,0:T(8,128)(2,1)} %collective-permute-done.17.refs_0_, bf16[768,2048]{1,0:T(8,128)(2,1)} %shard_map.75._.refs_1_, bf16[2048,2048]{1,0:T(8,128)(2,1)} %copy-done, f32[768,2048]{1,0:T(8,128)S(1)} %shard_map.93.refs_3_.refs_4_, ...), custom_call_target="tpu_custom_call" | custom-call | flops 1 | bytes 1 | tf_op jit(solution)/shard_map/pallas_call | solution.py:26
  203.3 3.8 %shard_map.95.refs_4_ = bf16[768,2048]{1,0:T(8,128)(2,1)} custom-call(s32[1]{0:T(128)} %constant.39.clone.1.at_ref, bf16[192,2048]{1,0:T(8,128)(2,1)S(1)} %collective-permute-done.16.refs_0_, bf16[768,2048]{1,0:T(8,128)(2,1)} %shard_map.75._.refs_1_, bf16[2048,2048]{1,0:T(8,128)(2,1)S(1)} %bitcast.25, ...), custom_call_target="tpu_custom_call", output_to_operand_aliasing={{}: (5, {})} | custom-call | flops 1 | bytes 1 | tf_op jit(solution)/shard_map/pallas_call | solution.py:26
  207.1 4.7 %collective-permute-done.13.refs_0_ = bf16[192,2048]{1,0:T(8,128)(2,1)} collective-permute-done((bf16[192,2048]{1,0:T(8,128)(2,1)}, bf16[192,2048]{1,0:T(8,128)(2,1)}, u32[]{:S(2)}, u32[]{:S(2)}) %collective-permute-start.13) | collective-permute-done | bytes 786464 | tf_op jit(solution)/shard_map/ppermute | solution.py:416
  211.8 4.1 %shard_map.96 = bf16[768,2048]{1,0:T(8,128)(2,1)} custom-call(s32[1]{0:T(128)} %constant.39.clone.1.at_ref, bf16[192,2048]{1,0:T(8,128)(2,1)} %collective-permute-done.13.refs_0_, bf16[768,2048]{1,0:T(8,128)(2,1)} %shard_map.75._.refs_1_, bf16[2048,2048]{1,0:T(8,128)(2,1)S(1)} %bitcast.25, ...), custom_call_target="tpu_custom_call", output_to_operand_aliasing={{}: (5, {})} | custom-call | flops 1 | bytes 1 | tf_op jit(solution)/shard_map/pallas_call | solution.py:26
  (77 shorter events, 0.8 us)
Async XLA Ops:
  0.0 44.2 %collective-permute-start.1 = (bf16[768,2048]{1,0:T(8,128)(2,1)}, bf16[768,2048]{1,0:T(8,128)(2,1)}, u32[]{:S(2)}, u32[]{:S(2)}) collective-permute-start(bf16[768,2048]{1,0:T(8,128)(2,1)} %refs_1_.7), channel_id=1, source_target_pairs={{1,2},{2,1},{5,6},{6,5},{9,10},{10,9},{13,14},{14,13},{17,18},{18,... | collective-permute-start | bytes 9437192 | tf_op jit(solution)/shard_map/ppermute | solution.py:390
  2.3 72.4 %collective-permute-start = (bf16[768,2048]{1,0:T(8,128)(2,1)}, bf16[768,2048]{1,0:T(8,128)(2,1)}, u32[]{:S(2)}, u32[]{:S(2)}) collective-permute-start(bf16[768,2048]{1,0:T(8,128)(2,1)} %refs_1_.7), channel_id=1, source_target_pairs={{0,1},{1,0},{2,3},{3,2},{4,5},{5,4},{6,7},{7,6},{8,9},{9,8},{10,11... | collective-permute-start | bytes 9437192 | tf_op jit(solution)/shard_map/ppermute | solution.py:389
  14.6 72.8 %collective-permute-start.4 = (bf16[784,2048]{1,0:T(8,128)(2,1)}, bf16[784,2048]{1,0:T(8,128)(2,1)}, u32[]{:S(2)}, u32[]{:S(2)}) collective-permute-start(bf16[784,2048]{1,0:T(8,128)(2,1)} %pad_maximum_fusion), channel_id=1, source_target_pairs={{0,8},{4,12},{8,0},{12,4},{1,9},{5,13},{9,1},{13,5},{2,10},{6,14},... | collective-permute-start | bytes 9633800 | tf_op jit(solution)/shard_map/ppermute | solution.py:353
  17.0 11.4 %copy-start.15 = (s32[5,32]{1,0:T(8,128)S(1)}, s32[5,32]{1,0:T(8,128)}, u32[]{:S(2)}) copy-start(s32[5,32]{1,0:T(8,128)} %pad_add_fusion.refs_2_.at_ref) | copy-start | bytes 1924
  36.3 1.4 copy-start.6
  37.7 1.3 copy-start.9
  39.0 1.4 copy-start.16
  40.3 1.4 copy-start.17
  41.7 36.7 %collective-permute-start.3 = (bf16[512,2048]{1,0:T(8,128)(2,1)}, bf16[512,2048]{1,0:T(8,128)(2,1)}, u32[]{:S(2)}, u32[]{:S(2)}) collective-permute-start(bf16[512,2048]{1,0:T(8,128)(2,1)} %bitcast.3), channel_id=1, source_target_pairs={{0,4},{4,0},{8,12},{12,8},{1,5},{5,1},{9,13},{13,9},{2,6},{6,2},{1... | collective-permute-start | bytes 6291464 | tf_op jit(solution)/shard_map/ppermute | solution.py:353
  44.2 65.9 %collective-permute-start.5 = (bf16[512,2048]{1,0:T(8,128)(2,1)}, bf16[512,2048]{1,0:T(8,128)(2,1)}, u32[]{:S(2)}, u32[]{:S(2)}) collective-permute-start(bf16[512,2048]{1,0:T(8,128)(2,1)} %bitcast.5), channel_id=1, source_target_pairs={{0,4},{4,0},{8,12},{12,8},{1,5},{5,1},{9,13},{13,9},{2,6},{6,2},{1... | collective-permute-start | bytes 6291464 | tf_op jit(solution)/shard_map/ppermute | solution.py:353
  44.2 101.4 %collective-permute-start.10 = (bf16[768,2048]{1,0:T(8,128)(2,1)}, bf16[768,2048]{1,0:T(8,128)(2,1)S(1)}, u32[]{:S(2)}, u32[]{:S(2)}) collective-permute-start(bf16[768,2048]{1,0:T(8,128)(2,1)} %shard_map.75._.refs_1_), channel_id=1, source_target_pairs={{1,0},{2,3},{5,4},{6,7},{9,8},{10,11},{13,12},{14,15},{17,16},{18,... | collective-permute-start | bytes 9437192 | tf_op jit(solution)/shard_map/ppermute | solution.py:392
  74.7 57.4 %collective-permute-start.7 = (bf16[512,2048]{1,0:T(8,128)(2,1)}, bf16[512,2048]{1,0:T(8,128)(2,1)}, u32[]{:S(2)}, u32[]{:S(2)}) collective-permute-start(bf16[512,2048]{1,0:T(8,128)(2,1)} %bitcast.29), channel_id=1, source_target_pairs={{0,12},{4,8},{8,4},{12,0},{1,13},{5,9},{9,5},{13,1},{2,14},{6,10},... | collective-permute-start | bytes 6291464 | tf_op jit(solution)/shard_map/ppermute | solution.py:353
  78.4 53.7 %collective-permute-start.8 = (bf16[384,2048]{1,0:T(8,128)(2,1)}, bf16[384,2048]{1,0:T(8,128)(2,1)}, u32[]{:S(2)}, u32[]{:S(2)}) collective-permute-start(bf16[384,2048]{1,0:T(8,128)(2,1)} %get-tuple-element.17.__1_), channel_id=1, source_target_pairs={{1,2},{2,1},{5,6},{6,5},{9,10},{10,9},{13,14},{14,13},{17,18},{18,... | collective-permute-start | bytes 4718600 | tf_op jit(solution)/shard_map/ppermute | solution.py:394
  87.3 60.7 %collective-permute-start.2 = (bf16[384,2048]{1,0:T(8,128)(2,1)}, bf16[384,2048]{1,0:T(8,128)(2,1)}, u32[]{:S(2)}, u32[]{:S(2)}) collective-permute-start(bf16[384,2048]{1,0:T(8,128)(2,1)} %get-tuple-element.16), channel_id=1, source_target_pairs={{1,2},{2,1},{5,6},{6,5},{9,10},{10,9},{13,14},{14,13},{17,18},{18,... | collective-permute-start | bytes 4718600 | tf_op jit(solution)/shard_map/ppermute | solution.py:394
  89.2 11.0 %copy-start.3 = (bf16[768,2048]{1,0:T(8,128)(2,1)S(1)}, bf16[768,2048]{1,0:T(8,128)(2,1)}, u32[]{:S(2)}) copy-start(bf16[768,2048]{1,0:T(8,128)(2,1)} %refs_1_.7) | copy-start | bytes 9437188
  100.2 9.0 %copy-start.2 = (f32[768,2048]{1,0:T(8,128)}, f32[768,2048]{1,0:T(8,128)S(1)}, u32[]{:S(2)}) copy-start(f32[768,2048]{1,0:T(8,128)S(1)} %shard_map.78.refs_4_) | copy-start | bytes 18874372
  118.5 13.6 %copy-start.14 = (f32[16,768]{1,0:T(8,128)}, f32[16,768]{1,0:T(8,128)S(1)}, u32[]{:S(2)}) copy-start(f32[16,768]{1,0:T(8,128)S(1)} %shard_map.80.__1_) | copy-start | bytes 147460
  118.5 12.9 %collective-permute-start.6 = (f32[16,768]{1,0:T(8,128)S(1)}, f32[16,768]{1,0:T(8,128)S(1)}, u32[]{:S(2)}, u32[]{:S(2)}) collective-permute-start(f32[16,768]{1,0:T(8,128)S(1)} %shard_map.80.__1_), channel_id=1, source_target_pairs={{0,8},{4,12},{8,0},{12,4},{1,9},{5,13},{9,1},{13,5},{2,10},{6,14},... | collective-permute-start | bytes 147464 | tf_op jit(solution)/shard_map/ppermute | solution.py:353
  132.1 49.9 %collective-permute-start.14 = (bf16[512,2048]{1,0:T(8,128)(2,1)}, bf16[512,2048]{1,0:T(8,128)(2,1)}, u32[]{:S(2)}, u32[]{:S(2)}) collective-permute-start(bf16[512,2048]{1,0:T(8,128)(2,1)} %bitcast.28), channel_id=1, source_target_pairs={{0,4},{4,0},{8,12},{12,8},{1,5},{5,1},{9,13},{13,9},{2,6},{6,2},{1... | collective-permute-start | bytes 6291464 | tf_op jit(solution)/shard_map/ppermute | solution.py:353
  132.2 1.6 copy-start.18
  132.2 49.8 %collective-permute-start.15 = (bf16[512,2048]{1,0:T(8,128)(2,1)}, bf16[512,2048]{1,0:T(8,128)(2,1)}, u32[]{:S(2)}, u32[]{:S(2)}) collective-permute-start(bf16[512,2048]{1,0:T(8,128)(2,1)} %shard_map.84.__1_), channel_id=1, source_target_pairs={{0,8},{4,12},{8,0},{12,4},{1,9},{5,13},{9,1},{13,5},{2,10},{6,14},... | collective-permute-start | bytes 6291464 | tf_op jit(solution)/shard_map/ppermute | solution.py:353
  133.8 3.9 %collective-permute-start.9 = (f32[16,768]{1,0:T(8,128)S(1)}, f32[16,768]{1,0:T(8,128)S(1)}, u32[]{:S(2)}, u32[]{:S(2)}) collective-permute-start(f32[16,768]{1,0:T(8,128)S(1)} %copy-done.18), channel_id=1, source_target_pairs={{0,1},{3,2},{4,5},{7,6},{8,9},{11,10},{12,13},{15,14},{16,17},{19,... | collective-permute-start | bytes 147464 | tf_op jit(solution)/shard_map/ppermute | solution.py:407
  137.7 57.4 %collective-permute-start.17 = (bf16[384,2048]{1,0:T(8,128)(2,1)}, bf16[384,2048]{1,0:T(8,128)(2,1)}, u32[]{:S(2)}, u32[]{:S(2)}) collective-permute-start(bf16[384,2048]{1,0:T(8,128)(2,1)} %shard_map.81.__1_.refs_0_), channel_id=1, source_target_pairs={{1,0},{2,3},{5,4},{6,7},{9,8},{10,11},{13,12},{14,15},{17,16},{18,... | collective-permute-start | bytes 4718600 | tf_op jit(solution)/shard_map/ppermute | solution.py:402
  145.6 1.7 copy-start.4
  147.2 1.9 copy-start.5
  147.2 16.8 %collective-permute-start.11 = (f32[16,768]{1,0:T(8,128)}, f32[16,768]{1,0:T(8,128)S(1)}, u32[]{:S(2)}, u32[]{:S(2)}) collective-permute-start(f32[16,768]{1,0:T(8,128)} %shard_map.86.refs_5_), channel_id=1, source_target_pairs={{1,2},{2,1},{5,6},{6,5},{9,10},{10,9},{13,14},{14,13},{17,18},{18,... | collective-permute-start | bytes 147464 | tf_op jit(solution)/shard_map/ppermute | solution.py:408
  149.1 0.8 copy-start.11
  161.3 2.7 %copy-start.1 = (f32[768,2048]{1,0:T(8,128)}, f32[768,2048]{1,0:T(8,128)S(1)}, u32[]{:S(2)}) copy-start(f32[768,2048]{1,0:T(8,128)S(1)} %shard_map.87.__1_.refs_6_) | copy-start | bytes 18874372
  164.6 14.1 %collective-permute-start.12 = (bf16[16,768]{1,0:T(8,128)(2,1)}, bf16[16,768]{1,0:T(8,128)(2,1)S(1)}, u32[]{:S(2)}, u32[]{:S(2)}) collective-permute-start(bf16[16,768]{1,0:T(8,128)(2,1)} %shard_map.88._), channel_id=1, source_target_pairs={{1,0},{2,3},{5,4},{6,7},{9,8},{10,11},{13,12},{14,15},{17,16},{18,... | collective-permute-start | bytes 73736 | tf_op jit(solution)/shard_map/ppermute | solution.py:411
  165.9 0.7 copy-start.12
  169.0 0.9 copy-start.7
  169.9 33.3 %collective-permute-start.16 = (bf16[192,2048]{1,0:T(8,128)(2,1)}, bf16[192,2048]{1,0:T(8,128)(2,1)S(1)}, u32[]{:S(2)}, u32[]{:S(2)}) collective-permute-start(bf16[192,2048]{1,0:T(8,128)(2,1)} %get-tuple-element.22.refs_1_), channel_id=1, source_target_pairs={{1,0},{2,3},{5,4},{6,7},{9,8},{10,11},{13,12},{14,15},{17,16},{18,... | collective-permute-start | bytes 2359304 | tf_op jit(solution)/shard_map/ppermute | solution.py:413
  175.5 3.3 %copy-start = (bf16[2048,2048]{1,0:T(8,128)(2,1)}, bf16[2048,2048]{1,0:T(8,128)(2,1)S(1)}, u32[]{:S(2)}) copy-start(bf16[2048,2048]{1,0:T(8,128)(2,1)S(1)} %shard_map.90.__1_.refs_2_) | copy-start | bytes 25165828
  178.7 2.5 %copy-start.13 = (bf16[16,768]{1,0:T(8,128)(2,1)S(1)}, bf16[16,768]{1,0:T(8,128)(2,1)}, u32[]{:S(2)}) copy-start(bf16[16,768]{1,0:T(8,128)(2,1)} %shard_map.88._) | copy-start | bytes 73732
  178.8 0.6 copy-start.19
  179.4 2.7 %copy-start.10 = (bf16[32,16,2048]{2,1,0:T(8,128)(2,1)S(1)}, bf16[32,16,2048]{2,1,0:T(8,128)(2,1)}, u32[]{:S(2)}) copy-start(bf16[32,16,2048]{2,1,0:T(8,128)(2,1)} %copy-done.9) | copy-start | bytes 6291460
  179.4 32.5 %collective-permute-start.13 = (bf16[192,2048]{1,0:T(8,128)(2,1)}, bf16[192,2048]{1,0:T(8,128)(2,1)}, u32[]{:S(2)}, u32[]{:S(2)}) collective-permute-start(bf16[192,2048]{1,0:T(8,128)(2,1)} %shard_map.92.refs_7_), channel_id=1, source_target_pairs={{1,0},{2,3},{5,4},{6,7},{9,8},{10,11},{13,12},{14,15},{17,16},{18,... | collective-permute-start | bytes 2359304 | tf_op jit(solution)/shard_map/ppermute | solution.py:416
  182.0 1.1 copy-start.8
  183.2 20.1 %slice-start = ((s8[8388608]{0:T(1024)(128)(4,1)}), s8[4194304]{0:T(1024)(128)(4,1)S(1)}, s32[]{:S(2)}) async-start(s8[8388608]{0:T(1024)(128)(4,1)} %bitcast.24), calls=%async_computation | async-start | bytes 8388608
  195.1 8.2 %slice-start.1 = ((s8[8388608]{0:T(1024)(128)(4,1)}), s8[4194304]{0:T(1024)(128)(4,1)S(1)}, s32[]{:S(2)}) async-start(s8[8388608]{0:T(1024)(128)(4,1)} %bitcast.24), calls=%async_computation.1 | async-start | bytes 8388608
